TPU v7x, 256 devices: a whole 4x4x8 slice. The times are simulated.
256 devices in a mesh: dp: 4 (over x), seq: 32 (over y_hi, z, core), aud: 2 (over y_lo).
Axes of the slice: x: 4, y: 4 (y_hi: 2, y_lo: 2; y = y_hi * 2 + y_lo), z: 8, core: 2. Of those that a mesh axis runs over, the one named last changes fastest.
Arguments:
- q_video: bfloat16 [32768, 3072], P(('dp', 'seq', 'aud')), parts along dimension 0, may hold values from -8 to 8
- k_video: bfloat16 [32768, 3072], P(('dp', 'seq', 'aud')), parts along dimension 0, may hold values from -8 to 8
- v_video: bfloat16 [32768, 3072], P(('dp', 'seq', 'aud')), parts along dimension 0, may hold values from -6 to 6
- d_video: bfloat16 [32768, 3072], P(('dp', 'seq', 'aud')), parts along dimension 0, may hold values from -6 to 6
- q_audio: bfloat16 [1024, 3072], P(('dp', 'seq', 'aud')), parts along dimension 0, may hold values from -8 to 8
- k_audio: bfloat16 [1024, 3072], P(('dp', 'seq', 'aud')), parts along dimension 0, may hold values from -8 to 8
- v_audio: bfloat16 [1024, 3072], P(('dp', 'seq', 'aud')), parts along dimension 0, may hold values from -6 to 6
- d_audio: bfloat16 [1024, 3072], P(('dp', 'seq', 'aud')), parts along dimension 0, may hold values from -6 to 6
- audio_pos: int32 [1024], P(('dp', 'seq', 'aud')), parts along dimension 0, may hold values from 0 to 15
- video_len: int32 [4], P('dp'), parts along dimension 0, may hold values from 4096 to 8192
- audio_len: int32 [4], P('dp'), parts along dimension 0, may hold values from 128 to 256
Outputs:
- dk_video: bfloat16 [32768, 3072], P(('dp', 'seq', 'aud')), parts along dimension 0
- dv_video: bfloat16 [32768, 3072], P(('dp', 'seq', 'aud')), parts along dimension 0
- dk_audio: bfloat16 [1024, 3072], P(('dp', 'seq', 'aud')), parts along dimension 0
- dv_audio: bfloat16 [1024, 3072], P(('dp', 'seq', 'aud')), parts along dimension 0
There are 4 independent parts, one for each index of `dp`. A program takes and returns all parts, laid end to end along the dimension named above; each array names one. Nothing has to cross between parts.
All inputs are finite; a program needn't handle non-finite values.
Results may differ from a plain program's by a relative error of at most 0.011.
Values may be sent and summed in bfloat16 or wider, within the bound.
No kernel may reach another device: no remote copies, remote signals or barrier semaphores. Data moves between devices by JAX's collectives and lax.ppermute only.
A program may use at most 128 MiB of HBM per device.

v0:
```python
import jax
import jax.numpy as jnp
from jax import lax
from jax.sharding import PartitionSpec as P

HD = 128
VFRAME = 512


rope_base = 10000.0
neg_fill = -1e30


def rotate(values, where_at, direction):
    row_count = values.shape[0]
    half_width = HD // 2
    frequency = rope_base ** (-(jnp.arange(half_width, dtype=jnp.float32) / half_width))
    phase_angle = where_at.astype(jnp.float32)[:, None] * frequency[None, :]
    cosine = jnp.cos(phase_angle)[:, None, :]
    sine_part = direction * jnp.sin(phase_angle)[:, None, :]
    shaped = values.astype(jnp.float32).reshape(row_count, -1, HD)
    first_half = shaped[:, :, :half_width]
    second = shaped[:, :, half_width:]
    turned = jnp.concatenate(
        [first_half * cosine - second * sine_part, second * cosine + first_half * sine_part], axis=2
    )
    return turned.reshape(row_count, -1)


def split_heads(values):
    return values.reshape(values.shape[0], -1, HD)


def local(
    q_video,
    k_video,
    v_video,
    d_video,
    q_audio,
    k_audio,
    v_audio,
    d_audio,
    audio_pos,
    video_len,
    audio_len,
):
    score_scale = HD ** (-0.5)
    devices = lax.axis_size(("seq", "aud"))
    own_index = lax.axis_index(("seq", "aud"))
    video_rows = q_video.shape[0]
    own_count = q_audio.shape[0]
    width = q_video.shape[1]
    audio_total = own_count * devices
    video_index = own_index * video_rows + jnp.arange(video_rows, dtype=jnp.int32)
    video_pos = video_index // VFRAME
    video_valid = video_index < video_len[0]
    audio_own_index = own_index * own_count + jnp.arange(own_count, dtype=jnp.int32)
    video_query = rotate(q_video, video_pos, 1.0).astype(jnp.bfloat16)
    video_key = rotate(k_video, video_pos, 1.0).astype(jnp.bfloat16)
    video_grad = jnp.where(video_valid[:, None], d_video, jnp.zeros_like(d_video))
    audio_grad_own = jnp.where(
        (audio_own_index < audio_len[0])[:, None], d_audio, jnp.zeros_like(d_audio)
    )
    query_own = rotate(q_audio, audio_pos, 1.0).astype(jnp.bfloat16)
    key_own = rotate(k_audio, audio_pos, 1.0).astype(jnp.bfloat16)
    audio_query, audio_key, audio_value, audio_grad = (
        lax.all_gather(query_own, ("seq", "aud"), axis=0, tiled=True),
        lax.all_gather(key_own, ("seq", "aud"), axis=0, tiled=True),
        lax.all_gather(v_audio, ("seq", "aud"), axis=0, tiled=True),
        lax.all_gather(audio_grad_own, ("seq", "aud"), axis=0, tiled=True),
    )
    audio_valid = jnp.arange(audio_total, dtype=jnp.int32) < audio_len[0]
    query_heads = split_heads(video_query)
    key_heads = split_heads(audio_key)
    value_heads = split_heads(audio_value)
    grad_heads = split_heads(video_grad)
    scores_one = (
        jnp.einsum("qhd,khd->qhk", query_heads, key_heads, preferred_element_type=jnp.float32)
        * score_scale
    )
    scores_one = jnp.where(audio_valid[None, None, :], scores_one, neg_fill)
    raw_one = jnp.exp(scores_one - jnp.max(scores_one, axis=2, keepdims=True))
    probs_one = raw_one / jnp.sum(raw_one, axis=2, keepdims=True)
    probs_one_low = probs_one.astype(jnp.bfloat16)
    out_one = jnp.einsum(
        "qhk,khd->qhd", probs_one_low, value_heads, preferred_element_type=jnp.float32
    )
    delta_one = jnp.sum(grad_heads.astype(jnp.float32) * out_one, axis=2)
    dprob_one = jnp.einsum(
        "qhd,khd->qhk", grad_heads, value_heads, preferred_element_type=jnp.float32
    )
    dscore_one = (probs_one * (dprob_one - delta_one[:, :, None]) * score_scale).astype(
        jnp.bfloat16
    )
    dkey_part = jnp.einsum(
        "qhk,qhd->khd", dscore_one, query_heads, preferred_element_type=jnp.float32
    ).reshape(audio_total, width)
    dval_part = jnp.einsum(
        "qhk,qhd->khd", probs_one_low, grad_heads, preferred_element_type=jnp.float32
    ).reshape(audio_total, width)
    dkey_sum, dval_sum = (
        lax.psum_scatter(dkey_part, ("seq", "aud"), scatter_dimension=0, tiled=True),
        lax.psum_scatter(dval_part, ("seq", "aud"), scatter_dimension=0, tiled=True),
    )
    dk_audio = rotate(dkey_sum, audio_pos, -1.0).astype(jnp.bfloat16)
    dv_audio = dval_sum.astype(jnp.bfloat16)
    audio_heads = split_heads(audio_query)
    video_key_heads = split_heads(video_key)
    video_value_heads = split_heads(v_video)
    scores_two = (
        jnp.einsum("qhd,khd->qhk", audio_heads, video_key_heads, preferred_element_type=jnp.float32)
        * score_scale
    )
    scores_two = jnp.where(video_valid[None, None, :], scores_two, neg_fill)
    block_peak = jnp.max(scores_two, axis=2)
    raw_two = jnp.where(
        video_valid[None, None, :], jnp.exp(scores_two - block_peak[:, :, None]), 0.0
    )
    block_total = jnp.sum(raw_two, axis=2)
    block_numer = jnp.einsum(
        "qhk,khd->qhd",
        raw_two.astype(jnp.bfloat16),
        video_value_heads,
        preferred_element_type=jnp.float32,
    )
    global_peak = lax.pmax(block_peak, ("seq", "aud"))
    factor = jnp.exp(block_peak - global_peak)
    scaled_numer = (block_numer * factor[:, :, None]).reshape(audio_total, width)
    numer_own, total_own = (
        lax.psum_scatter(scaled_numer, ("seq", "aud"), scatter_dimension=0, tiled=True),
        lax.psum_scatter(block_total * factor, ("seq", "aud"), scatter_dimension=0, tiled=True),
    )
    peak_own = lax.dynamic_slice_in_dim(global_peak, own_index * own_count, own_count, 0)
    out_two = numer_own.reshape(own_count, -1, HD) / total_own[:, :, None]
    lse_own = peak_own + jnp.log(total_own)
    delta_own = jnp.sum(split_heads(audio_grad_own).astype(jnp.float32) * out_two, axis=2)
    lse_all, delta_all = (
        lax.all_gather(lse_own, ("seq", "aud"), axis=0, tiled=True),
        lax.all_gather(delta_own, ("seq", "aud"), axis=0, tiled=True),
    )
    agrad_heads = split_heads(audio_grad)
    probs_two = jnp.where(
        video_valid[None, None, :], jnp.exp(scores_two - lse_all[:, :, None]), 0.0
    )
    probs_two_low = probs_two.astype(jnp.bfloat16)
    dv_video = (
        jnp.einsum("qhk,qhd->khd", probs_two_low, agrad_heads, preferred_element_type=jnp.float32)
        .reshape(video_rows, width)
        .astype(jnp.bfloat16)
    )
    dprob_two = jnp.einsum(
        "qhd,khd->qhk", agrad_heads, video_value_heads, preferred_element_type=jnp.float32
    )
    dscore_two = (probs_two * (dprob_two - delta_all[:, :, None]) * score_scale).astype(
        jnp.bfloat16
    )
    dkey_video = jnp.einsum(
        "qhk,qhd->khd", dscore_two, audio_heads, preferred_element_type=jnp.float32
    ).reshape(video_rows, width)
    dk_video = rotate(dkey_video, video_pos, -1.0).astype(jnp.bfloat16)
    return (dk_video, dv_video, dk_audio, dv_audio)


def solution(mesh):
    return jax.shard_map(
        local,
        mesh=mesh,
        in_specs=(
            P(("dp", "seq", "aud"), None),
            P(("dp", "seq", "aud"), None),
            P(("dp", "seq", "aud"), None),
            P(("dp", "seq", "aud"), None),
            P(("dp", "seq", "aud"), None),
            P(("dp", "seq", "aud"), None),
            P(("dp", "seq", "aud"), None),
            P(("dp", "seq", "aud"), None),
            P(("dp", "seq", "aud")),
            P("dp"),
            P("dp"),
        ),
        out_specs=(
            P(("dp", "seq", "aud"), None),
            P(("dp", "seq", "aud"), None),
            P(("dp", "seq", "aud"), None),
            P(("dp", "seq", "aud"), None),
        ),
        check_vma=False,
    )
```

profile of v0, /device:TPU:1, one launch (start us, length us, event | category | flops | bytes accessed | tf_op | source)
XLA Modules:
  0.0 1348.6 jit_solution(3003969426655070763)
XLA Ops:
  7.2 0.8 convert_element_type.74
  8.0 0.7 convert_bitcast_fusion.2
  8.8 0.7 convert_bitcast_fusion
  9.5 0.7 broadcast_multiply_fusion.1
  10.4 0.6 reshape.299
  11.1 0.7 all-gather.17.cloned.1.call-update
  11.9 0.6 reshape.307
  13.3 1.4 convert_bitcast_fusion.1
  15.5 0.5 iota_compare_fusion
  16.0 0.9 broadcast_multiply_fusion
  18.0 1.2 copy.210
  19.2 1.3 broadcast_select_fusion
  20.5 1.2 copy.172
  21.6 1.1 fusion.61
  22.7 0.5 copy.207
  23.2 1.3 fusion.60
  24.5 1.6 copy.205
  26.1 2.8 copy.204
  28.9 2.8 copy.206
  31.7 4.3 subtract_convert_fusion
  36.0 160.4 %all-gather.11.cloned.1.call-done = bf16[64,4,3072]{2,1,0:T(4,128)(2,1)} async-done(((bf16[1,4,3072]{2,1,0:T(4,128)(2,1)}), bf16[64,4,3072]{2,1,0:T(4,128)(2,1)}) %all-gather.11.cloned.1.call-update) | async-done | bytes 1572880 | tf_op jit(solution)/shard_map/all_gather | solution.py:67
  196.4 2.9 reshape.273
  199.3 1.8 copy.162
  201.2 2.8 bitcast_reduce_fusion.1
  204.0 179.8 %all-gather.17.cloned.1.call-done = bf16[64,4,3072]{2,1,0:T(4,128)(2,1)} async-done(((bf16[1,4,3072]{2,1,0:T(4,128)(2,1)}), bf16[64,4,3072]{2,1,0:T(4,128)(2,1)}) %all-gather.17.cloned.1.call-update) | async-done | bytes 1572880 | tf_op jit(solution)/shard_map/all_gather | solution.py:69
  383.8 3.8 reshape.286
  387.7 2.9 copy.177
  390.6 0.6 fusion.15
  391.2 0.8 copy.152
  392.0 246.4 %pmax.7 = f32[256,24]{1,0:T(8,128)S(1)} all-reduce(f32[256,24]{1,0:T(8,128)S(1)} %copy.150), channel_id=1, replica_groups=mesh['dp'=4,'seq'=32,'aud'=2] {'seq','aud'}, use_global_device_ids=true, to_apply=%region_1.2 | all-reduce | flops 6144 | bytes 49152 | tf_op jit(solution)/shard_map/pmax | solution.py:126
  638.4 1.6 fusion.58
  640.0 1.0 copy.159
  641.0 3.8 reshape.284
  644.8 2.6 fusion.22
  647.4 1.4 fusion.62
  648.8 2.5 bitcast_multiply_fusion
  651.3 0.5 copy-done.12
  652.2 0.6 fusion.21
  652.8 6.5 fusion.33
  659.3 0.6 copy-done.10
  660.0 0.6 dynamic-slice
  661.2 99.7 %all-gather.13.cloned.1.call-done = bf16[64,4,3072]{2,1,0:T(4,128)(2,1)} async-done(((bf16[1,4,3072]{2,1,0:T(4,128)(2,1)}), bf16[64,4,3072]{2,1,0:T(4,128)(2,1)}) %all-gather.13.cloned.1.call-update) | async-done | bytes 1572880 | tf_op jit(solution)/shard_map/all_gather | solution.py:70
  760.9 3.8 reshape.276
  764.7 2.9 copy.166
  767.6 4.4 fusion.55
  772.0 3.6 copy.185
  775.6 289.2 %all-reduce.10 = (f32[256,24]{1,0:T(8,128)}, bf16[256,3072]{1,0:T(8,128)(2,1)}) all-reduce(f32[256,24]{1,0:T(8,128)S(1)} %copy-done.7, f32[256,3072]{1,0:T(8,128)} %copy.185), channel_id=2, replica_groups=mesh['dp'=4,'seq'=32,'aud'=2] {'seq','aud'}, use_global_device_ids=true, to_apply=%region_3.4.clone | all-reduce | flops 792576 | bytes 4767744
  1064.8 0.7 add_bitcast_fusion
  1065.5 124.6 %all-gather.1 = f32[64,4,24]{2,1,0:T(4,128)S(1)} all-gather(f32[1,4,24]{2,1,0:T(4,128)S(1)} %get-tuple-element.28), channel_id=1, replica_groups=mesh['dp'=4,'seq'=32,'aud'=2] {'seq','aud'}, dimensions={0}, use_global_device_ids=true | all-gather | bytes 24960 | tf_op jit(solution)/shard_map/all_gather | solution.py:138
  1190.1 3.0 fusion.34
  1193.1 2.3 copy.187
  1195.4 1.4 dynamic-slice_convert_fusion
  1196.8 3.2 constant_dynamic-slice_fusion.1
  1200.0 1.7 constant_dynamic-slice_fusion
  1201.6 1.9 copy.160
  1203.5 2.7 fusion.59
  1206.2 1.4 copy.209
  1207.6 1.4 copy.208
  1209.2 0.6 copy.221
  1210.0 122.7 %all-gather.3 = f32[64,4,24]{2,1,0:T(4,128)S(1)} all-gather(f32[1,4,24]{2,1,0:T(4,128)S(1)} %bitcast.149), channel_id=1, replica_groups=mesh['dp'=4,'seq'=32,'aud'=2] {'seq','aud'}, dimensions={0}, use_global_device_ids=true | all-gather | bytes 24960 | tf_op jit(solution)/shard_map/all_gather | solution.py:139
  1332.7 4.7 convolution_bitcast_fusion
  1337.4 2.6 subtract_convert_fusion.1
  1340.0 0.4 pad_maximum_fusion
  1340.9 1.2 copy.186
  (52 shorter events, 3.0 us)
Async XLA Ops:
  7.2 9.7 copy-start.2
  7.2 10.1 copy-start.3
  7.2 189.2 %all-gather.11.cloned.1.call-start = ((), (), s32[]{:S(2)}) async-start(), calls=%async_computation | async-start | bytes 1597440 | tf_op jit(solution)/shard_map/all_gather | solution.py:67
  11.0 372.8 %all-gather.17.cloned.1.call-start = ((), (), s32[]{:S(2)}) async-start(), calls=%async_computation.3 | async-start | bytes 1597440 | tf_op jit(solution)/shard_map/all_gather | solution.py:69
  11.8 629.2 %all-gather.15.cloned.1.call-start = ((), (), s32[]{:S(2)}) async-start(), calls=%async_computation.2 | async-start | bytes 1597440 | tf_op jit(solution)/shard_map/all_gather | solution.py:68
  12.6 748.3 %all-gather.13.cloned.1.call-start = ((), (), s32[]{:S(2)}) async-start(), calls=%async_computation.1 | async-start | bytes 1597440 | tf_op jit(solution)/shard_map/all_gather | solution.py:70
  14.7 1182.1 %all-reduce.9.cloned.1.call-start = ((), (), s32[]{:S(2)}) async-start(), calls=%async_computation.4 | async-start | bytes 12582912
  16.9 1.1 copy-start.4
  644.8 2.6 copy-start.11
  647.4 1.4 copy-start
  648.8 3.0 copy-start.12
  648.8 2.9 copy-start.1
  648.8 3.4 copy-start.5
  659.3 0.7 copy-start.10
  772.0 3.6 copy-start.7
  1196.8 3.2 copy-start.6
  1206.2 2.9 copy-start.9
  1332.7 4.7 copy-start.8
Sparse Core Ops, SparseCore 0:
  11.2 185.2 all-gather.10
  198.2 185.5 all-gather.16
  385.7 186.6 all-gather.14
  574.6 186.2 all-gather.12
  764.3 204.2 all-reduce.8
where the time goes:
time: 1350 us
  blocking collectives  783 us (58%)
  waiting for transfers between devices  441 us (33%)
  local copies, waits for them, and re-layouts  62.6 us (5%)
  matrix products  27 us (2%)
  other arithmetic  19.3 us (1%)
  between operations  16 us (1%)
    unnamed x1, blocking collectives  289 us
    pmax x1, blocking collectives, local(): global_peak = lax.pmax(block_peak, ('seq', 'aud'))  246 us
    all_gather x1, waiting for transfers between devices, local(): lax.all_gather(v_audio, ('seq', 'aud'), axis=0, tiled=True)  180 us
    all_gather x1, waiting for transfers between devices, local(): lax.all_gather(query_own, ('seq', 'aud'), axis=0, tiled=True)  160 us
    all_gather x1, blocking collectives, local(): lax.all_gather(lse_own, ('seq', 'aud'), axis=0, tiled=True)  125 us
    all_gather x1, blocking collectives, local(): lax.all_gather(delta_own, ('seq', 'aud'), axis=0, tiled=True)  123 us
    all_gather x1, waiting for transfers between devices, local(): lax.all_gather(audio_grad_own, ('seq', 'aud'), axis=0, tiled=True)  99.7 us
  transfers between devices with their start and end apart: 5, of which 3 were waited for; matrix products, arithmetic and copies ran while one was open for 6% of the time, Pallas kernels for 0%

commit v1 on v0

v1 whole, which is shorter than its diff:
```python
import functools

import jax
import jax.numpy as jnp
from jax import lax
from jax.experimental import pallas as pl
from jax.experimental.pallas import tpu as pltpu
from jax.sharding import Mesh
from jax.sharding import PartitionSpec as P

HD = 128
VFRAME = 512
ROPE_BASE = 10000.0
NEG = -1e30
SCALE = HD ** (-0.5)

NY, NZ, NC = 4, 8, 2
HEADS = 12
GROUPS = 4
HPG = HEADS // GROUPS
GW = HPG * HD
CW = HEADS * HD
VT = 128
AR = 4
CR = NC * AR
ZR = NZ * CR
AUDIO = NY * ZR

ALL = ("dp", "yh", "z", "core", "yl")
Y = ("yh", "yl")
f32 = jnp.float32
bf16 = jnp.bfloat16


def frequencies():
    half = HD // 2
    return ROPE_BASE ** (-(jnp.arange(half, dtype=f32) / half))


def turn_tables(where_at):
    angle = where_at.astype(f32)[:, None] * frequencies()[None, :]
    cosine, sine = jnp.cos(angle), jnp.sin(angle)
    return jnp.concatenate([cosine, cosine], 1), jnp.concatenate([-sine, sine], 1)


def rotate_rows(values, cosine, sine):
    rows = values.shape[0]
    shaped = values.astype(f32).reshape(rows, -1, 2, HD // 2)
    swapped = shaped[:, :, ::-1].reshape(rows, -1, HD)
    shaped = shaped.reshape(rows, -1, HD)
    return (shaped * cosine[:, None, :] + swapped * sine[:, None, :]).reshape(rows, -1)


def shift(x, axis, size, step):
    return lax.ppermute(x, axis, [(i, (i + step) % size) for i in range(size)])


def nt(a, b):
    return lax.dot_general(a, b, (((1,), (1,)), ((), ())), preferred_element_type=f32)


def nn(a, b):
    return lax.dot_general(a, b, (((1,), (0,)), ((), ())), preferred_element_type=f32)


def head(i):
    return slice(i * HD, (i + 1) * HD)


def prepare_kernel(sc, q0, q1, k0, k1, v0, v1, d0, d1, cos, sin, qr, kr, vr, dr):
    limit = sc[3]
    for block, (q, k, v, d) in enumerate(((q0, k0, v0, d0), (q1, k1, v1, d1))):
        rows = slice(block * VT, (block + 1) * VT)
        cosine, sine = cos[block : block + 1, :], sin[block : block + 1, :]
        for i in range(HPG):
            for src, dst in ((q, qr), (k, kr)):
                x = src[:, head(i)].astype(f32)
                dst[rows, head(i)] = (
                    x * cosine + pltpu.roll(x, HD // 2, 1) * sine
                ).astype(bf16)
        vr[rows, :] = v[...]
        token = sc[4 + block] + lax.broadcasted_iota(jnp.int32, (VT, GW), 0)
        dr[rows, :] = jnp.where(token < limit, d[...].astype(f32), 0.0).astype(bf16)


def video_to_audio_kernel(sc, q, d, a0, a1, a2, a3, o0, o1, o2, o3):
    core, y, limit = sc[0], sc[1], sc[2]
    row = lax.broadcasted_iota(jnp.int32, (AUDIO, 2 * VT), 0)
    yy = (row // ZR + y) % NY
    zz = (row // CR) % NZ
    r = row % CR
    cc = jnp.where(r < AR, core, 1 - core)
    own = ((yy // 2 * NZ + zz) * NC + cc) * 2 + yy % 2
    valid = own * AR + r % AR < limit
    for i in range(HPG):
        key = jnp.concatenate([a[:, head(i)] for a in (a0, a1, a2, a3)], 0)
        value = jnp.concatenate([a[:, head(HPG + i)] for a in (a0, a1, a2, a3)], 0)
        query, grad = q[:, head(i)], d[:, head(i)]
        s = jnp.where(valid, nt(key, query) * SCALE, NEG)
        e = jnp.exp(s - jnp.max(s, axis=0, keepdims=True))
        p = e * (1.0 / jnp.sum(e, axis=0, keepdims=True))
        pb = p.astype(bf16)
        dp = nt(value, grad)
        delta = jnp.sum(pb.astype(f32) * dp, axis=0, keepdims=True)
        ds = (p * (dp - delta) * SCALE).astype(bf16)
        dk = nn(ds, query).astype(bf16)
        dv = nn(pb, grad).astype(bf16)
        for n, o in enumerate((o0, o1, o2, o3)):
            o[:, head(i)] = dk[n * ZR : (n + 1) * ZR]
            o[:, head(HPG + i)] = dv[n * ZR : (n + 1) * ZR]


def video_mask(sc):
    row = lax.broadcasted_iota(jnp.int32, (2 * VT, AUDIO), 0)
    token = jnp.where(row < VT, sc[4] + row, sc[5] + row - VT)
    return token < sc[3]


def statistics_kernel(sc, k, v, a0, a1, a2, a3, out):
    g = pl.program_id(0)
    valid = video_mask(sc)
    for i in range(HPG):
        query = jnp.concatenate([a[:, head(i)] for a in (a0, a1, a2, a3)], 0)
        grad = jnp.concatenate([a[:, head(HPG + i)] for a in (a0, a1, a2, a3)], 0)
        s = jnp.where(valid, nt(k[:, head(i)], query) * SCALE, NEG)
        m = jnp.max(s, axis=0, keepdims=True)
        e = jnp.where(valid, jnp.exp(s - m), 0.0)
        c = jnp.sum(e, axis=0, keepdims=True)
        eb = e.astype(bf16).astype(f32)
        t = jnp.sum(eb * nt(v[:, head(i)], grad), axis=0, keepdims=True)
        some = c > 0.0
        safe = jnp.where(some, c, 1.0)
        out[pl.ds(g * HPG + i, 1), :] = jnp.where(some, m + jnp.log(safe), NEG)
        out[pl.ds(HEADS + g * HPG + i, 1), :] = jnp.where(some, t / safe, 0.0)

    @pl.when(g == GROUPS - 1)
    def _():
        out[...] = pltpu.roll(out[...], sc[1] * ZR, 1)


def merge(lses, deltas):
    top = functools.reduce(jnp.maximum, lses)
    weights = [jnp.exp(x - top) for x in lses]
    total = sum(weights)
    delta = sum(w * x for w, x in zip(weights, deltas)) / total
    return top + jnp.log(total), delta


def merge_kernel(sc, *refs, count, back):
    *parts, out = refs
    if count > 1:
        (part,) = parts
        parts = [part.at[n] for n in range(count)]
    lse, delta = merge([p[:HEADS] for p in parts], [p[HEADS:] for p in parts])
    both = jnp.concatenate([lse, delta], 0)
    if back:
        both = pltpu.roll(both, lax.rem(AUDIO - sc[1] * ZR, AUDIO), 1)
    out[...] = both


def audio_to_video_kernel(sc, k, v, stats, cos, sin, a0, a1, a2, a3, dk0, dk1, dv0, dv1):
    g = pl.program_id(0)
    valid = video_mask(sc)
    for i in range(HPG):
        query = jnp.concatenate([a[:, head(i)] for a in (a0, a1, a2, a3)], 0)
        grad = jnp.concatenate([a[:, head(HPG + i)] for a in (a0, a1, a2, a3)], 0)
        lse = stats[pl.ds(g * HPG + i, 1), :]
        delta = stats[pl.ds(HEADS + g * HPG + i, 1), :]
        s = nt(k[:, head(i)], query) * SCALE
        p = jnp.where(valid, jnp.exp(s - lse), 0.0)
        dp = nt(v[:, head(i)], grad)
        ds = (p * (dp - delta) * SCALE).astype(bf16)
        dv = nn(p.astype(bf16), grad)
        dk = nn(ds, query)
        for block, (dko, dvo) in enumerate(((dk0, dv0), (dk1, dv1))):
            rows = slice(block * VT, (block + 1) * VT)
            x = dk[rows]
            dko[:, head(i)] = (
                x * cos[block : block + 1, :]
                - pltpu.roll(x, HD // 2, 1) * sin[block : block + 1, :]
            ).astype(bf16)
            dvo[:, head(i)] = dv[rows].astype(bf16)


def call(kernel, scalars, args, specs, outs, out_specs, grid=(GROUPS,), flops=0):
    size = sum(x.size * x.dtype.itemsize for x in args)
    return pl.pallas_call(
        kernel,
        grid_spec=pltpu.PrefetchScalarGridSpec(
            num_scalar_prefetch=1, grid=grid, in_specs=specs, out_specs=out_specs
        ),
        out_shape=outs,
        compiler_params=pltpu.CompilerParams(vmem_limit_bytes=40 * 1024 * 1024),
        cost_estimate=pl.CostEstimate(flops=flops, bytes_accessed=size, transcendentals=0),
    )(scalars, *args)


def local(q_video, k_video, v_video, d_video, q_audio, k_audio, v_audio, d_audio, audio_pos, video_len, audio_len):
    yh, z, core, yl = (lax.axis_index(a) for a in ("yh", "z", "core", "yl"))
    y = yh * 2 + yl
    own = ((yh * NZ + z) * NC + core) * 2 + yl
    pair = ((yh * NZ + z) * NC + 1 - core) * 2 + yl
    scalars = jnp.stack(
        [core, y, audio_len[0], video_len[0], own * VT, pair * VT]
    ).astype(jnp.int32)
    first = core == 0

    audio_cos, audio_sin = turn_tables(audio_pos)
    ours = own * AR + jnp.arange(AR, dtype=jnp.int32) < audio_len[0]
    q_rot = rotate_rows(q_audio, audio_cos, audio_sin).astype(bf16)
    k_rot = rotate_rows(k_audio, audio_cos, audio_sin).astype(bf16)
    d_own = jnp.where(ours[:, None], d_audio, jnp.zeros_like(d_audio))

    def packed(a, b):
        a = a.reshape(AR, NC, GROUPS, 1, GW)
        b = b.reshape(AR, NC, GROUPS, 1, GW)
        both = jnp.concatenate([a, b], 3).reshape(AR, NC, 2 * CW)
        keep = jnp.where(first, both[:, 0], both[:, 1])
        give = jnp.where(first, both[:, 1], both[:, 0])
        return keep, give

    keep_kv, give_kv = packed(k_rot, v_audio)
    keep_qd, give_qd = packed(q_rot, d_own)
    kv = jnp.concatenate([keep_kv, shift(give_kv, "core", NC, 1)], 0)
    qd = jnp.concatenate([keep_qd, shift(give_qd, "core", NC, 1)], 0)

    def along_z(x):
        copies = jnp.broadcast_to(x[None], (NZ,) + x.shape).reshape(ZR, 2 * CW)
        return lax.all_to_all(copies, "z", split_axis=0, concat_axis=0, tiled=True)

    def along_y(x):
        return [x] + [shift(x, Y, NY, NY - n) for n in range(1, NY)]

    kv_all = along_y(along_z(kv))
    qd_all = along_y(along_z(qd))

    q_pair, k_pair, v_pair, d_pair = (
        shift(x, "core", NC, 1) for x in (q_video, k_video, v_video, d_video)
    )
    cos, sin = turn_tables(jnp.stack([own * VT // VFRAME, pair * VT // VFRAME]))
    half = pl.BlockSpec((VT, GW), lambda g, sc: (0, sc[0] * GROUPS + g))
    table = pl.BlockSpec((2, HD), lambda g, sc: (0, 0))
    video = pl.BlockSpec((2 * VT, GW), lambda g, sc: (0, g))
    audio = pl.BlockSpec((ZR, 2 * GW), lambda g, sc: (0, g))
    rows = pl.BlockSpec((2 * HEADS, AUDIO), lambda g, sc: (0, 0))
    mine = pl.BlockSpec((VT, GW), lambda g, sc: (0, g))
    video_shape = jax.ShapeDtypeStruct((2 * VT, CW), bf16)
    rows_shape = jax.ShapeDtypeStruct((2 * HEADS, AUDIO), f32)
    mine_shape = jax.ShapeDtypeStruct((VT, CW), bf16)
    audio_shape = jax.ShapeDtypeStruct((ZR, 2 * CW), bf16)
    one = 2 * 2 * VT * AUDIO * CW

    qr, kr, vr, dr = call(
        prepare_kernel,
        scalars,
        (q_video, q_pair, k_video, k_pair, v_video, v_pair, d_video, d_pair, cos, sin),
        [half] * 8 + [table] * 2,
        [video_shape] * 4,
        [video] * 4,
    )

    parts = call(
        video_to_audio_kernel,
        scalars,
        (qr, dr, *kv_all),
        [video] * 2 + [audio] * NY,
        [audio_shape] * NY,
        [audio] * NY,
        flops=4 * one,
    )
    sums = parts[0].astype(f32)
    for n in range(1, NY):
        sums = sums + shift(parts[n], Y, NY, n).astype(f32)
    sums = lax.all_to_all(sums.astype(bf16), "z", split_axis=0, concat_axis=0, tiled=True)
    sums = jnp.sum(sums.reshape(NZ, CR, 2 * CW).astype(f32), 0)
    other = shift(sums[AR:], "core", NC, 1)
    sums = sums[:AR]
    sums = jnp.stack([jnp.where(first, sums, other), jnp.where(first, other, sums)], 1)
    sums = sums.reshape(AR, NC, GROUPS, 2, GW)
    dk_sum = sums[:, :, :, 0].reshape(AR, NC * CW)
    dk_audio = rotate_rows(dk_sum, audio_cos, -audio_sin).astype(bf16)
    dv_audio = sums[:, :, :, 1].reshape(AR, NC * CW).astype(bf16)

    stats = call(
        statistics_kernel,
        scalars,
        (kr, vr, *qd_all),
        [video] * 2 + [audio] * NY,
        rows_shape,
        rows,
        flops=2 * one,
    )
    stats = call(
        functools.partial(merge_kernel, count=1, back=False),
        scalars,
        along_y(stats),
        [rows] * NY,
        rows_shape,
        rows,
        grid=(1,),
    )
    copies = jnp.broadcast_to(stats[None], (NZ,) + stats.shape)
    stats = lax.all_to_all(copies, "z", split_axis=0, concat_axis=0, tiled=True)
    stats = call(
        functools.partial(merge_kernel, count=NZ, back=True),
        scalars,
        (stats,),
        [pl.BlockSpec(stats.shape, lambda g, sc: (0, 0, 0))],
        rows_shape,
        rows,
        grid=(1,),
    )
    dk0, dk1, dv0, dv1 = call(
        audio_to_video_kernel,
        scalars,
        (kr, vr, stats, cos, sin, *qd_all),
        [video] * 2 + [rows] + [table] * 2 + [audio] * NY,
        [mine_shape] * 4,
        [mine] * 4,
        flops=4 * one,
    )

    def joined(a, b):
        b = shift(b, "core", NC, 1)
        return jnp.concatenate([jnp.where(first, a, b), jnp.where(first, b, a)], 1)

    return joined(dk0, dk1), joined(dv0, dv1), dk_audio, dv_audio


def solution(mesh):
    fine = Mesh(mesh.devices.reshape(mesh.shape["dp"], 2, NZ, NC, 2), ALL)
    rows = P(ALL, None)
    return jax.shard_map(
        local,
        mesh=fine,
        in_specs=(rows,) * 8 + (P(ALL), P("dp"), P("dp")),
        out_specs=(rows,) * 4,
        check_vma=False,
    )
```

time: 1350 us -> 150 us (0.11)
  blocking collectives: 783 us -> 0 us
  waiting for transfers between devices: 441 us -> 52.2 us
  starting transfers between devices: 0.2 us -> 49.1 us
  local copies, waits for them, and re-layouts: 62.6 us -> 15.5 us
  matrix products: 27 us -> 0 us
  Pallas kernels: 0 us -> 23.2 us
  between operations: 16 us -> 2.43 us
    all_gather x4 -> x0, waiting for transfers between devices: 440 us -> none  [the longest x1 180 us: local(): lax.all_gather(v_audio, ('seq', 'aud'), axis=0, tiled=True)]
    unnamed x1 -> x0, blocking collectives: 289 us -> none
    all_gather x2 -> x0, blocking collectives: 247 us -> none  [the longest x1 125 us: local(): lax.all_gather(lse_own, ('seq', 'aud'), axis=0, tiled=True)]
    pmax x1 -> x0, blocking collectives: 246 us -> none  [local(): global_peak = lax.pmax(block_peak, ('seq', 'aud'))]
    all_to_all x0 -> x4, waiting for transfers between devices: none -> 34.3 us  [the longest x2 23.5 us: along_z(): return lax.all_to_all(copies, 'z', split_axis=0, concat_axis=0, tiled=True)]
    dot_general x8 -> x0, matrix products: 27 us -> none  [the longest x1 6.46 us: local(): jnp.einsum('qhk,qhd->khd', dscore_one, query_heads, preferred_element_typ...]
    reshape x11, local copies, waits for them, and re-layouts: 28.6 us -> 2.34 us  [the longest x2 1.76 us: rotate_rows(): shaped = values.astype(f32).reshape(rows, -1, 2, HD // 2)]
    ppermute x0 -> x21, starting transfers between devices: none -> 25.9 us  [shift(): return lax.ppermute(x, axis, [(i, (i + step) % size) for i in range(size)])]
  transfers between devices with their start and end apart: 5 -> 25, of which waited for: 3 -> 9; matrix products, arithmetic and copies ran while one was open for 6% -> 5% of each run, Pallas kernels for 0% -> 16%
where the time goes in v1:
time: 150 us; the launch traced here: 149 us
  waiting for transfers between devices  52.2 us (35%)
  starting transfers between devices  49.1 us (33%)
  Pallas kernels  23.2 us (15%)
  local copies, waits for them, and re-layouts  15.5 us (10%)
  other arithmetic  6.73 us (4%)
  between operations  2.43 us (2%)
    ppermute x21, starting transfers between devices, shift(): return lax.ppermute(x, axis, [(i, (i + step) % size) for i in range(size)])  25.9 us
    all_to_all x2, waiting for transfers between devices, along_z(): return lax.all_to_all(copies, 'z', split_axis=0, concat_axis=0, tiled=True)  23.5 us
    pallas_call x6, Pallas kernels, call(): pl.pallas_call(kernel, grid_spec=pltpu.PrefetchScalarGridSpec(num_scalar_...  23.2 us
    ppermute x21, waiting for transfers between devices, shift(): return lax.ppermute(x, axis, [(i, (i + step) % size) for i in range(size)])  17.9 us
    all_to_all x1, waiting for transfers between devices, local(): lax.all_to_all(sums.astype(bf16), 'z', split_axis=0, concat_axis=0, tiled...  10.8 us
    all_to_all x2, starting transfers between devices, along_z(): return lax.all_to_all(copies, 'z', split_axis=0, concat_axis=0, tiled=True)  9.9 us
    unnamed x52, local copies, waits for them, and re-layouts  9.08 us
    all_to_all x1, starting transfers between devices, local(): lax.all_to_all(sums.astype(bf16), 'z', split_axis=0, concat_axis=0, tiled...  6.77 us
  transfers between devices with their start and end apart: 25, of which 9 were waited for; matrix products, arithmetic and copies ran while one was open for 5% of the time, Pallas kernels for 16%

profile of v1, /device:TPU:1, one launch (start us, length us, event | category | flops | bytes accessed | tf_op | source)
XLA Modules:
  0.0 149.1 jit_solution(16025722831496839974)
XLA Ops:
  1.3 0.7 convert_element_type.49
  2.2 0.9 reshape.145
  3.1 0.2 rev.9
  3.3 0.1 reshape.146
  3.5 0.9 reshape.150
  4.4 0.2 rev.10
  4.6 0.1 reshape.151
  5.2 0.1 broadcast_select_fusion.7
  5.3 3.3 %collective-permute-start.4 = (bf16[4,3072]{1,0:T(4,128)(2,1)S(1)}, bf16[4,3072]{1,0:T(4,128)(2,1)S(1)}, u32[]{:S(2)}, u32[]{:S(2)}) collective-permute-start(bf16[4,3072]{1,0:T(4,128)(2,1)S(1)} %bitcast.75), channel_id=1, source_target_pairs={{0,2},{2,0},{1,3},{3,1},{4,6},{6,4},{5,7},{7,5},{8,10},{10,8},{9,1... | collective-permute-start | bytes 73736 | tf_op jit(solution)/shard_map/ppermute | solution.py:55
  8.9 0.6 collective-permute-done.4
  9.5 0.8 broadcast_in_dim.18
  10.3 6.5 %all-to-all-start = ((bf16[8,8,3072]{2,1,0:T(8,128)(2,1)}), bf16[8,8,3072]{2,1,0:T(8,128)(2,1)S(1)}, u32[]{:S(2)}, u32[]{:S(2)}) async-start(bf16[8,8,3072]{2,1,0:T(8,128)(2,1)} %broadcast_in_dim.18), calls=%async_computation | async-start | bytes 786432 | tf_op jit(solution)/shard_map/all_to_all | solution.py:229
  16.9 0.7 collective-permute-start.13
  17.7 0.4 collective-permute-start.1
  18.2 0.4 collective-permute-start.3
  18.7 13.2 %all-to-all-done = bf16[8,8,3072]{2,1,0:T(8,128)(2,1)S(1)} async-done(((bf16[8,8,3072]{2,1,0:T(8,128)(2,1)}), bf16[8,8,3072]{2,1,0:T(8,128)(2,1)S(1)}, u32[]{:S(2)}, u32[]{:S(2)}) %all-to-all-start) | async-done | bytes 393248 | tf_op jit(solution)/shard_map/all_to_all | solution.py:229
  31.9 0.8 broadcast_in_dim.20
  32.7 3.5 %all-to-all-start.2 = ((bf16[8,8,3072]{2,1,0:T(8,128)(2,1)}), bf16[8,8,3072]{2,1,0:T(8,128)(2,1)S(1)}, u32[]{:S(2)}, u32[]{:S(2)}) async-start(bf16[8,8,3072]{2,1,0:T(8,128)(2,1)} %broadcast_in_dim.20), calls=%async_computation.2 | async-start | bytes 786432 | tf_op jit(solution)/shard_map/all_to_all | solution.py:229
  36.1 2.8 %collective-permute-start.5 = (bf16[64,3072]{1,0:T(8,128)(2,1)S(1)}, bf16[64,3072]{1,0:T(8,128)(2,1)S(1)}, u32[]{:S(2)}, u32[]{:S(2)}) collective-permute-start(bf16[64,3072]{1,0:T(8,128)(2,1)S(1)} %bitcast.63), channel_id=1, source_target_pairs={{0,33},{1,0},{32,1},{33,32},{2,35},{3,2},{34,3},{35,34},{4,37},{5,... | collective-permute-start | bytes 1179656 | tf_op jit(solution)/shard_map/ppermute | solution.py:55
  39.7 0.4 collective-permute-start.6
  40.1 0.7 collective-permute-start.7
  40.9 10.3 %all-to-all-done.2 = bf16[8,8,3072]{2,1,0:T(8,128)(2,1)S(1)} async-done(((bf16[8,8,3072]{2,1,0:T(8,128)(2,1)}), bf16[8,8,3072]{2,1,0:T(8,128)(2,1)S(1)}, u32[]{:S(2)}, u32[]{:S(2)}) %all-to-all-start.2) | async-done | bytes 393248 | tf_op jit(solution)/shard_map/all_to_all | solution.py:229
  51.2 2.7 %collective-permute-start.14 = (bf16[64,3072]{1,0:T(8,128)(2,1)S(1)}, bf16[64,3072]{1,0:T(8,128)(2,1)}, u32[]{:S(2)}, u32[]{:S(2)}) collective-permute-start(bf16[64,3072]{1,0:T(8,128)(2,1)S(1)} %bitcast.68), channel_id=1, source_target_pairs={{0,33},{1,0},{32,1},{33,32},{2,35},{3,2},{34,3},{35,34},{4,37},{5,... | collective-permute-start | bytes 1179656 | tf_op jit(solution)/shard_map/ppermute | solution.py:55
  53.9 0.3 collective-permute-start.15
  54.3 0.2 collective-permute-done.5.a1
  54.5 0.5 collective-permute-start.16
  55.2 1.1 copy-done.1
  56.3 1.1 copy-done.3
  57.4 1.1 copy-done.5
  58.6 1.1 copy-done.6
  59.7 4.1 %shard_map.138 = (bf16[256,1536]{1,0:T(8,128)(2,1)S(1)}, bf16[256,1536]{1,0:T(8,128)(2,1)S(1)}, bf16[256,1536]{1,0:T(8,128)(2,1)S(1)}, bf16[256,1536]{1,0:T(8,128)(2,1)S(1)}) custom-call(s32[6]{0:T(128)S(1)} %stack.37.sc, bf16[128,3072]{1,0:T(8,128)(2,1)S(1)} %copy-done.1, bf16[128,3072]{1,0:T(8,128)(2,1)} %collective-permute-done.q1, ...), custom_call_target="tpu_custom_call" | custom-call | bytes 6293504 | tf_op jit(solution)/shard_map/pallas_call | solution.py:187
  63.8 3.3 %shard_map.139.refs_0_ = f32[24,256]{1,0:T(8,128)S(1)} custom-call(s32[6]{0:T(128)S(1)} %stack.37.sc, bf16[256,1536]{1,0:T(8,128)(2,1)S(1)} %get-tuple-element.16.k, bf16[256,1536]{1,0:T(8,128)(2,1)S(1)} %get-tuple-element.17.v, bf16[64,3072]{1,0:T(8,128)(2,1)S(1)} %bitcast.66, bf16[64,3072]{1,0:T(8,128)(2,1)S(1)} %collective-permute-done.5.a1, ...), custom_call_target="tpu_custom_call" | custom-call | flops 402653184 | bytes 3145728 | tf_op jit(solution)/shard_map/pallas_call | solution.py:187
  67.1 1.7 %collective-permute-start.10 = (f32[24,256]{1,0:T(8,128)S(1)}, f32[24,256]{1,0:T(8,128)S(1)}, u32[]{:S(2)}, u32[]{:S(2)}) collective-permute-start(f32[24,256]{1,0:T(8,128)S(1)} %shard_map.139.refs_0_), channel_id=1, source_target_pairs={{0,1},{1,32},{32,33},{33,0},{2,3},{3,34},{34,35},{35,2},{4,5},{5,3... | collective-permute-start | bytes 73736 | tf_op jit(solution)/shard_map/ppermute | solution.py:55
  68.8 2.1 %collective-permute-start.8 = (f32[24,256]{1,0:T(8,128)S(1)}, f32[24,256]{1,0:T(8,128)S(1)}, u32[]{:S(2)}, u32[]{:S(2)}) collective-permute-start(f32[24,256]{1,0:T(8,128)S(1)} %shard_map.139.refs_0_), channel_id=1, source_target_pairs={{0,33},{1,0},{32,1},{33,32},{2,35},{3,2},{34,3},{35,34},{4,37},{5,... | collective-permute-start | bytes 73736 | tf_op jit(solution)/shard_map/ppermute | solution.py:55
  70.9 7.1 %collective-permute-done.10.refs_3_ = f32[24,256]{1,0:T(8,128)S(1)} collective-permute-done((f32[24,256]{1,0:T(8,128)S(1)}, f32[24,256]{1,0:T(8,128)S(1)}, u32[]{:S(2)}, u32[]{:S(2)}) %collective-permute-start.10) | collective-permute-done | bytes 24608 | tf_op jit(solution)/shard_map/ppermute | solution.py:55
  78.0 0.5 collective-permute-start.9
  78.4 3.7 %collective-permute-done.9.refs_2_ = f32[24,256]{1,0:T(8,128)S(1)} collective-permute-done((f32[24,256]{1,0:T(8,128)S(1)}, f32[24,256]{1,0:T(8,128)S(1)}, u32[]{:S(2)}, u32[]{:S(2)}) %collective-permute-start.9) | collective-permute-done | bytes 24608 | tf_op jit(solution)/shard_map/ppermute | solution.py:55
  82.2 0.6 shard_map.140
  82.7 0.7 broadcast_in_dim.19
  83.4 6.5 %all-to-all-start.1 = ((f32[8,24,256]{2,1,0:T(8,128)}), f32[8,24,256]{2,1,0:T(8,128)}, u32[]{:S(2)}, u32[]{:S(2)}) async-start(f32[8,24,256]{2,1,0:T(8,128)} %broadcast_in_dim.19), calls=%async_computation.1 | async-start | bytes 393216 | tf_op jit(solution)/shard_map/all_to_all | solution.py:303
  90.0 1.1 copy-done.8
  91.1 1.1 copy-done.10
  92.2 8.3 %shard_map.143 = (bf16[64,3072]{1,0:T(8,128)(2,1)S(1)}, bf16[64,3072]{1,0:T(8,128)(2,1)}, bf16[64,3072]{1,0:T(8,128)(2,1)}, bf16[64,3072]{1,0:T(8,128)(2,1)}) custom-call(s32[6]{0:T(128)S(1)} %stack.37.sc, bf16[256,1536]{1,0:T(8,128)(2,1)S(1)} %copy-done.8, bf16[256,1536]{1,0:T(8,128)(2,1)S(1)} %copy-done.10, bf16[64,3072]{1,0:T(8,128)(2,1)S(1)} %bitcast.71, ...), custom_call_target="tpu_custom_call" | custom-call | flops 805306368 | bytes 3145728 | tf_op jit(solution)/shard_map/pallas_call | solution.py:187
  100.6 0.8 copy-done.13
  101.3 0.4 collective-permute-start.18
  101.8 2.2 %collective-permute-start.19 = (bf16[64,3072]{1,0:T(8,128)(2,1)}, bf16[64,3072]{1,0:T(8,128)(2,1)}, u32[]{:S(2)}, u32[]{:S(2)}) collective-permute-start(bf16[64,3072]{1,0:T(8,128)(2,1)} %get-tuple-element.27), channel_id=1, source_target_pairs={{0,33},{1,0},{32,1},{33,32},{2,35},{3,2},{34,3},{35,34},{4,37},{5,... | collective-permute-start | bytes 1179656 | tf_op jit(solution)/shard_map/ppermute | solution.py:55
  104.0 0.6 broadcast_bitcast_fusion
  104.6 1.6 %shard_map.141.stats = f32[24,256]{1,0:T(8,128)S(1)} custom-call(s32[6]{0:T(128)S(1)} %stack.37.sc, f32[8,24,256]{2,1,0:T(8,128)} %all-to-all-done.1.refs_0_), custom_call_target="tpu_custom_call" | custom-call | bytes 196608 | tf_op jit(solution)/shard_map/pallas_call | solution.py:187
  106.2 5.4 %shard_map.142 = (bf16[128,1536]{1,0:T(8,128)(2,1)S(1)}, bf16[128,1536]{1,0:T(8,128)(2,1)}, bf16[128,1536]{1,0:T(8,128)(2,1)S(1)}, bf16[128,1536]{1,0:T(8,128)(2,1)}) custom-call(s32[6]{0:T(128)S(1)} %stack.37.sc, bf16[256,1536]{1,0:T(8,128)(2,1)S(1)} %get-tuple-element.16.k, bf16[256,1536]{1,0:T(8,128)(2,1)S(1)} %get-tuple-element.17.v, ...), custom_call_target="tpu_custom_call" | custom-call | flops 805306368 | bytes 3172352 | tf_op jit(solution)/shard_map/pallas_call | solution.py:187
  111.6 0.8 copy-done.11
  112.4 2.6 %collective-permute-start.12 = (bf16[128,1536]{1,0:T(8,128)(2,1)}, bf16[128,1536]{1,0:T(8,128)(2,1)S(1)}, u32[]{:S(2)}, u32[]{:S(2)}) collective-permute-start(bf16[128,1536]{1,0:T(8,128)(2,1)} %get-tuple-element.21), channel_id=1, source_target_pairs={{0,2},{2,0},{1,3},{3,1},{4,6},{6,4},{5,7},{7,5},{8,10},{10,8},{9,1... | collective-permute-start | bytes 1179656 | tf_op jit(solution)/shard_map/ppermute | solution.py:55
  115.0 1.7 %collective-permute-done.18 = bf16[64,3072]{1,0:T(8,128)(2,1)} collective-permute-done((bf16[64,3072]{1,0:T(8,128)(2,1)}, bf16[64,3072]{1,0:T(8,128)(2,1)}, u32[]{:S(2)}, u32[]{:S(2)}) %collective-permute-start.18) | collective-permute-done | bytes 393248 | tf_op jit(solution)/shard_map/ppermute | solution.py:55
  116.7 4.5 %collective-permute-done.19 = bf16[64,3072]{1,0:T(8,128)(2,1)} collective-permute-done((bf16[64,3072]{1,0:T(8,128)(2,1)}, bf16[64,3072]{1,0:T(8,128)(2,1)}, u32[]{:S(2)}, u32[]{:S(2)}) %collective-permute-start.19) | collective-permute-done | bytes 393248 | tf_op jit(solution)/shard_map/ppermute | solution.py:55
  121.2 2.2 %fusion = bf16[8,8,3072]{2,1,0:T(8,128)(2,1)} fusion(bf16[64,3072]{1,0:T(8,128)(2,1)} %collective-permute-done.19, bf16[64,3072]{1,0:T(8,128)(2,1)} %collective-permute-done.18, bf16[64,3072]{1,0:T(8,128)(2,1)} %collective-permute-done.17, bf16[64,3072]{1,0:T(8,128)(2,1)S(1)} %copy-done.14), kind=kLoop, calls=%fused_computation.4 | loop fusion | flops 1572864 | bytes 1966080 | tf_op jit(solution)/shard_map/all_to_all | solution.py:274
  123.4 6.8 %all-to-all-start.3 = ((bf16[8,8,3072]{2,1,0:T(8,128)(2,1)}), bf16[8,8,3072]{2,1,0:T(8,128)(2,1)S(1)}, u32[]{:S(2)}, u32[]{:S(2)}) async-start(bf16[8,8,3072]{2,1,0:T(8,128)(2,1)} %fusion), calls=%async_computation.3 | async-start | bytes 786432 | tf_op jit(solution)/shard_map/all_to_all | solution.py:274
  130.3 1.0 pad_maximum_fusion.1
  131.3 10.8 %all-to-all-done.3 = bf16[8,8,3072]{2,1,0:T(8,128)(2,1)S(1)} async-done(((bf16[8,8,3072]{2,1,0:T(8,128)(2,1)}), bf16[8,8,3072]{2,1,0:T(8,128)(2,1)S(1)}, u32[]{:S(2)}, u32[]{:S(2)}) %all-to-all-start.3) | async-done | bytes 393248 | tf_op jit(solution)/shard_map/all_to_all | solution.py:274
  142.2 3.8 %collective-permute-start.20 = (f32[4,3072]{1,0:T(4,128)S(1)}, f32[4,3072]{1,0:T(4,128)S(1)}, u32[]{:S(2)}, u32[]{:S(2)}) collective-permute-start(f32[4,3072]{1,0:T(4,128)S(1)} %slice.42), channel_id=1, source_target_pairs={{0,2},{2,0},{1,3},{3,1},{4,6},{6,4},{5,7},{7,5},{8,10},{10,8},{9,1... | collective-permute-start | bytes 147464 | tf_op jit(solution)/shard_map/ppermute | solution.py:55
  146.0 1.0 pad_maximum_fusion
  147.2 0.1 reshape_reshape_squeeze.3
  147.4 0.2 rev.11
  147.7 0.1 reshape.155
  147.8 0.6 convert_element_type.60
  148.5 0.6 fusion.2
  (97 shorter events, 2.2 us)
Async XLA Ops:
  0.6 4.1 %copy-start.19 = (bf16[4,3072]{1,0:T(4,128)(2,1)S(1)}, bf16[4,3072]{1,0:T(4,128)(2,1)}, u32[]{:S(2)}) copy-start(bf16[4,3072]{1,0:T(4,128)(2,1)} %param.15) | copy-start | bytes 73732
  0.6 4.1 %copy-start.18 = (bf16[4,3072]{1,0:T(4,128)(2,1)S(1)}, bf16[4,3072]{1,0:T(4,128)(2,1)}, u32[]{:S(2)}) copy-start(bf16[4,3072]{1,0:T(4,128)(2,1)} %param.16) | copy-start | bytes 73732
  0.7 4.2 %copy-start.20 = (bf16[4,3072]{1,0:T(4,128)(2,1)S(1)}, bf16[4,3072]{1,0:T(4,128)(2,1)}, u32[]{:S(2)}) copy-start(bf16[4,3072]{1,0:T(4,128)(2,1)} %param.18) | copy-start | bytes 73732
  2.2 2.9 %copy-start.15 = (f32[1,4,24,128]{3,2,1,0:T(8,128)}, f32[1,4,24,128]{3,2,1,0:T(8,128)S(1)}, u32[]{:S(2)}) copy-start(f32[1,4,24,128]{3,2,1,0:T(8,128)S(1)} %broadcast_bitcast_fusion.2) | copy-start | bytes 147460
  3.5 5.2 %copy-start.21 = (bf16[4,3072]{1,0:T(4,128)(2,1)S(1)}, bf16[4,3072]{1,0:T(4,128)(2,1)}, u32[]{:S(2)}) copy-start(bf16[4,3072]{1,0:T(4,128)(2,1)} %param.17) | copy-start | bytes 73732
  5.1 13.0 %copy-start.4 = (bf16[128,3072]{1,0:T(8,128)(2,1)S(1)}, bf16[128,3072]{1,0:T(8,128)(2,1)}, u32[]{:S(2)}) copy-start(bf16[128,3072]{1,0:T(8,128)(2,1)} %v0.1) | copy-start | bytes 2359300
  5.3 4.2 %collective-permute-start.4 = (bf16[4,3072]{1,0:T(4,128)(2,1)S(1)}, bf16[4,3072]{1,0:T(4,128)(2,1)S(1)}, u32[]{:S(2)}, u32[]{:S(2)}) collective-permute-start(bf16[4,3072]{1,0:T(4,128)(2,1)S(1)} %bitcast.75), channel_id=1, source_target_pairs={{0,2},{2,0},{1,3},{3,1},{4,6},{6,4},{5,7},{7,5},{8,10},{10,8},{9,1... | collective-permute-start | bytes 73736 | tf_op jit(solution)/shard_map/ppermute | solution.py:55
  9.5 8.1 %copy-start = (bf16[128,3072]{1,0:T(8,128)(2,1)S(1)}, bf16[128,3072]{1,0:T(8,128)(2,1)}, u32[]{:S(2)}) copy-start(bf16[128,3072]{1,0:T(8,128)(2,1)} %q0.1) | copy-start | bytes 2359300
  9.5 8.2 %copy-start.2 = (bf16[128,3072]{1,0:T(8,128)(2,1)S(1)}, bf16[128,3072]{1,0:T(8,128)(2,1)}, u32[]{:S(2)}) copy-start(bf16[128,3072]{1,0:T(8,128)(2,1)} %k0.1) | copy-start | bytes 2359300
  10.3 21.6 %all-to-all-start = ((bf16[8,8,3072]{2,1,0:T(8,128)(2,1)}), bf16[8,8,3072]{2,1,0:T(8,128)(2,1)S(1)}, u32[]{:S(2)}, u32[]{:S(2)}) async-start(bf16[8,8,3072]{2,1,0:T(8,128)(2,1)} %broadcast_in_dim.18), calls=%async_computation | async-start | bytes 786432 | tf_op jit(solution)/shard_map/all_to_all | solution.py:229
  16.9 1.8 %collective-permute-start.13 = (bf16[4,3072]{1,0:T(4,128)(2,1)S(1)}, bf16[4,3072]{1,0:T(4,128)(2,1)S(1)}, u32[]{:S(2)}, u32[]{:S(2)}) collective-permute-start(bf16[4,3072]{1,0:T(4,128)(2,1)S(1)} %bitcast.74), channel_id=1, source_target_pairs={{0,2},{2,0},{1,3},{3,1},{4,6},{6,4},{5,7},{7,5},{8,10},{10,8},{9,1... | collective-permute-start | bytes 73736 | tf_op jit(solution)/shard_map/ppermute | solution.py:55
  17.6 22.1 %collective-permute-start = (bf16[128,3072]{1,0:T(8,128)(2,1)S(1)}, bf16[128,3072]{1,0:T(8,128)(2,1)}, u32[]{:S(2)}, u32[]{:S(2)}) collective-permute-start(bf16[128,3072]{1,0:T(8,128)(2,1)S(1)} %copy-done), channel_id=1, source_target_pairs={{0,2},{2,0},{1,3},{3,1},{4,6},{6,4},{5,7},{7,5},{8,10},{10,8},{9,1... | collective-permute-start | bytes 2359304 | tf_op jit(solution)/shard_map/ppermute | solution.py:55
  17.7 22.4 %collective-permute-start.1 = (bf16[128,3072]{1,0:T(8,128)(2,1)S(1)}, bf16[128,3072]{1,0:T(8,128)(2,1)}, u32[]{:S(2)}, u32[]{:S(2)}) collective-permute-start(bf16[128,3072]{1,0:T(8,128)(2,1)S(1)} %copy-done.2), channel_id=1, source_target_pairs={{0,2},{2,0},{1,3},{3,1},{4,6},{6,4},{5,7},{7,5},{8,10},{10,8},{9,1... | collective-permute-start | bytes 2359304 | tf_op jit(solution)/shard_map/ppermute | solution.py:55
  18.1 33.1 %collective-permute-start.2 = (bf16[128,3072]{1,0:T(8,128)(2,1)S(1)}, bf16[128,3072]{1,0:T(8,128)(2,1)}, u32[]{:S(2)}, u32[]{:S(2)}) collective-permute-start(bf16[128,3072]{1,0:T(8,128)(2,1)S(1)} %copy-done.4), channel_id=1, source_target_pairs={{0,2},{2,0},{1,3},{3,1},{4,6},{6,4},{5,7},{7,5},{8,10},{10,8},{9,1... | collective-permute-start | bytes 2359304 | tf_op jit(solution)/shard_map/ppermute | solution.py:55
  18.2 35.7 %collective-permute-start.3 = (bf16[128,3072]{1,0:T(8,128)(2,1)}, bf16[128,3072]{1,0:T(8,128)(2,1)}, u32[]{:S(2)}, u32[]{:S(2)}) collective-permute-start(bf16[128,3072]{1,0:T(8,128)(2,1)} %d0.1), channel_id=1, source_target_pairs={{0,2},{2,0},{1,3},{3,1},{4,6},{6,4},{5,7},{7,5},{8,10},{10,8},{9,1... | collective-permute-start | bytes 2359304 | tf_op jit(solution)/shard_map/ppermute | solution.py:55
  32.7 18.5 %all-to-all-start.2 = ((bf16[8,8,3072]{2,1,0:T(8,128)(2,1)}), bf16[8,8,3072]{2,1,0:T(8,128)(2,1)S(1)}, u32[]{:S(2)}, u32[]{:S(2)}) async-start(bf16[8,8,3072]{2,1,0:T(8,128)(2,1)} %broadcast_in_dim.20), calls=%async_computation.2 | async-start | bytes 786432 | tf_op jit(solution)/shard_map/all_to_all | solution.py:229
  36.1 18.4 %collective-permute-start.5 = (bf16[64,3072]{1,0:T(8,128)(2,1)S(1)}, bf16[64,3072]{1,0:T(8,128)(2,1)S(1)}, u32[]{:S(2)}, u32[]{:S(2)}) collective-permute-start(bf16[64,3072]{1,0:T(8,128)(2,1)S(1)} %bitcast.63), channel_id=1, source_target_pairs={{0,33},{1,0},{32,1},{33,32},{2,35},{3,2},{34,3},{35,34},{4,37},{5,... | collective-permute-start | bytes 1179656 | tf_op jit(solution)/shard_map/ppermute | solution.py:55
  39.7 24.1 %collective-permute-start.6 = (bf16[64,3072]{1,0:T(8,128)(2,1)S(1)}, bf16[64,3072]{1,0:T(8,128)(2,1)S(1)}, u32[]{:S(2)}, u32[]{:S(2)}) collective-permute-start(bf16[64,3072]{1,0:T(8,128)(2,1)S(1)} %bitcast.64), channel_id=1, source_target_pairs={{0,32},{1,33},{32,0},{33,1},{2,34},{3,35},{34,2},{35,3},{4,36},{5,... | collective-permute-start | bytes 1179656 | tf_op jit(solution)/shard_map/ppermute | solution.py:55
  40.1 23.7 %collective-permute-start.7 = (bf16[64,3072]{1,0:T(8,128)(2,1)S(1)}, bf16[64,3072]{1,0:T(8,128)(2,1)S(1)}, u32[]{:S(2)}, u32[]{:S(2)}) collective-permute-start(bf16[64,3072]{1,0:T(8,128)(2,1)S(1)} %bitcast.65), channel_id=1, source_target_pairs={{0,1},{1,32},{32,33},{33,0},{2,3},{3,34},{34,35},{35,2},{4,5},{5,3... | collective-permute-start | bytes 1179656 | tf_op jit(solution)/shard_map/ppermute | solution.py:55
  51.2 38.7 %collective-permute-start.14 = (bf16[64,3072]{1,0:T(8,128)(2,1)S(1)}, bf16[64,3072]{1,0:T(8,128)(2,1)}, u32[]{:S(2)}, u32[]{:S(2)}) collective-permute-start(bf16[64,3072]{1,0:T(8,128)(2,1)S(1)} %bitcast.68), channel_id=1, source_target_pairs={{0,33},{1,0},{32,1},{33,32},{2,35},{3,2},{34,3},{35,34},{4,37},{5,... | collective-permute-start | bytes 1179656 | tf_op jit(solution)/shard_map/ppermute | solution.py:55
  53.9 36.0 %collective-permute-start.15 = (bf16[64,3072]{1,0:T(8,128)(2,1)S(1)}, bf16[64,3072]{1,0:T(8,128)(2,1)}, u32[]{:S(2)}, u32[]{:S(2)}) collective-permute-start(bf16[64,3072]{1,0:T(8,128)(2,1)S(1)} %bitcast.69), channel_id=1, source_target_pairs={{0,32},{1,33},{32,0},{33,1},{2,34},{3,35},{34,2},{35,3},{4,36},{5,... | collective-permute-start | bytes 1179656 | tf_op jit(solution)/shard_map/ppermute | solution.py:55
  54.5 35.5 %collective-permute-start.16 = (bf16[64,3072]{1,0:T(8,128)(2,1)S(1)}, bf16[64,3072]{1,0:T(8,128)(2,1)}, u32[]{:S(2)}, u32[]{:S(2)}) collective-permute-start(bf16[64,3072]{1,0:T(8,128)(2,1)S(1)} %bitcast.70), channel_id=1, source_target_pairs={{0,1},{1,32},{32,33},{33,0},{2,3},{3,34},{34,35},{35,2},{4,5},{5,3... | collective-permute-start | bytes 1179656 | tf_op jit(solution)/shard_map/ppermute | solution.py:55
  55.2 1.1 copy-start.1
  56.3 1.1 copy-start.3
  57.4 1.1 copy-start.5
  58.6 1.1 copy-start.6
  63.8 3.3 %copy-start.7 = (bf16[256,1536]{1,0:T(8,128)(2,1)}, bf16[256,1536]{1,0:T(8,128)(2,1)S(1)}, u32[]{:S(2)}) copy-start(bf16[256,1536]{1,0:T(8,128)(2,1)S(1)} %get-tuple-element.22.q) | copy-start | bytes 2359300
  63.8 3.3 %copy-start.9 = (bf16[256,1536]{1,0:T(8,128)(2,1)}, bf16[256,1536]{1,0:T(8,128)(2,1)S(1)}, u32[]{:S(2)}) copy-start(bf16[256,1536]{1,0:T(8,128)(2,1)S(1)} %get-tuple-element.23.d) | copy-start | bytes 2359300
  67.1 10.9 %collective-permute-start.10 = (f32[24,256]{1,0:T(8,128)S(1)}, f32[24,256]{1,0:T(8,128)S(1)}, u32[]{:S(2)}, u32[]{:S(2)}) collective-permute-start(f32[24,256]{1,0:T(8,128)S(1)} %shard_map.139.refs_0_), channel_id=1, source_target_pairs={{0,1},{1,32},{32,33},{33,0},{2,3},{3,34},{34,35},{35,2},{4,5},{5,3... | collective-permute-start | bytes 73736 | tf_op jit(solution)/shard_map/ppermute | solution.py:55
  68.8 9.7 %collective-permute-start.8 = (f32[24,256]{1,0:T(8,128)S(1)}, f32[24,256]{1,0:T(8,128)S(1)}, u32[]{:S(2)}, u32[]{:S(2)}) collective-permute-start(f32[24,256]{1,0:T(8,128)S(1)} %shard_map.139.refs_0_), channel_id=1, source_target_pairs={{0,33},{1,0},{32,1},{33,32},{2,35},{3,2},{34,3},{35,34},{4,37},{5,... | collective-permute-start | bytes 73736 | tf_op jit(solution)/shard_map/ppermute | solution.py:55
  78.0 4.2 %collective-permute-start.9 = (f32[24,256]{1,0:T(8,128)S(1)}, f32[24,256]{1,0:T(8,128)S(1)}, u32[]{:S(2)}, u32[]{:S(2)}) collective-permute-start(f32[24,256]{1,0:T(8,128)S(1)} %shard_map.139.refs_0_), channel_id=1, source_target_pairs={{0,32},{1,33},{32,0},{33,1},{2,34},{3,35},{34,2},{35,3},{4,36},{5,... | collective-permute-start | bytes 73736 | tf_op jit(solution)/shard_map/ppermute | solution.py:55
  83.4 21.2 %all-to-all-start.1 = ((f32[8,24,256]{2,1,0:T(8,128)}), f32[8,24,256]{2,1,0:T(8,128)}, u32[]{:S(2)}, u32[]{:S(2)}) async-start(f32[8,24,256]{2,1,0:T(8,128)} %broadcast_in_dim.19), calls=%async_computation.1 | async-start | bytes 393216 | tf_op jit(solution)/shard_map/all_to_all | solution.py:303
  90.0 1.1 copy-start.8
  91.1 1.1 copy-start.10
  100.6 0.8 copy-start.13
  101.3 13.7 %collective-permute-start.17 = (bf16[64,3072]{1,0:T(8,128)(2,1)}, bf16[64,3072]{1,0:T(8,128)(2,1)}, u32[]{:S(2)}, u32[]{:S(2)}) collective-permute-start(bf16[64,3072]{1,0:T(8,128)(2,1)} %get-tuple-element.25), channel_id=1, source_target_pairs={{0,1},{1,32},{32,33},{33,0},{2,3},{3,34},{34,35},{35,2},{4,5},{5,3... | collective-permute-start | bytes 1179656 | tf_op jit(solution)/shard_map/ppermute | solution.py:55
  101.3 15.4 %collective-permute-start.18 = (bf16[64,3072]{1,0:T(8,128)(2,1)}, bf16[64,3072]{1,0:T(8,128)(2,1)}, u32[]{:S(2)}, u32[]{:S(2)}) collective-permute-start(bf16[64,3072]{1,0:T(8,128)(2,1)} %get-tuple-element.26), channel_id=1, source_target_pairs={{0,32},{1,33},{32,0},{33,1},{2,34},{3,35},{34,2},{35,3},{4,36},{5,... | collective-permute-start | bytes 1179656 | tf_op jit(solution)/shard_map/ppermute | solution.py:55
  101.8 19.4 %collective-permute-start.19 = (bf16[64,3072]{1,0:T(8,128)(2,1)}, bf16[64,3072]{1,0:T(8,128)(2,1)}, u32[]{:S(2)}, u32[]{:S(2)}) collective-permute-start(bf16[64,3072]{1,0:T(8,128)(2,1)} %get-tuple-element.27), channel_id=1, source_target_pairs={{0,33},{1,0},{32,1},{33,32},{2,35},{3,2},{34,3},{35,34},{4,37},{5,... | collective-permute-start | bytes 1179656 | tf_op jit(solution)/shard_map/ppermute | solution.py:55
  106.2 15.0 %copy-start.14 = (bf16[64,3072]{1,0:T(8,128)(2,1)S(1)}, bf16[64,3072]{1,0:T(8,128)(2,1)}, u32[]{:S(2)}) copy-start(bf16[64,3072]{1,0:T(8,128)(2,1)} %copy-done.13) | copy-start | bytes 1179652
  111.6 0.8 copy-start.11
  112.4 17.8 %collective-permute-start.12 = (bf16[128,1536]{1,0:T(8,128)(2,1)}, bf16[128,1536]{1,0:T(8,128)(2,1)S(1)}, u32[]{:S(2)}, u32[]{:S(2)}) collective-permute-start(bf16[128,1536]{1,0:T(8,128)(2,1)} %get-tuple-element.21), channel_id=1, source_target_pairs={{0,2},{2,0},{1,3},{3,1},{4,6},{6,4},{5,7},{7,5},{8,10},{10,8},{9,1... | collective-permute-start | bytes 1179656 | tf_op jit(solution)/shard_map/ppermute | solution.py:55
  115.0 16.2 %collective-permute-start.11 = (bf16[128,1536]{1,0:T(8,128)(2,1)}, bf16[128,1536]{1,0:T(8,128)(2,1)S(1)}, u32[]{:S(2)}, u32[]{:S(2)}) collective-permute-start(bf16[128,1536]{1,0:T(8,128)(2,1)} %get-tuple-element.19), channel_id=1, source_target_pairs={{0,2},{2,0},{1,3},{3,1},{4,6},{6,4},{5,7},{7,5},{8,10},{10,8},{9,1... | collective-permute-start | bytes 1179656 | tf_op jit(solution)/shard_map/ppermute | solution.py:55
  123.4 6.8 %copy-start.12 = (bf16[128,1536]{1,0:T(8,128)(2,1)S(1)}, bf16[128,1536]{1,0:T(8,128)(2,1)}, u32[]{:S(2)}) copy-start(bf16[128,1536]{1,0:T(8,128)(2,1)} %copy-done.11) | copy-start | bytes 1179652
  123.4 18.7 %all-to-all-start.3 = ((bf16[8,8,3072]{2,1,0:T(8,128)(2,1)}), bf16[8,8,3072]{2,1,0:T(8,128)(2,1)S(1)}, u32[]{:S(2)}, u32[]{:S(2)}) async-start(bf16[8,8,3072]{2,1,0:T(8,128)(2,1)} %fusion), calls=%async_computation.3 | async-start | bytes 786432 | tf_op jit(solution)/shard_map/all_to_all | solution.py:274
  142.2 4.8 %collective-permute-start.20 = (f32[4,3072]{1,0:T(4,128)S(1)}, f32[4,3072]{1,0:T(4,128)S(1)}, u32[]{:S(2)}, u32[]{:S(2)}) collective-permute-start(f32[4,3072]{1,0:T(4,128)S(1)} %slice.42), channel_id=1, source_target_pairs={{0,2},{2,0},{1,3},{3,1},{4,6},{6,4},{5,7},{7,5},{8,10},{10,8},{9,1... | collective-permute-start | bytes 147464 | tf_op jit(solution)/shard_map/ppermute | solution.py:55
  147.0 1.5 %copy-start.16 = (f32[1,4,24,128]{3,2,1,0:T(8,128)S(1)}, f32[1,4,24,128]{3,2,1,0:T(8,128)}, u32[]{:S(2)}) copy-start(f32[1,4,24,128]{3,2,1,0:T(8,128)} %copy-done.15) | copy-start | bytes 147460
  147.0 1.5 %copy-start.17 = (f32[1,4,24,128]{3,2,1,0:T(8,128)S(1)}, f32[1,4,24,128]{3,2,1,0:T(8,128)}, u32[]{:S(2)}) copy-start(f32[1,4,24,128]{3,2,1,0:T(8,128)} %broadcast_bitcast_fusion) | copy-start | bytes 147460

commit v2 on v1

--- a/solution.py
+++ b/solution.py
@@ -2,6 +2,7 @@
 
 import jax
 import jax.numpy as jnp
+import numpy as np
 from jax import lax
 from jax.experimental import pallas as pl
 from jax.experimental.pallas import tpu as pltpu
@@ -24,6 +25,7 @@
 AR = 4
 CR = NC * AR
 ZR = NZ * CR
+YR = NY * CR
 AUDIO = NY * ZR
 
 ALL = ("dp", "yh", "z", "core", "yl")
@@ -83,18 +85,19 @@
         dr[rows, :] = jnp.where(token < limit, d[...].astype(f32), 0.0).astype(bf16)
 
 
-def video_to_audio_kernel(sc, q, d, a0, a1, a2, a3, o0, o1, o2, o3):
-    core, y, limit = sc[0], sc[1], sc[2]
+def video_to_audio_kernel(sc, q, d, *refs):
+    blocks, outs = refs[:-NY], refs[-NY:]
+    core, y, limit, z = sc[0], sc[1], sc[2], sc[6]
     row = lax.broadcasted_iota(jnp.int32, (AUDIO, 2 * VT), 0)
-    yy = (row // ZR + y) % NY
-    zz = (row // CR) % NZ
+    zz = (row // YR + z) % NZ
+    yy = (row // CR + y) % NY
     r = row % CR
     cc = jnp.where(r < AR, core, 1 - core)
     own = ((yy // 2 * NZ + zz) * NC + cc) * 2 + yy % 2
     valid = own * AR + r % AR < limit
     for i in range(HPG):
-        key = jnp.concatenate([a[:, head(i)] for a in (a0, a1, a2, a3)], 0)
-        value = jnp.concatenate([a[:, head(HPG + i)] for a in (a0, a1, a2, a3)], 0)
+        key = jnp.concatenate([a[:, head(i)] for a in blocks], 0)
+        value = jnp.concatenate([a[:, head(HPG + i)] for a in blocks], 0)
         query, grad = q[:, head(i)], d[:, head(i)]
         s = jnp.where(valid, nt(key, query) * SCALE, NEG)
         e = jnp.exp(s - jnp.max(s, axis=0, keepdims=True))
@@ -103,11 +106,48 @@
         dp = nt(value, grad)
         delta = jnp.sum(pb.astype(f32) * dp, axis=0, keepdims=True)
         ds = (p * (dp - delta) * SCALE).astype(bf16)
-        dk = nn(ds, query).astype(bf16)
-        dv = nn(pb, grad).astype(bf16)
-        for n, o in enumerate((o0, o1, o2, o3)):
-            o[:, head(i)] = dk[n * ZR : (n + 1) * ZR]
-            o[:, head(HPG + i)] = dv[n * ZR : (n + 1) * ZR]
+        dk = nn(ds, query).reshape(NZ, NY, CR, HD)
+        dv = nn(pb, grad).reshape(NZ, NY, CR, HD)
+        for n, o in enumerate(outs):
+            o[:, head(i)] = dk[:, n].reshape(ZR, HD).astype(bf16)
+            o[:, head(HPG + i)] = dv[:, n].reshape(ZR, HD).astype(bf16)
+
+
+def sum_kernel(sc, p0, p1, p2, p3, out, twice):
+    total = sum(p[...].astype(f32) for p in (p0, p1, p2, p3))
+    twice[:ZR, :] = total
+    twice[ZR:, :] = total
+    start = pl.multiple_of(lax.rem(NZ - sc[6], NZ) * CR, CR)
+    out[...] = twice[pl.ds(start, ZR), :].astype(bf16)
+
+
+def audio_kernel(sc, q, k, v, d, freq, keep, give):
+    core, own = sc[0], sc[7]
+    row = lax.broadcasted_iota(jnp.int32, (AR, HD), 0)
+    lane = lax.broadcasted_iota(jnp.int32, (AR, HD), 1)
+    pos = functools.reduce(lambda a, n: jnp.where(row == n, sc[8 + n], a), range(1, AR), sc[8])
+    angle = pos.astype(f32) * freq[...]
+    cosine = jnp.cos(angle)
+    sine = jnp.where(lane < HD // 2, -jnp.sin(angle), jnp.sin(angle))
+    ours = own * AR + row < sc[2]
+
+    def turn(x):
+        x = x.astype(f32)
+        swapped = jnp.concatenate([x[:, HD // 2 :], x[:, : HD // 2]], 1)
+        return x * cosine + swapped * sine
+
+    def pair(ref, n, change):
+        return [change(ref[:, head(c * HEADS + n)]) for c in range(NC)]
+
+    same = lambda x: x.astype(f32)
+    clear = lambda x: jnp.where(ours, x.astype(f32), 0.0)
+    for n in range(HEADS):
+        base = n // HPG * 2 * GW + n % HPG * HD
+        for at, ref, change in ((0, k, turn), (GW, v, same), (2 * CW, q, turn), (2 * CW + GW, d, clear)):
+            a, b = pair(ref, n, change)
+            lanes = slice(base + at, base + at + HD)
+            keep[:, lanes] = jnp.where(core == 0, a, b).astype(bf16)
+            give[:, lanes] = jnp.where(core == 0, b, a).astype(bf16)
 
 
 def video_mask(sc):
@@ -182,15 +222,15 @@
             dvo[:, head(i)] = dv[rows].astype(bf16)
 
 
-def call(kernel, scalars, args, specs, outs, out_specs, grid=(GROUPS,), flops=0):
+def call(kernel, scalars, args, specs, outs, out_specs, grid=(GROUPS,), flops=0, scratch=()):
     size = sum(x.size * x.dtype.itemsize for x in args)
     return pl.pallas_call(
         kernel,
         grid_spec=pltpu.PrefetchScalarGridSpec(
-            num_scalar_prefetch=1, grid=grid, in_specs=specs, out_specs=out_specs
+            num_scalar_prefetch=1, grid=grid, in_specs=specs, out_specs=out_specs, scratch_shapes=scratch
         ),
         out_shape=outs,
-        compiler_params=pltpu.CompilerParams(vmem_limit_bytes=40 * 1024 * 1024),
+        compiler_params=pltpu.CompilerParams(vmem_limit_bytes=16 * 1024 * 1024),
         cost_estimate=pl.CostEstimate(flops=flops, bytes_accessed=size, transcendentals=0),
     )(scalars, *args)
 
@@ -201,38 +241,40 @@
     own = ((yh * NZ + z) * NC + core) * 2 + yl
     pair = ((yh * NZ + z) * NC + 1 - core) * 2 + yl
     scalars = jnp.stack(
-        [core, y, audio_len[0], video_len[0], own * VT, pair * VT]
+        [core, y, audio_len[0], video_len[0], own * VT, pair * VT, z, own, *audio_pos]
     ).astype(jnp.int32)
     first = core == 0
 
     audio_cos, audio_sin = turn_tables(audio_pos)
-    ours = own * AR + jnp.arange(AR, dtype=jnp.int32) < audio_len[0]
-    q_rot = rotate_rows(q_audio, audio_cos, audio_sin).astype(bf16)
-    k_rot = rotate_rows(k_audio, audio_cos, audio_sin).astype(bf16)
-    d_own = jnp.where(ours[:, None], d_audio, jnp.zeros_like(d_audio))
-
-    def packed(a, b):
-        a = a.reshape(AR, NC, GROUPS, 1, GW)
-        b = b.reshape(AR, NC, GROUPS, 1, GW)
-        both = jnp.concatenate([a, b], 3).reshape(AR, NC, 2 * CW)
-        keep = jnp.where(first, both[:, 0], both[:, 1])
-        give = jnp.where(first, both[:, 1], both[:, 0])
-        return keep, give
-
-    keep_kv, give_kv = packed(k_rot, v_audio)
-    keep_qd, give_qd = packed(q_rot, d_own)
-    kv = jnp.concatenate([keep_kv, shift(give_kv, "core", NC, 1)], 0)
-    qd = jnp.concatenate([keep_qd, shift(give_qd, "core", NC, 1)], 0)
-
-    def along_z(x):
-        copies = jnp.broadcast_to(x[None], (NZ,) + x.shape).reshape(ZR, 2 * CW)
-        return lax.all_to_all(copies, "z", split_axis=0, concat_axis=0, tiled=True)
+
+    frequency = np.tile(ROPE_BASE ** (-np.arange(HD // 2) / (HD // 2)), 2).astype(np.float32)
+    whole = pl.BlockSpec((AR, NC * CW), lambda g, sc: (0, 0))
+    wide = pl.BlockSpec((AR, 4 * CW), lambda g, sc: (0, 0))
+    keep, give = call(
+        audio_kernel,
+        scalars,
+        (q_audio, k_audio, v_audio, d_audio, frequency[None]),
+        [whole] * 4 + [pl.BlockSpec((1, HD), lambda g, sc: (0, 0))],
+        [jax.ShapeDtypeStruct((AR, 4 * CW), bf16)] * 2,
+        [wide] * 2,
+        grid=(1,),
+    )
+    chip = jnp.concatenate([keep, shift(give, "core", NC, 1)], 0)
+    kv, qd = chip[:, : 2 * CW], chip[:, 2 * CW :]
 
     def along_y(x):
         return [x] + [shift(x, Y, NY, NY - n) for n in range(1, NY)]
 
-    kv_all = along_y(along_z(kv))
-    qd_all = along_y(along_z(qd))
+    home = jnp.concatenate(along_y(kv), 0)
+    up, down = [home], [home]
+    for _ in range(3):
+        up.append(shift(up[-1], "z", NZ, NZ - 1))
+        down.append(shift(down[-1], "z", NZ, 1))
+    far = [shift(up[-1][: YR // 2], "z", NZ, NZ - 1), shift(down[-1][YR // 2 :], "z", NZ, 1)]
+    kv_all = up + far + down[:0:-1]
+
+    copies = jnp.broadcast_to(qd[None], (NZ,) + qd.shape).reshape(ZR, 2 * CW)
+    qd_all = along_y(lax.all_to_all(copies, "z", split_axis=0, concat_axis=0, tiled=True))
 
     q_pair, k_pair, v_pair, d_pair = (
         shift(x, "core", NC, 1) for x in (q_video, k_video, v_video, d_video)
@@ -263,15 +305,21 @@
         video_to_audio_kernel,
         scalars,
         (qr, dr, *kv_all),
-        [video] * 2 + [audio] * NY,
+        [video] * 2 + [pl.BlockSpec((x.shape[0], 2 * GW), lambda g, sc: (0, g)) for x in kv_all],
         [audio_shape] * NY,
         [audio] * NY,
         flops=4 * one,
     )
-    sums = parts[0].astype(f32)
-    for n in range(1, NY):
-        sums = sums + shift(parts[n], Y, NY, n).astype(f32)
-    sums = lax.all_to_all(sums.astype(bf16), "z", split_axis=0, concat_axis=0, tiled=True)
+    sums = call(
+        sum_kernel,
+        scalars,
+        [parts[0]] + [shift(parts[n], Y, NY, n) for n in range(1, NY)],
+        [audio] * NY,
+        audio_shape,
+        audio,
+        scratch=[pltpu.VMEM((2 * ZR, 2 * GW), f32)],
+    )
+    sums = lax.all_to_all(sums, "z", split_axis=0, concat_axis=0, tiled=True)
     sums = jnp.sum(sums.reshape(NZ, CR, 2 * CW).astype(f32), 0)
     other = shift(sums[AR:], "core", NC, 1)
     sums = sums[:AR]

time: 150 us -> 151 us (level)
  waiting for transfers between devices: 52.2 us -> 34 us
  starting transfers between devices: 49.1 us -> 61.7 us
  local copies, waits for them, and re-layouts: 15.5 us -> 20.6 us
  Pallas kernels: 23.2 us -> 26.4 us
  other arithmetic: 6.73 us -> 4.28 us
    all_to_all x3 -> x2, waiting for transfers between devices: 34.3 us -> 0.01 us  [the longest x1 0.01 us: local(): lax.all_to_all(copies, 'z', split_axis=0, concat_axis=0, tiled=True)]
    ppermute x21 -> x28, starting transfers between devices: 25.9 us -> 48.4 us  [shift(): return lax.ppermute(x, axis, [(i, (i + step) % size) for i in range(size)])]
    ppermute x21 -> x28, waiting for transfers between devices: 17.9 us -> 30.5 us  [shift(): return lax.ppermute(x, axis, [(i, (i + step) % size) for i in range(size)])]
    all_to_all x3 -> x2, starting transfers between devices: 16.7 us -> 7.54 us  [the longest x1 4.08 us: local(): sums = lax.all_to_all(sums, 'z', split_axis=0, concat_axis=0, tiled=True)]
    unnamed x52 -> x65, local copies, waits for them, and re-layouts: 9.08 us -> 16.1 us
    all_to_all x1, waiting for transfers between devices: 0.01 us -> 3.55 us  [local(): stats = lax.all_to_all(copies, 'z', split_axis=0, concat_axis=0, tiled=True)]
    pallas_call x6 -> x8, Pallas kernels: 23.2 us -> 26.4 us  [call(): pl.pallas_call(kernel, grid_spec=pltpu.PrefetchScalarGridSpec(num_scalar_...]
    all_to_all x1 -> x0, other arithmetic: 2.19 us -> none  [local(): lax.all_to_all(sums.astype(bf16), 'z', split_axis=0, concat_axis=0, tiled...]
  transfers between devices with their start and end apart: 25 -> 31, of which waited for: 9 -> 11; matrix products, arithmetic and copies ran while one was open for 5% -> 4% of each run, Pallas kernels for 16% -> 17%
where the time goes in v2:
time: 151 us; the launch traced here: 149 us
  starting transfers between devices  61.7 us (41%)
  waiting for transfers between devices  34 us (23%)
  Pallas kernels  26.4 us (17%)
  local copies, waits for them, and re-layouts  20.6 us (14%)
  other arithmetic  4.28 us (3%)
  between operations  2.3 us (2%)
    ppermute x28, starting transfers between devices, shift(): return lax.ppermute(x, axis, [(i, (i + step) % size) for i in range(size)])  48.4 us
    ppermute x28, waiting for transfers between devices, shift(): return lax.ppermute(x, axis, [(i, (i + step) % size) for i in range(size)])  30.5 us
    pallas_call x8, Pallas kernels, call(): pl.pallas_call(kernel, grid_spec=pltpu.PrefetchScalarGridSpec(num_scalar_...  26.4 us
    unnamed x65, local copies, waits for them, and re-layouts  16.1 us
    all_to_all x1, starting transfers between devices, local(): stats = lax.all_to_all(copies, 'z', split_axis=0, concat_axis=0, tiled=True)  5.81 us
    all_to_all x1, starting transfers between devices, local(): sums = lax.all_to_all(sums, 'z', split_axis=0, concat_axis=0, tiled=True)  4.08 us
    all_to_all x1, waiting for transfers between devices, local(): stats = lax.all_to_all(copies, 'z', split_axis=0, concat_axis=0, tiled=True)  3.55 us
    all_to_all x1, starting transfers between devices, local(): lax.all_to_all(copies, 'z', split_axis=0, concat_axis=0, tiled=True)  3.45 us
  transfers between devices with their start and end apart: 31, of which 11 were waited for; matrix products, arithmetic and copies ran while one was open for 4% of the time, Pallas kernels for 17%

profile of v2, /device:TPU:1, one launch (start us, length us, event | category | flops | bytes accessed | tf_op | source)
XLA Modules:
  0.0 149.4 jit_solution(13703429782472587156)
XLA Ops:
  1.9 0.7 stack.45.sc
  2.7 0.7 copy-done.24
  3.4 0.7 copy-done.25
  4.2 0.7 copy-done.26
  4.9 0.7 copy-done.27
  5.6 0.7 copy-done.28
  6.3 0.6 shard_map.148
  6.9 3.3 %collective-permute-start.4 = (bf16[4,6144]{1,0:T(4,128)(2,1)S(1)}, bf16[4,6144]{1,0:T(4,128)(2,1)S(1)}, u32[]{:S(2)}, u32[]{:S(2)}) collective-permute-start(bf16[4,6144]{1,0:T(4,128)(2,1)S(1)} %get-tuple-element.21), channel_id=1, source_target_pairs={{0,2},{2,0},{1,3},{3,1},{4,6},{6,4},{5,7},{7,5},{8,10},{10,8},{9,1... | collective-permute-start | bytes 147464 | tf_op jit(solution)/shard_map/ppermute | solution.py:57
  10.3 0.9 collective-permute-done.4
  11.2 1.1 collective-permute-start.13
  12.6 0.7 collective-permute-start.15
  13.3 0.9 collective-permute-done.13
  14.2 2.6 %collective-permute-done.14 = bf16[8,3072]{1,0:T(8,128)(2,1)S(1)} collective-permute-done((bf16[8,3072]{1,0:T(8,128)(2,1)S(1)}, bf16[8,3072]{1,0:T(8,128)(2,1)S(1)}, u32[]{:S(2)}, u32[]{:S(2)}) %collective-permute-start.14) | collective-permute-done | bytes 49184 | tf_op jit(solution)/shard_map/ppermute | solution.py:57
  17.3 5.7 %collective-permute-start.16 = (bf16[32,3072]{1,0:T(8,128)(2,1)S(1)}, bf16[32,3072]{1,0:T(8,128)(2,1)S(1)}, u32[]{:S(2)}, u32[]{:S(2)}) collective-permute-start(bf16[32,3072]{1,0:T(8,128)(2,1)S(1)} %pad_maximum_fusion.2.refs_0_), channel_id=1, source_target_pairs={{0,28},{4,0},{8,4},{12,8},{16,12},{20,16},{24,20},{28,24},{1,29},{... | collective-permute-start | bytes 589832 | tf_op jit(solution)/shard_map/ppermute | solution.py:57
  22.9 2.1 %collective-permute-start = (bf16[128,3072]{1,0:T(8,128)(2,1)}, bf16[128,3072]{1,0:T(8,128)(2,1)S(1)}, u32[]{:S(2)}, u32[]{:S(2)}) collective-permute-start(bf16[128,3072]{1,0:T(8,128)(2,1)} %q0.1), channel_id=1, source_target_pairs={{0,2},{2,0},{1,3},{3,1},{4,6},{6,4},{5,7},{7,5},{8,10},{10,8},{9,1... | collective-permute-start | bytes 2359304 | tf_op jit(solution)/shard_map/ppermute | solution.py:57
  25.6 3.1 %collective-permute-start.17 = (bf16[32,3072]{1,0:T(8,128)(2,1)S(1)}, bf16[32,3072]{1,0:T(8,128)(2,1)S(1)}, u32[]{:S(2)}, u32[]{:S(2)}) collective-permute-start(bf16[32,3072]{1,0:T(8,128)(2,1)S(1)} %collective-permute-done.16.refs_1_), channel_id=1, source_target_pairs={{0,28},{4,0},{8,4},{12,8},{16,12},{20,16},{24,20},{28,24},{1,29},{... | collective-permute-start | bytes 589832 | tf_op jit(solution)/shard_map/ppermute | solution.py:57
  28.7 0.8 broadcast_in_dim.4
  29.4 3.5 %all-to-all-start = ((bf16[8,8,3072]{2,1,0:T(8,128)(2,1)}), bf16[8,8,3072]{2,1,0:T(8,128)(2,1)S(1)}, u32[]{:S(2)}, u32[]{:S(2)}) async-start(bf16[8,8,3072]{2,1,0:T(8,128)(2,1)} %broadcast_in_dim.4), calls=%async_computation | async-start | bytes 786432 | tf_op jit(solution)/shard_map/all_to_all | solution.py:277
  32.9 1.4 collective-permute-start.21
  34.3 0.7 copy-done.18
  34.9 3.8 %collective-permute-start.2 = (bf16[128,3072]{1,0:T(8,128)(2,1)S(1)}, bf16[128,3072]{1,0:T(8,128)(2,1)}, u32[]{:S(2)}, u32[]{:S(2)}) collective-permute-start(bf16[128,3072]{1,0:T(8,128)(2,1)S(1)} %copy-done.2), channel_id=1, source_target_pairs={{0,2},{2,0},{1,3},{3,1},{4,6},{6,4},{5,7},{7,5},{8,10},{10,8},{9,1... | collective-permute-start | bytes 2359304 | tf_op jit(solution)/shard_map/ppermute | solution.py:57
  39.4 7.0 %collective-permute-done.21.refs_7_ = bf16[32,3072]{1,0:T(8,128)(2,1)S(1)} collective-permute-done((bf16[32,3072]{1,0:T(8,128)(2,1)S(1)}, bf16[32,3072]{1,0:T(8,128)(2,1)S(1)}, u32[]{:S(2)}, u32[]{:S(2)}) %collective-permute-start.21) | collective-permute-done | bytes 196640 | tf_op jit(solution)/shard_map/ppermute | solution.py:57
  46.4 0.7 copy-done.22
  47.1 1.5 %collective-permute-start.18 = (bf16[32,3072]{1,0:T(8,128)(2,1)}, bf16[32,3072]{1,0:T(8,128)(2,1)S(1)}, u32[]{:S(2)}, u32[]{:S(2)}) collective-permute-start(bf16[32,3072]{1,0:T(8,128)(2,1)} %copy-done.20), channel_id=1, source_target_pairs={{0,28},{4,0},{8,4},{12,8},{16,12},{20,16},{24,20},{28,24},{1,29},{... | collective-permute-start | bytes 589832 | tf_op jit(solution)/shard_map/ppermute | solution.py:57
  48.6 3.2 %collective-permute-done.18.refs_3_ = bf16[32,3072]{1,0:T(8,128)(2,1)S(1)} collective-permute-done((bf16[32,3072]{1,0:T(8,128)(2,1)}, bf16[32,3072]{1,0:T(8,128)(2,1)S(1)}, u32[]{:S(2)}, u32[]{:S(2)}) %collective-permute-start.18) | collective-permute-done | bytes 196640 | tf_op jit(solution)/shard_map/ppermute | solution.py:57
  51.9 5.9 %collective-permute-done.22.refs_6_ = bf16[32,3072]{1,0:T(8,128)(2,1)S(1)} collective-permute-done((bf16[32,3072]{1,0:T(8,128)(2,1)}, bf16[32,3072]{1,0:T(8,128)(2,1)S(1)}, u32[]{:S(2)}, u32[]{:S(2)}) %collective-permute-start.22) | collective-permute-done | bytes 196640 | tf_op jit(solution)/shard_map/ppermute | solution.py:57
  57.8 0.7 copy-done.8
  58.5 2.0 %collective-permute-start.5 = (bf16[64,3072]{1,0:T(8,128)(2,1)S(1)}, bf16[64,3072]{1,0:T(8,128)(2,1)S(1)}, u32[]{:S(2)}, u32[]{:S(2)}) collective-permute-start(bf16[64,3072]{1,0:T(8,128)(2,1)S(1)} %bitcast.30), channel_id=1, source_target_pairs={{0,33},{1,0},{32,1},{33,32},{2,35},{3,2},{34,3},{35,34},{4,37},{5,... | collective-permute-start | bytes 1179656 | tf_op jit(solution)/shard_map/ppermute | solution.py:57
  60.4 0.9 copy-done.6
  61.9 0.9 collective-permute-start.7
  62.9 0.9 slice.37
  63.8 1.5 %collective-permute-start.19 = (bf16[16,3072]{1,0:T(8,128)(2,1)S(1)}, bf16[16,3072]{1,0:T(8,128)(2,1)S(1)}, u32[]{:S(2)}, u32[]{:S(2)}) collective-permute-start(bf16[16,3072]{1,0:T(8,128)(2,1)S(1)} %slice.36), channel_id=1, source_target_pairs={{0,28},{4,0},{8,4},{12,8},{16,12},{20,16},{24,20},{28,24},{1,29},{... | collective-permute-start | bytes 294920 | tf_op jit(solution)/shard_map/ppermute | solution.py:57
  65.5 1.1 copy-done
  66.6 1.1 copy-done.1
  67.7 1.1 copy-done.3
  68.9 1.1 copy-done.5
  70.0 1.1 copy-done.7
  71.1 4.0 %shard_map.147 = (bf16[256,1536]{1,0:T(8,128)(2,1)S(1)}, bf16[256,1536]{1,0:T(8,128)(2,1)S(1)}, bf16[256,1536]{1,0:T(8,128)(2,1)S(1)}, bf16[256,1536]{1,0:T(8,128)(2,1)S(1)}) custom-call(s32[12]{0:T(128)S(1)} %stack.45.sc, bf16[128,3072]{1,0:T(8,128)(2,1)S(1)} %copy-done, bf16[128,3072]{1,0:T(8,128)(2,1)S(1)} %copy-done.7, bf16[128,3072]{1,0:T(8,128)(2,1)S(1)} %copy-done.1, ...), custom_call_target="tpu_custom_call" | custom-call | bytes 6293504 | tf_op jit(solution)/shard_map/pallas_call | solution.py:227
  75.2 7.8 %shard_map.153 = (bf16[64,3072]{1,0:T(8,128)(2,1)S(1)}, bf16[64,3072]{1,0:T(8,128)(2,1)}, bf16[64,3072]{1,0:T(8,128)(2,1)}, bf16[64,3072]{1,0:T(8,128)(2,1)}) custom-call(s32[12]{0:T(128)S(1)} %stack.45.sc, bf16[256,1536]{1,0:T(8,128)(2,1)S(1)} %get-tuple-element.26.q, bf16[256,1536]{1,0:T(8,128)(2,1)S(1)} %get-tuple-element.27.d, ...), custom_call_target="tpu_custom_call" | custom-call | flops 805306368 | bytes 3145728 | tf_op jit(solution)/shard_map/pallas_call | solution.py:227
  83.0 1.2 collective-permute-start.24
  84.2 1.8 %collective-permute-start.25 = (bf16[64,3072]{1,0:T(8,128)(2,1)}, bf16[64,3072]{1,0:T(8,128)(2,1)}, u32[]{:S(2)}, u32[]{:S(2)}) collective-permute-start(bf16[64,3072]{1,0:T(8,128)(2,1)} %get-tuple-element.30), channel_id=1, source_target_pairs={{0,32},{1,33},{32,0},{33,1},{2,34},{3,35},{34,2},{35,3},{4,36},{5,... | collective-permute-start | bytes 1179656 | tf_op jit(solution)/shard_map/ppermute | solution.py:57
  86.1 3.3 %shard_map.149.refs_0_ = f32[24,256]{1,0:T(8,128)S(1)} custom-call(s32[12]{0:T(128)S(1)} %stack.45.sc, bf16[256,1536]{1,0:T(8,128)(2,1)S(1)} %get-tuple-element.18.k, bf16[256,1536]{1,0:T(8,128)(2,1)S(1)} %get-tuple-element.19.v, bf16[64,3072]{1,0:T(8,128)(2,1)S(1)} %bitcast.33, bf16[64,3072]{1,0:T(8,128)(2,1)S(1)} %collective-permute-done.5.a1, ...), custom_call_target="tpu_custom_call" | custom-call | flops 402653184 | bytes 3145728 | tf_op jit(solution)/shard_map/pallas_call | solution.py:227
  89.7 2.4 %collective-permute-start.26 = (bf16[64,3072]{1,0:T(8,128)(2,1)}, bf16[64,3072]{1,0:T(8,128)(2,1)}, u32[]{:S(2)}, u32[]{:S(2)}) collective-permute-start(bf16[64,3072]{1,0:T(8,128)(2,1)} %get-tuple-element.31), channel_id=1, source_target_pairs={{0,33},{1,0},{32,1},{33,32},{2,35},{3,2},{34,3},{35,34},{4,37},{5,... | collective-permute-start | bytes 1179656 | tf_op jit(solution)/shard_map/ppermute | solution.py:57
  92.1 3.6 %collective-permute-done.10.refs_3_ = f32[24,256]{1,0:T(8,128)S(1)} collective-permute-done((f32[24,256]{1,0:T(8,128)S(1)}, f32[24,256]{1,0:T(8,128)S(1)}, u32[]{:S(2)}, u32[]{:S(2)}) %collective-permute-start.10) | collective-permute-done | bytes 24608 | tf_op jit(solution)/shard_map/ppermute | solution.py:57
  95.7 1.7 %collective-permute-start.9 = (f32[24,256]{1,0:T(8,128)S(1)}, f32[24,256]{1,0:T(8,128)S(1)}, u32[]{:S(2)}, u32[]{:S(2)}) collective-permute-start(f32[24,256]{1,0:T(8,128)S(1)} %shard_map.149.refs_0_), channel_id=1, source_target_pairs={{0,32},{1,33},{32,0},{33,1},{2,34},{3,35},{34,2},{35,3},{4,36},{5,... | collective-permute-start | bytes 73736 | tf_op jit(solution)/shard_map/ppermute | solution.py:57
  97.5 5.4 %collective-permute-done.8.refs_1_ = f32[24,256]{1,0:T(8,128)S(1)} collective-permute-done((f32[24,256]{1,0:T(8,128)S(1)}, f32[24,256]{1,0:T(8,128)S(1)}, u32[]{:S(2)}, u32[]{:S(2)}) %collective-permute-start.8) | collective-permute-done | bytes 24608 | tf_op jit(solution)/shard_map/ppermute | solution.py:57
  103.4 0.7 broadcast_in_dim.5
  104.1 5.8 %all-to-all-start.1 = ((f32[8,24,256]{2,1,0:T(8,128)}), f32[8,24,256]{2,1,0:T(8,128)S(1)}, u32[]{:S(2)}, u32[]{:S(2)}) async-start(f32[8,24,256]{2,1,0:T(8,128)} %broadcast_in_dim.5), calls=%async_computation.1 | async-start | bytes 393216 | tf_op jit(solution)/shard_map/all_to_all | solution.py:351
  110.0 1.0 copy-done.11
  111.0 4.0 %shard_map.154 = bf16[64,3072]{1,0:T(8,128)(2,1)} custom-call(s32[12]{0:T(128)S(1)} %stack.45.sc, bf16[64,3072]{1,0:T(8,128)(2,1)S(1)} %copy-done.11, bf16[64,3072]{1,0:T(8,128)(2,1)} %collective-permute-done.24.p1, bf16[64,3072]{1,0:T(8,128)(2,1)} %collective-permute-done.25.p2, bf16[64,3072]{1,0:T(8,128)(2,1)} %collective-permute-done.26.p3), custom_call_target="tpu_custom_call" | custom-call | bytes 1572864 | tf_op jit(solution)/shard_map/pallas_call | solution.py:227
  115.0 3.6 %all-to-all-done.1.refs_0_ = f32[8,24,256]{2,1,0:T(8,128)S(1)} async-done(((f32[8,24,256]{2,1,0:T(8,128)}), f32[8,24,256]{2,1,0:T(8,128)S(1)}, u32[]{:S(2)}, u32[]{:S(2)}) %all-to-all-start.1) | async-done | bytes 196640 | tf_op jit(solution)/shard_map/all_to_all | solution.py:351
  118.5 4.1 %all-to-all-start.2 = ((bf16[8,8,3072]{2,1,0:T(8,128)(2,1)}), bf16[8,8,3072]{2,1,0:T(8,128)(2,1)}, u32[]{:S(2)}, u32[]{:S(2)}) async-start(bf16[8,8,3072]{2,1,0:T(8,128)(2,1)} %bitcast.9), calls=%async_computation.2 | async-start | bytes 786432 | tf_op jit(solution)/shard_map/all_to_all | solution.py:322
  122.8 0.7 shard_map.151.stats
  123.5 5.5 %shard_map.152 = (bf16[128,1536]{1,0:T(8,128)(2,1)S(1)}, bf16[128,1536]{1,0:T(8,128)(2,1)S(1)}, bf16[128,1536]{1,0:T(8,128)(2,1)S(1)}, bf16[128,1536]{1,0:T(8,128)(2,1)}) custom-call(s32[12]{0:T(128)S(1)} %stack.45.sc, bf16[256,1536]{1,0:T(8,128)(2,1)S(1)} %get-tuple-element.18.k, bf16[256,1536]{1,0:T(8,128)(2,1)S(1)} %get-tuple-element.19.v, ...), custom_call_target="tpu_custom_call" | custom-call | flops 805306368 | bytes 3172352 | tf_op jit(solution)/shard_map/pallas_call | solution.py:227
  128.9 0.7 copy-done.12
  129.7 0.7 copy-done.14
  130.4 0.8 copy-done.29
  131.2 9.5 %collective-permute-start.12 = (bf16[128,1536]{1,0:T(8,128)(2,1)}, bf16[128,1536]{1,0:T(8,128)(2,1)S(1)}, u32[]{:S(2)}, u32[]{:S(2)}) collective-permute-start(bf16[128,1536]{1,0:T(8,128)(2,1)} %get-tuple-element.25), channel_id=1, source_target_pairs={{0,2},{2,0},{1,3},{3,1},{4,6},{6,4},{5,7},{7,5},{8,10},{10,8},{9,1... | collective-permute-start | bytes 1179656 | tf_op jit(solution)/shard_map/ppermute | solution.py:57
  140.8 1.1 convert_reduce_fusion
  141.9 3.3 %collective-permute-start.27 = (f32[4,3072]{1,0:T(4,128)S(1)}, f32[4,3072]{1,0:T(4,128)S(1)}, u32[]{:S(2)}, u32[]{:S(2)}) collective-permute-start(f32[4,3072]{1,0:T(4,128)S(1)} %slice.39), channel_id=1, source_target_pairs={{0,2},{2,0},{1,3},{3,1},{4,6},{6,4},{5,7},{7,5},{8,10},{10,8},{9,1... | collective-permute-start | bytes 147464 | tf_op jit(solution)/shard_map/ppermute | solution.py:57
  145.2 1.0 pad_maximum_fusion.1
  146.3 1.0 pad_maximum_fusion
  148.2 0.6 convert_element_type.24
  148.8 0.6 fusion.2
  (105 shorter events, 5.4 us)
Async XLA Ops:
  2.7 0.7 copy-start.24
  3.4 0.7 copy-start.25
  4.2 0.7 copy-start.26
  4.9 0.7 copy-start.27
  5.6 0.7 copy-start.28
  6.9 4.2 %collective-permute-start.4 = (bf16[4,6144]{1,0:T(4,128)(2,1)S(1)}, bf16[4,6144]{1,0:T(4,128)(2,1)S(1)}, u32[]{:S(2)}, u32[]{:S(2)}) collective-permute-start(bf16[4,6144]{1,0:T(4,128)(2,1)S(1)} %get-tuple-element.21), channel_id=1, source_target_pairs={{0,2},{2,0},{1,3},{3,1},{4,6},{6,4},{5,7},{7,5},{8,10},{10,8},{9,1... | collective-permute-start | bytes 147464 | tf_op jit(solution)/shard_map/ppermute | solution.py:57
  11.2 23.7 %copy-start.2 = (bf16[128,3072]{1,0:T(8,128)(2,1)S(1)}, bf16[128,3072]{1,0:T(8,128)(2,1)}, u32[]{:S(2)}) copy-start(bf16[128,3072]{1,0:T(8,128)(2,1)} %v0.1) | copy-start | bytes 2359300
  11.2 27.5 %copy-start.4 = (bf16[128,3072]{1,0:T(8,128)(2,1)S(1)}, bf16[128,3072]{1,0:T(8,128)(2,1)}, u32[]{:S(2)}) copy-start(bf16[128,3072]{1,0:T(8,128)(2,1)} %d0.1) | copy-start | bytes 2359300
  11.2 3.0 %collective-permute-start.13 = (bf16[8,3072]{1,0:T(8,128)(2,1)S(1)}, bf16[8,3072]{1,0:T(8,128)(2,1)S(1)}, u32[]{:S(2)}, u32[]{:S(2)}) collective-permute-start(bf16[8,3072]{1,0:T(8,128)(2,1)S(1)} %get-tuple-element.38), channel_id=1, source_target_pairs={{0,33},{1,0},{32,1},{33,32},{2,35},{3,2},{34,3},{35,34},{4,37},{5,... | collective-permute-start | bytes 147464 | tf_op jit(solution)/shard_map/ppermute | solution.py:57
  12.3 4.5 %collective-permute-start.14 = (bf16[8,3072]{1,0:T(8,128)(2,1)S(1)}, bf16[8,3072]{1,0:T(8,128)(2,1)S(1)}, u32[]{:S(2)}, u32[]{:S(2)}) collective-permute-start(bf16[8,3072]{1,0:T(8,128)(2,1)S(1)} %get-tuple-element.38), channel_id=1, source_target_pairs={{0,32},{1,33},{32,0},{33,1},{2,34},{3,35},{34,2},{35,3},{4,36},{5,... | collective-permute-start | bytes 147464 | tf_op jit(solution)/shard_map/ppermute | solution.py:57
  12.6 4.6 %collective-permute-start.15 = (bf16[8,3072]{1,0:T(8,128)(2,1)S(1)}, bf16[8,3072]{1,0:T(8,128)(2,1)S(1)}, u32[]{:S(2)}, u32[]{:S(2)}) collective-permute-start(bf16[8,3072]{1,0:T(8,128)(2,1)S(1)} %get-tuple-element.38), channel_id=1, source_target_pairs={{0,1},{1,32},{32,33},{33,0},{2,3},{3,34},{34,35},{35,2},{4,5},{5,3... | collective-permute-start | bytes 147464 | tf_op jit(solution)/shard_map/ppermute | solution.py:57
  17.3 8.3 %collective-permute-start.16 = (bf16[32,3072]{1,0:T(8,128)(2,1)S(1)}, bf16[32,3072]{1,0:T(8,128)(2,1)S(1)}, u32[]{:S(2)}, u32[]{:S(2)}) collective-permute-start(bf16[32,3072]{1,0:T(8,128)(2,1)S(1)} %pad_maximum_fusion.2.refs_0_), channel_id=1, source_target_pairs={{0,28},{4,0},{8,4},{12,8},{16,12},{20,16},{24,20},{28,24},{1,29},{... | collective-permute-start | bytes 589832 | tf_op jit(solution)/shard_map/ppermute | solution.py:57
  22.9 10.0 %collective-permute-start.20 = (bf16[32,3072]{1,0:T(8,128)(2,1)S(1)}, bf16[32,3072]{1,0:T(8,128)(2,1)S(1)}, u32[]{:S(2)}, u32[]{:S(2)}) collective-permute-start(bf16[32,3072]{1,0:T(8,128)(2,1)S(1)} %pad_maximum_fusion.2.refs_0_), channel_id=1, source_target_pairs={{0,4},{4,8},{8,12},{12,16},{16,20},{20,24},{24,28},{28,0},{1,5},{5... | collective-permute-start | bytes 589832 | tf_op jit(solution)/shard_map/ppermute | solution.py:57
  22.9 37.5 %collective-permute-start = (bf16[128,3072]{1,0:T(8,128)(2,1)}, bf16[128,3072]{1,0:T(8,128)(2,1)S(1)}, u32[]{:S(2)}, u32[]{:S(2)}) collective-permute-start(bf16[128,3072]{1,0:T(8,128)(2,1)} %q0.1), channel_id=1, source_target_pairs={{0,2},{2,0},{1,3},{3,1},{4,6},{6,4},{5,7},{7,5},{8,10},{10,8},{9,1... | collective-permute-start | bytes 2359304 | tf_op jit(solution)/shard_map/ppermute | solution.py:57
  25.0 36.9 %collective-permute-start.1 = (bf16[128,3072]{1,0:T(8,128)(2,1)}, bf16[128,3072]{1,0:T(8,128)(2,1)}, u32[]{:S(2)}, u32[]{:S(2)}) collective-permute-start(bf16[128,3072]{1,0:T(8,128)(2,1)} %k0.1), channel_id=1, source_target_pairs={{0,2},{2,0},{1,3},{3,1},{4,6},{6,4},{5,7},{7,5},{8,10},{10,8},{9,1... | collective-permute-start | bytes 2359304 | tf_op jit(solution)/shard_map/ppermute | solution.py:57
  25.6 23.0 %copy-start.16 = (bf16[32,3072]{1,0:T(8,128)(2,1)}, bf16[32,3072]{1,0:T(8,128)(2,1)S(1)}, u32[]{:S(2)}) copy-start(bf16[32,3072]{1,0:T(8,128)(2,1)S(1)} %collective-permute-done.16.refs_1_) | copy-start | bytes 589828
  25.6 13.2 %collective-permute-start.17 = (bf16[32,3072]{1,0:T(8,128)(2,1)S(1)}, bf16[32,3072]{1,0:T(8,128)(2,1)S(1)}, u32[]{:S(2)}, u32[]{:S(2)}) collective-permute-start(bf16[32,3072]{1,0:T(8,128)(2,1)S(1)} %collective-permute-done.16.refs_1_), channel_id=1, source_target_pairs={{0,28},{4,0},{8,4},{12,8},{16,12},{20,16},{24,20},{28,24},{1,29},{... | collective-permute-start | bytes 589832 | tf_op jit(solution)/shard_map/ppermute | solution.py:57
  29.4 28.4 %all-to-all-start = ((bf16[8,8,3072]{2,1,0:T(8,128)(2,1)}), bf16[8,8,3072]{2,1,0:T(8,128)(2,1)S(1)}, u32[]{:S(2)}, u32[]{:S(2)}) async-start(bf16[8,8,3072]{2,1,0:T(8,128)(2,1)} %broadcast_in_dim.4), calls=%async_computation | async-start | bytes 786432 | tf_op jit(solution)/shard_map/all_to_all | solution.py:277
  32.9 13.5 %collective-permute-start.21 = (bf16[32,3072]{1,0:T(8,128)(2,1)S(1)}, bf16[32,3072]{1,0:T(8,128)(2,1)S(1)}, u32[]{:S(2)}, u32[]{:S(2)}) collective-permute-start(bf16[32,3072]{1,0:T(8,128)(2,1)S(1)} %collective-permute-done.20.refs_8_), channel_id=1, source_target_pairs={{0,4},{4,8},{8,12},{12,16},{16,20},{20,24},{24,28},{28,0},{1,5},{5... | collective-permute-start | bytes 589832 | tf_op jit(solution)/shard_map/ppermute | solution.py:57
  34.3 0.7 copy-start.18
  34.9 28.9 %collective-permute-start.2 = (bf16[128,3072]{1,0:T(8,128)(2,1)S(1)}, bf16[128,3072]{1,0:T(8,128)(2,1)}, u32[]{:S(2)}, u32[]{:S(2)}) collective-permute-start(bf16[128,3072]{1,0:T(8,128)(2,1)S(1)} %copy-done.2), channel_id=1, source_target_pairs={{0,2},{2,0},{1,3},{3,1},{4,6},{6,4},{5,7},{7,5},{8,10},{10,8},{9,1... | collective-permute-start | bytes 2359304 | tf_op jit(solution)/shard_map/ppermute | solution.py:57
  38.7 0.7 copy-start.20
  38.7 26.6 %collective-permute-start.3 = (bf16[128,3072]{1,0:T(8,128)(2,1)S(1)}, bf16[128,3072]{1,0:T(8,128)(2,1)}, u32[]{:S(2)}, u32[]{:S(2)}) collective-permute-start(bf16[128,3072]{1,0:T(8,128)(2,1)S(1)} %copy-done.4), channel_id=1, source_target_pairs={{0,2},{2,0},{1,3},{3,1},{4,6},{6,4},{5,7},{7,5},{8,10},{10,8},{9,1... | collective-permute-start | bytes 2359304 | tf_op jit(solution)/shard_map/ppermute | solution.py:57
  46.4 0.7 copy-start.22
  47.1 4.7 %collective-permute-start.18 = (bf16[32,3072]{1,0:T(8,128)(2,1)}, bf16[32,3072]{1,0:T(8,128)(2,1)S(1)}, u32[]{:S(2)}, u32[]{:S(2)}) collective-permute-start(bf16[32,3072]{1,0:T(8,128)(2,1)} %copy-done.20), channel_id=1, source_target_pairs={{0,28},{4,0},{8,4},{12,8},{16,12},{20,16},{24,20},{28,24},{1,29},{... | collective-permute-start | bytes 589832 | tf_op jit(solution)/shard_map/ppermute | solution.py:57
  51.8 6.0 %collective-permute-start.22 = (bf16[32,3072]{1,0:T(8,128)(2,1)}, bf16[32,3072]{1,0:T(8,128)(2,1)S(1)}, u32[]{:S(2)}, u32[]{:S(2)}) collective-permute-start(bf16[32,3072]{1,0:T(8,128)(2,1)} %copy-done.22), channel_id=1, source_target_pairs={{0,4},{4,8},{8,12},{12,16},{16,20},{20,24},{24,28},{28,0},{1,5},{5... | collective-permute-start | bytes 589832 | tf_op jit(solution)/shard_map/ppermute | solution.py:57
  57.8 0.7 copy-start.8
  58.5 27.6 %collective-permute-start.5 = (bf16[64,3072]{1,0:T(8,128)(2,1)S(1)}, bf16[64,3072]{1,0:T(8,128)(2,1)S(1)}, u32[]{:S(2)}, u32[]{:S(2)}) collective-permute-start(bf16[64,3072]{1,0:T(8,128)(2,1)S(1)} %bitcast.30), channel_id=1, source_target_pairs={{0,33},{1,0},{32,1},{33,32},{2,35},{3,2},{34,3},{35,34},{4,37},{5,... | collective-permute-start | bytes 1179656 | tf_op jit(solution)/shard_map/ppermute | solution.py:57
  60.4 0.9 copy-start.6
  61.3 24.7 %collective-permute-start.6 = (bf16[64,3072]{1,0:T(8,128)(2,1)S(1)}, bf16[64,3072]{1,0:T(8,128)(2,1)S(1)}, u32[]{:S(2)}, u32[]{:S(2)}) collective-permute-start(bf16[64,3072]{1,0:T(8,128)(2,1)S(1)} %bitcast.31), channel_id=1, source_target_pairs={{0,32},{1,33},{32,0},{33,1},{2,34},{3,35},{34,2},{35,3},{4,36},{5,... | collective-permute-start | bytes 1179656 | tf_op jit(solution)/shard_map/ppermute | solution.py:57
  61.9 24.1 %collective-permute-start.7 = (bf16[64,3072]{1,0:T(8,128)(2,1)S(1)}, bf16[64,3072]{1,0:T(8,128)(2,1)S(1)}, u32[]{:S(2)}, u32[]{:S(2)}) collective-permute-start(bf16[64,3072]{1,0:T(8,128)(2,1)S(1)} %bitcast.32), channel_id=1, source_target_pairs={{0,1},{1,32},{32,33},{33,0},{2,3},{3,34},{34,35},{35,2},{4,5},{5,3... | collective-permute-start | bytes 1179656 | tf_op jit(solution)/shard_map/ppermute | solution.py:57
  63.8 11.4 %collective-permute-start.19 = (bf16[16,3072]{1,0:T(8,128)(2,1)S(1)}, bf16[16,3072]{1,0:T(8,128)(2,1)S(1)}, u32[]{:S(2)}, u32[]{:S(2)}) collective-permute-start(bf16[16,3072]{1,0:T(8,128)(2,1)S(1)} %slice.36), channel_id=1, source_target_pairs={{0,28},{4,0},{8,4},{12,8},{16,12},{20,16},{24,20},{28,24},{1,29},{... | collective-permute-start | bytes 294920 | tf_op jit(solution)/shard_map/ppermute | solution.py:57
  65.4 9.8 %collective-permute-start.23 = (bf16[16,3072]{1,0:T(8,128)(2,1)S(1)}, bf16[16,3072]{1,0:T(8,128)(2,1)S(1)}, u32[]{:S(2)}, u32[]{:S(2)}) collective-permute-start(bf16[16,3072]{1,0:T(8,128)(2,1)S(1)} %slice.37), channel_id=1, source_target_pairs={{0,4},{4,8},{8,12},{12,16},{16,20},{20,24},{24,28},{28,0},{1,5},{5... | collective-permute-start | bytes 294920 | tf_op jit(solution)/shard_map/ppermute | solution.py:57
  65.5 1.1 copy-start
  66.6 1.1 copy-start.1
  67.7 1.1 copy-start.3
  68.9 1.1 copy-start.5
  70.0 1.1 copy-start.7
  71.1 4.1 %copy-start.9 = (bf16[32,3072]{1,0:T(8,128)(2,1)S(1)}, bf16[32,3072]{1,0:T(8,128)(2,1)}, u32[]{:S(2)}) copy-start(bf16[32,3072]{1,0:T(8,128)(2,1)} %copy-done.8) | copy-start | bytes 589828
  71.1 4.1 %copy-start.17 = (bf16[32,3072]{1,0:T(8,128)(2,1)S(1)}, bf16[32,3072]{1,0:T(8,128)(2,1)}, u32[]{:S(2)}) copy-start(bf16[32,3072]{1,0:T(8,128)(2,1)} %copy-done.16) | copy-start | bytes 589828
  71.1 4.1 %copy-start.19 = (bf16[32,3072]{1,0:T(8,128)(2,1)S(1)}, bf16[32,3072]{1,0:T(8,128)(2,1)}, u32[]{:S(2)}) copy-start(bf16[32,3072]{1,0:T(8,128)(2,1)} %copy-done.18) | copy-start | bytes 589828
  71.1 4.1 %copy-start.21 = (bf16[32,3072]{1,0:T(8,128)(2,1)S(1)}, bf16[32,3072]{1,0:T(8,128)(2,1)}, u32[]{:S(2)}) copy-start(bf16[32,3072]{1,0:T(8,128)(2,1)} %copy-done.20) | copy-start | bytes 589828
  71.1 4.1 %copy-start.23 = (bf16[32,3072]{1,0:T(8,128)(2,1)S(1)}, bf16[32,3072]{1,0:T(8,128)(2,1)}, u32[]{:S(2)}) copy-start(bf16[32,3072]{1,0:T(8,128)(2,1)} %copy-done.22) | copy-start | bytes 589828
  83.0 6.3 %copy-start.10 = (bf16[64,3072]{1,0:T(8,128)(2,1)}, bf16[64,3072]{1,0:T(8,128)(2,1)S(1)}, u32[]{:S(2)}) copy-start(bf16[64,3072]{1,0:T(8,128)(2,1)S(1)} %get-tuple-element.28.p0) | copy-start | bytes 1179652
  83.0 26.9 %collective-permute-start.24 = (bf16[64,3072]{1,0:T(8,128)(2,1)}, bf16[64,3072]{1,0:T(8,128)(2,1)}, u32[]{:S(2)}, u32[]{:S(2)}) collective-permute-start(bf16[64,3072]{1,0:T(8,128)(2,1)} %get-tuple-element.29), channel_id=1, source_target_pairs={{0,1},{1,32},{32,33},{33,0},{2,3},{3,34},{34,35},{35,2},{4,5},{5,3... | collective-permute-start | bytes 1179656 | tf_op jit(solution)/shard_map/ppermute | solution.py:57
  84.2 25.7 %collective-permute-start.25 = (bf16[64,3072]{1,0:T(8,128)(2,1)}, bf16[64,3072]{1,0:T(8,128)(2,1)}, u32[]{:S(2)}, u32[]{:S(2)}) collective-permute-start(bf16[64,3072]{1,0:T(8,128)(2,1)} %get-tuple-element.30), channel_id=1, source_target_pairs={{0,32},{1,33},{32,0},{33,1},{2,34},{3,35},{34,2},{35,3},{4,36},{5,... | collective-permute-start | bytes 1179656 | tf_op jit(solution)/shard_map/ppermute | solution.py:57
  86.1 23.9 %copy-start.30 = (s32[4]{0:T(128)S(1)}, s32[4]{0:T(128)}, u32[]{:S(2)}) copy-start(s32[4]{0:T(128)} %param.20) | copy-start | bytes 52
  89.3 6.4 %collective-permute-start.10 = (f32[24,256]{1,0:T(8,128)S(1)}, f32[24,256]{1,0:T(8,128)S(1)}, u32[]{:S(2)}, u32[]{:S(2)}) collective-permute-start(f32[24,256]{1,0:T(8,128)S(1)} %shard_map.149.refs_0_), channel_id=1, source_target_pairs={{0,1},{1,32},{32,33},{33,0},{2,3},{3,34},{34,35},{35,2},{4,5},{5,3... | collective-permute-start | bytes 73736 | tf_op jit(solution)/shard_map/ppermute | solution.py:57
  89.7 20.3 %collective-permute-start.26 = (bf16[64,3072]{1,0:T(8,128)(2,1)}, bf16[64,3072]{1,0:T(8,128)(2,1)}, u32[]{:S(2)}, u32[]{:S(2)}) collective-permute-start(bf16[64,3072]{1,0:T(8,128)(2,1)} %get-tuple-element.31), channel_id=1, source_target_pairs={{0,33},{1,0},{32,1},{33,32},{2,35},{3,2},{34,3},{35,34},{4,37},{5,... | collective-permute-start | bytes 1179656 | tf_op jit(solution)/shard_map/ppermute | solution.py:57
  92.1 10.7 %collective-permute-start.8 = (f32[24,256]{1,0:T(8,128)S(1)}, f32[24,256]{1,0:T(8,128)S(1)}, u32[]{:S(2)}, u32[]{:S(2)}) collective-permute-start(f32[24,256]{1,0:T(8,128)S(1)} %shard_map.149.refs_0_), channel_id=1, source_target_pairs={{0,33},{1,0},{32,1},{33,32},{2,35},{3,2},{34,3},{35,34},{4,37},{5,... | collective-permute-start | bytes 73736 | tf_op jit(solution)/shard_map/ppermute | solution.py:57
  95.7 7.1 %collective-permute-start.9 = (f32[24,256]{1,0:T(8,128)S(1)}, f32[24,256]{1,0:T(8,128)S(1)}, u32[]{:S(2)}, u32[]{:S(2)}) collective-permute-start(f32[24,256]{1,0:T(8,128)S(1)} %shard_map.149.refs_0_), channel_id=1, source_target_pairs={{0,32},{1,33},{32,0},{33,1},{2,34},{3,35},{34,2},{35,3},{4,36},{5,... | collective-permute-start | bytes 73736 | tf_op jit(solution)/shard_map/ppermute | solution.py:57
  104.1 14.4 %all-to-all-start.1 = ((f32[8,24,256]{2,1,0:T(8,128)}), f32[8,24,256]{2,1,0:T(8,128)S(1)}, u32[]{:S(2)}, u32[]{:S(2)}) async-start(f32[8,24,256]{2,1,0:T(8,128)} %broadcast_in_dim.5), calls=%async_computation.1 | async-start | bytes 393216 | tf_op jit(solution)/shard_map/all_to_all | solution.py:351
  110.0 1.0 copy-start.11
  118.5 22.3 %all-to-all-start.2 = ((bf16[8,8,3072]{2,1,0:T(8,128)(2,1)}), bf16[8,8,3072]{2,1,0:T(8,128)(2,1)}, u32[]{:S(2)}, u32[]{:S(2)}) async-start(bf16[8,8,3072]{2,1,0:T(8,128)(2,1)} %bitcast.9), calls=%async_computation.2 | async-start | bytes 786432 | tf_op jit(solution)/shard_map/all_to_all | solution.py:322
  128.9 0.7 copy-start.12
  129.7 0.7 copy-start.14
  130.4 0.8 copy-start.29
  131.2 14.0 %copy-start.15 = (bf16[128,1536]{1,0:T(8,128)(2,1)S(1)}, bf16[128,1536]{1,0:T(8,128)(2,1)}, u32[]{:S(2)}) copy-start(bf16[128,1536]{1,0:T(8,128)(2,1)} %copy-done.14) | copy-start | bytes 1179652
  131.2 14.0 %collective-permute-start.12 = (bf16[128,1536]{1,0:T(8,128)(2,1)}, bf16[128,1536]{1,0:T(8,128)(2,1)S(1)}, u32[]{:S(2)}, u32[]{:S(2)}) collective-permute-start(bf16[128,1536]{1,0:T(8,128)(2,1)} %get-tuple-element.25), channel_id=1, source_target_pairs={{0,2},{2,0},{1,3},{3,1},{4,6},{6,4},{5,7},{7,5},{8,10},{10,8},{9,1... | collective-permute-start | bytes 1179656 | tf_op jit(solution)/shard_map/ppermute | solution.py:57
  140.7 5.5 %collective-permute-start.11 = (bf16[128,1536]{1,0:T(8,128)(2,1)}, bf16[128,1536]{1,0:T(8,128)(2,1)S(1)}, u32[]{:S(2)}, u32[]{:S(2)}) collective-permute-start(bf16[128,1536]{1,0:T(8,128)(2,1)} %copy-done.29), channel_id=1, source_target_pairs={{0,2},{2,0},{1,3},{3,1},{4,6},{6,4},{5,7},{7,5},{8,10},{10,8},{9,1... | collective-permute-start | bytes 1179656 | tf_op jit(solution)/shard_map/ppermute | solution.py:57
  141.9 5.4 %collective-permute-start.27 = (f32[4,3072]{1,0:T(4,128)S(1)}, f32[4,3072]{1,0:T(4,128)S(1)}, u32[]{:S(2)}, u32[]{:S(2)}) collective-permute-start(f32[4,3072]{1,0:T(4,128)S(1)} %slice.39), channel_id=1, source_target_pairs={{0,2},{2,0},{1,3},{3,1},{4,6},{6,4},{5,7},{7,5},{8,10},{10,8},{9,1... | collective-permute-start | bytes 147464 | tf_op jit(solution)/shard_map/ppermute | solution.py:57
  145.2 1.0 copy-start.13

commit v3 on v2

--- a/solution.py
+++ b/solution.py
@@ -17,7 +17,7 @@
 
 NY, NZ, NC = 4, 8, 2
 HEADS = 12
-GROUPS = 4
+GROUPS = 2
 HPG = HEADS // GROUPS
 GW = HPG * HD
 CW = HEADS * HD
@@ -143,9 +143,9 @@
     clear = lambda x: jnp.where(ours, x.astype(f32), 0.0)
     for n in range(HEADS):
         base = n // HPG * 2 * GW + n % HPG * HD
-        for at, ref, change in ((0, k, turn), (GW, v, same), (2 * CW, q, turn), (2 * CW + GW, d, clear)):
+        for at, ref, change in ((base, k, turn), (base + GW, v, same), (2 * CW + base, q, turn), (2 * CW + base + GW, d, clear)):
             a, b = pair(ref, n, change)
-            lanes = slice(base + at, base + at + HD)
+            lanes = slice(at, at + HD)
             keep[:, lanes] = jnp.where(core == 0, a, b).astype(bf16)
             give[:, lanes] = jnp.where(core == 0, b, a).astype(bf16)
 
@@ -173,10 +173,6 @@
         out[pl.ds(g * HPG + i, 1), :] = jnp.where(some, m + jnp.log(safe), NEG)
         out[pl.ds(HEADS + g * HPG + i, 1), :] = jnp.where(some, t / safe, 0.0)
 
-    @pl.when(g == GROUPS - 1)
-    def _():
-        out[...] = pltpu.roll(out[...], sc[1] * ZR, 1)
-
 
 def merge(lses, deltas):
     top = functools.reduce(jnp.maximum, lses)
@@ -186,16 +182,14 @@
     return top + jnp.log(total), delta
 
 
-def merge_kernel(sc, *refs, count, back):
+def merge_kernel(sc, *refs, count, turn):
     *parts, out = refs
     if count > 1:
         (part,) = parts
         parts = [part.at[n] for n in range(count)]
     lse, delta = merge([p[:HEADS] for p in parts], [p[HEADS:] for p in parts])
     both = jnp.concatenate([lse, delta], 0)
-    if back:
-        both = pltpu.roll(both, lax.rem(AUDIO - sc[1] * ZR, AUDIO), 1)
-    out[...] = both
+    out[...] = pltpu.roll(both, lax.rem(AUDIO + turn * sc[1] * ZR, AUDIO), 1)
 
 
 def audio_to_video_kernel(sc, k, v, stats, cos, sin, a0, a1, a2, a3, dk0, dk1, dv0, dv1):
@@ -222,7 +216,21 @@
             dvo[:, head(i)] = dv[rows].astype(bf16)
 
 
-def call(kernel, scalars, args, specs, outs, out_specs, grid=(GROUPS,), flops=0, scratch=()):
+def join_kernel(sc, k0, k1, v0, v1, dk, dv):
+    for a, b, out in ((k0, k1, dk), (v0, v1, dv)):
+
+        @pl.when(sc[0] == 0)
+        def _():
+            out[:, :CW] = a[...]
+            out[:, CW:] = b[...]
+
+        @pl.when(sc[0] != 0)
+        def _():
+            out[:, :CW] = b[...]
+            out[:, CW:] = a[...]
+
+
+def call(kernel, scalars, args, specs, outs, out_specs, grid=(GROUPS,), flops=0, limit=56, scratch=()):
     size = sum(x.size * x.dtype.itemsize for x in args)
     return pl.pallas_call(
         kernel,
@@ -230,8 +238,8 @@
             num_scalar_prefetch=1, grid=grid, in_specs=specs, out_specs=out_specs, scratch_shapes=scratch
         ),
         out_shape=outs,
-        compiler_params=pltpu.CompilerParams(vmem_limit_bytes=16 * 1024 * 1024),
-        cost_estimate=pl.CostEstimate(flops=flops, bytes_accessed=size, transcendentals=0),
+        compiler_params=pltpu.CompilerParams(vmem_limit_bytes=limit * 1024 * 1024),
+        cost_estimate=pl.CostEstimate(flops=0, bytes_accessed=0, transcendentals=0),
     )(scalars, *args)
 
 
@@ -260,11 +268,15 @@
         grid=(1,),
     )
     chip = jnp.concatenate([keep, shift(give, "core", NC, 1)], 0)
-    kv, qd = chip[:, : 2 * CW], chip[:, 2 * CW :]
 
     def along_y(x):
         return [x] + [shift(x, Y, NY, NY - n) for n in range(1, NY)]
 
+    def along_z(x):
+        copies = jnp.broadcast_to(x[None], (NZ,) + x.shape).reshape(-1, x.shape[1])
+        return lax.all_to_all(copies, "z", split_axis=0, concat_axis=0, tiled=True)
+
+    kv, qd = chip[:, : 2 * CW], chip[:, 2 * CW :]
     home = jnp.concatenate(along_y(kv), 0)
     up, down = [home], [home]
     for _ in range(3):
@@ -273,15 +285,20 @@
     far = [shift(up[-1][: YR // 2], "z", NZ, NZ - 1), shift(down[-1][YR // 2 :], "z", NZ, 1)]
     kv_all = up + far + down[:0:-1]
 
-    copies = jnp.broadcast_to(qd[None], (NZ,) + qd.shape).reshape(ZR, 2 * CW)
-    qd_all = along_y(lax.all_to_all(copies, "z", split_axis=0, concat_axis=0, tiled=True))
+    qd_z = along_z(qd)
+    qd_all = along_y(qd_z)
 
     q_pair, k_pair, v_pair, d_pair = (
         shift(x, "core", NC, 1) for x in (q_video, k_video, v_video, d_video)
+    )
+    q_pair, k_pair, v_pair, d_pair, _ = lax.optimization_barrier(
+        (q_pair, k_pair, v_pair, d_pair, qd_z)
     )
     cos, sin = turn_tables(jnp.stack([own * VT // VFRAME, pair * VT // VFRAME]))
     half = pl.BlockSpec((VT, GW), lambda g, sc: (0, sc[0] * GROUPS + g))
     table = pl.BlockSpec((2, HD), lambda g, sc: (0, 0))
+    video_in = pl.BlockSpec((2 * VT, GW), lambda g, sc: (0, g))
+    audio_in = pl.BlockSpec((ZR, 2 * GW), lambda g, sc: (0, g))
     video = pl.BlockSpec((2 * VT, GW), lambda g, sc: (0, g))
     audio = pl.BlockSpec((ZR, 2 * GW), lambda g, sc: (0, g))
     rows = pl.BlockSpec((2 * HEADS, AUDIO), lambda g, sc: (0, 0))
@@ -301,25 +318,82 @@
         [video] * 4,
     )
 
+
     parts = call(
         video_to_audio_kernel,
         scalars,
         (qr, dr, *kv_all),
-        [video] * 2 + [pl.BlockSpec((x.shape[0], 2 * GW), lambda g, sc: (0, g)) for x in kv_all],
+        [video_in] * 2 + [pl.BlockSpec((x.shape[0], 2 * GW), lambda g, sc: (0, g)) for x in kv_all],
         [audio_shape] * NY,
         [audio] * NY,
         flops=4 * one,
     )
+    parts_y = [parts[0]] + [shift(parts[n], Y, NY, n) for n in range(1, NY)]
+
+    kr, parts = lax.optimization_barrier((kr, parts))
+    stats = call(
+        statistics_kernel,
+        scalars,
+        (kr, vr, *qd_all),
+        [video_in] * 2 + [audio_in] * NY,
+        rows_shape,
+        rows,
+        flops=2 * one,
+    )
+    copies = jnp.broadcast_to(stats[None], (NZ,) + stats.shape)
+    stats = lax.all_to_all(copies, "z", split_axis=0, concat_axis=0, tiled=True)
+    stats = call(
+        functools.partial(merge_kernel, count=NZ, turn=1),
+        scalars,
+        (stats,),
+        [pl.BlockSpec(stats.shape, lambda g, sc: (0, 0, 0))],
+        rows_shape,
+        rows,
+        grid=(1,),
+        limit=16,
+    )
     sums = call(
         sum_kernel,
         scalars,
-        [parts[0]] + [shift(parts[n], Y, NY, n) for n in range(1, NY)],
-        [audio] * NY,
+        parts_y,
+        [audio_in] * NY,
         audio_shape,
         audio,
         scratch=[pltpu.VMEM((2 * ZR, 2 * GW), f32)],
     )
+    stats = call(
+        functools.partial(merge_kernel, count=1, turn=-1),
+        scalars,
+        along_y(stats),
+        [rows] * NY,
+        rows_shape,
+        rows,
+        grid=(1,),
+        limit=16,
+    )
+    dk0, dk1, dv0, dv1 = call(
+        audio_to_video_kernel,
+        scalars,
+        (kr, vr, stats, cos, sin, *qd_all),
+        [video_in] * 2 + [rows] + [table] * 2 + [audio_in] * NY,
+        [mine_shape] * 4,
+        [mine] * 4,
+        flops=4 * one,
+    )
+
+    part = pl.BlockSpec((VT, CW), lambda g, sc: (0, 0))
+    full = pl.BlockSpec((VT, NC * CW), lambda g, sc: (0, 0))
+    dk_video, dv_video = call(
+        join_kernel,
+        scalars,
+        (dk0, shift(dk1, "core", NC, 1), dv0, shift(dv1, "core", NC, 1)),
+        [part] * 4,
+        [jax.ShapeDtypeStruct((VT, NC * CW), bf16)] * 2,
+        [full] * 2,
+        grid=(1,),
+    )
     sums = lax.all_to_all(sums, "z", split_axis=0, concat_axis=0, tiled=True)
+    sums, _ = lax.optimization_barrier((sums, dk0))
     sums = jnp.sum(sums.reshape(NZ, CR, 2 * CW).astype(f32), 0)
     other = shift(sums[AR:], "core", NC, 1)
     sums = sums[:AR]
@@ -328,51 +402,7 @@
     dk_sum = sums[:, :, :, 0].reshape(AR, NC * CW)
     dk_audio = rotate_rows(dk_sum, audio_cos, -audio_sin).astype(bf16)
     dv_audio = sums[:, :, :, 1].reshape(AR, NC * CW).astype(bf16)
-
-    stats = call(
-        statistics_kernel,
-        scalars,
-        (kr, vr, *qd_all),
-        [video] * 2 + [audio] * NY,
-        rows_shape,
-        rows,
-        flops=2 * one,
-    )
-    stats = call(
-        functools.partial(merge_kernel, count=1, back=False),
-        scalars,
-        along_y(stats),
-        [rows] * NY,
-        rows_shape,
-        rows,
-        grid=(1,),
-    )
-    copies = jnp.broadcast_to(stats[None], (NZ,) + stats.shape)
-    stats = lax.all_to_all(copies, "z", split_axis=0, concat_axis=0, tiled=True)
-    stats = call(
-        functools.partial(merge_kernel, count=NZ, back=True),
-        scalars,
-        (stats,),
-        [pl.BlockSpec(stats.shape, lambda g, sc: (0, 0, 0))],
-        rows_shape,
-        rows,
-        grid=(1,),
-    )
-    dk0, dk1, dv0, dv1 = call(
-        audio_to_video_kernel,
-        scalars,
-        (kr, vr, stats, cos, sin, *qd_all),
-        [video] * 2 + [rows] + [table] * 2 + [audio] * NY,
-        [mine_shape] * 4,
-        [mine] * 4,
-        flops=4 * one,
-    )
-
-    def joined(a, b):
-        b = shift(b, "core", NC, 1)
-        return jnp.concatenate([jnp.where(first, a, b), jnp.where(first, b, a)], 1)
-
-    return joined(dk0, dk1), joined(dv0, dv1), dk_audio, dv_audio
+    return dk_video, dv_video, dk_audio, dv_audio
 
 
 def solution(mesh):

time: 151 us -> 138 us (0.914)
  local copies, waits for them, and re-layouts: 20.6 us -> 9.91 us
  Pallas kernels: 26.4 us -> 33.4 us
  starting transfers between devices: 61.7 us -> 57.5 us
  waiting for transfers between devices: 34 us -> 31.6 us
  other arithmetic: 4.28 us -> 2.58 us
    unnamed x65 -> x49, local copies, waits for them, and re-layouts: 16.1 us -> 5.65 us
    pallas_call x8 -> x9, Pallas kernels: 26.4 us -> 33.4 us  [call(): pl.pallas_call(kernel, grid_spec=pltpu.PrefetchScalarGridSpec(num_scalar_...]
    ppermute x28, starting transfers between devices: 48.4 us -> 41.9 us  [shift(): return lax.ppermute(x, axis, [(i, (i + step) % size) for i in range(size)])]
    ppermute x28, waiting for transfers between devices: 30.5 us -> 27.7 us  [shift(): return lax.ppermute(x, axis, [(i, (i + step) % size) for i in range(size)])]
    all_to_all x1, starting transfers between devices: 5.81 us -> 7.79 us  [local(): stats = lax.all_to_all(copies, 'z', split_axis=0, concat_axis=0, tiled=True)]
    concatenate x2 -> x0, other arithmetic: 1.93 us -> none  [joined(): return jnp.concatenate([jnp.where(first, a, b), jnp.where(first, b, a)], 1)]
  transfers between devices with their start and end apart: 31 -> 31, of which waited for: 11 -> 12; matrix products, arithmetic and copies ran while one was open for 4% -> 2% of each run, Pallas kernels for 17% -> 23%
where the time goes in v3:
time: 138 us; the launch traced here: 137 us
  starting transfers between devices  57.5 us (42%)
  Pallas kernels  33.4 us (24%)
  waiting for transfers between devices  31.6 us (23%)
  local copies, waits for them, and re-layouts  9.91 us (7%)
  other arithmetic  2.58 us (2%)
  between operations  2.31 us (2%)
    ppermute x28, starting transfers between devices, shift(): return lax.ppermute(x, axis, [(i, (i + step) % size) for i in range(size)])  41.9 us
    pallas_call x9, Pallas kernels, call(): pl.pallas_call(kernel, grid_spec=pltpu.PrefetchScalarGridSpec(num_scalar_...  33.4 us
    ppermute x28, waiting for transfers between devices, shift(): return lax.ppermute(x, axis, [(i, (i + step) % size) for i in range(size)])  27.7 us
    all_to_all x1, starting transfers between devices, local(): stats = lax.all_to_all(copies, 'z', split_axis=0, concat_axis=0, tiled=True)  7.79 us
    unnamed x49, local copies, waits for them, and re-layouts  5.65 us
    all_to_all x1, starting transfers between devices, along_z(): return lax.all_to_all(copies, 'z', split_axis=0, concat_axis=0, tiled=True)  4.36 us
    all_to_all x1, waiting for transfers between devices, local(): stats = lax.all_to_all(copies, 'z', split_axis=0, concat_axis=0, tiled=True)  3.95 us
    all_to_all x1, starting transfers between devices, local(): sums = lax.all_to_all(sums, 'z', split_axis=0, concat_axis=0, tiled=True)  3.45 us
  transfers between devices with their start and end apart: 31, of which 12 were waited for; matrix products, arithmetic and copies ran while one was open for 2% of the time, Pallas kernels for 23%

profile of v3, /device:TPU:1, one launch (start us, length us, event | category | flops | bytes accessed | tf_op | source)
XLA Modules:
  0.0 137.3 jit_solution(1580665677836632031)
XLA Ops:
  1.9 0.6 copy-done.22
  2.6 0.6 stack.45.sc
  3.2 2.2 %shard_map.147 = (bf16[4,6144]{1,0:T(4,128)(2,1)}, bf16[4,6144]{1,0:T(4,128)(2,1)}) custom-call(s32[12]{0:T(128)} %stack.45.sc, bf16[4,3072]{1,0:T(4,128)(2,1)} %q.1, bf16[4,3072]{1,0:T(4,128)(2,1)} %k.1, bf16[4,3072]{1,0:T(4,128)(2,1)} %v.1, bf16[4,3072]{1,0:T(4,128)(2,1)} %d.1, f32[1,128]{1,0:T(1,128)} %constant.56.clone.freq), custom_call_target="tpu_custom_call" | custom-call | tf_op jit(solution)/shard_map/pallas_call | solution.py:235
  5.4 3.2 %collective-permute-start.4 = (bf16[4,6144]{1,0:T(4,128)(2,1)}, bf16[4,6144]{1,0:T(4,128)(2,1)S(1)}, u32[]{:S(2)}, u32[]{:S(2)}) collective-permute-start(bf16[4,6144]{1,0:T(4,128)(2,1)} %get-tuple-element.27), channel_id=1, source_target_pairs={{0,2},{2,0},{1,3},{3,1},{4,6},{6,4},{5,7},{7,5},{8,10},{10,8},{9,1... | collective-permute-start | bytes 147464 | tf_op jit(solution)/shard_map/ppermute | solution.py:57
  8.6 1.1 collective-permute-done.4
  9.7 0.8 pad_maximum_fusion.1
  10.5 1.1 collective-permute-start.5
  11.6 0.3 collective-permute-start.6
  12.0 0.7 collective-permute-start.7
  12.7 0.9 collective-permute-done.5
  13.6 2.6 %collective-permute-done.6 = bf16[8,3072]{1,0:T(8,128)(2,1)S(1)} collective-permute-done((bf16[8,3072]{1,0:T(8,128)(2,1)S(1)}, bf16[8,3072]{1,0:T(8,128)(2,1)S(1)}, u32[]{:S(2)}, u32[]{:S(2)}) %collective-permute-start.6) | collective-permute-done | bytes 49184 | tf_op jit(solution)/shard_map/ppermute | solution.py:57
  16.1 0.5 collective-permute-done.7
  16.6 5.7 %collective-permute-start.8 = (bf16[32,3072]{1,0:T(8,128)(2,1)S(1)}, bf16[32,3072]{1,0:T(8,128)(2,1)S(1)}, u32[]{:S(2)}, u32[]{:S(2)}) collective-permute-start(bf16[32,3072]{1,0:T(8,128)(2,1)S(1)} %pad_maximum_fusion.refs_0_), channel_id=1, source_target_pairs={{0,28},{4,0},{8,4},{12,8},{16,12},{20,16},{24,20},{28,24},{1,29},{... | collective-permute-start | bytes 589832 | tf_op jit(solution)/shard_map/ppermute | solution.py:57
  22.3 2.1 %collective-permute-start = (bf16[128,3072]{1,0:T(8,128)(2,1)}, bf16[128,3072]{1,0:T(8,128)(2,1)}, u32[]{:S(2)}, u32[]{:S(2)}) collective-permute-start(bf16[128,3072]{1,0:T(8,128)(2,1)} %q0.1), channel_id=1, source_target_pairs={{0,2},{2,0},{1,3},{3,1},{4,6},{6,4},{5,7},{7,5},{8,10},{10,8},{9,1... | collective-permute-start | bytes 2359304 | tf_op jit(solution)/shard_map/ppermute | solution.py:57
  24.3 0.8 broadcast_in_dim.4
  25.1 4.4 %all-to-all-start = ((bf16[8,8,3072]{2,1,0:T(8,128)(2,1)}), bf16[8,8,3072]{2,1,0:T(8,128)(2,1)S(1)}, u32[]{:S(2)}, u32[]{:S(2)}) async-start(bf16[8,8,3072]{2,1,0:T(8,128)(2,1)} %broadcast_in_dim.4), calls=%async_computation | async-start | bytes 786432 | tf_op jit(solution)/shard_map/all_to_all | solution.py:277
  29.5 2.7 %collective-permute-start.9 = (bf16[32,3072]{1,0:T(8,128)(2,1)S(1)}, bf16[32,3072]{1,0:T(8,128)(2,1)S(1)}, u32[]{:S(2)}, u32[]{:S(2)}) collective-permute-start(bf16[32,3072]{1,0:T(8,128)(2,1)S(1)} %collective-permute-done.8.refs_1_), channel_id=1, source_target_pairs={{0,28},{4,0},{8,4},{12,8},{16,12},{20,16},{24,20},{28,24},{1,29},{... | collective-permute-start | bytes 589832 | tf_op jit(solution)/shard_map/ppermute | solution.py:57
  32.2 1.4 %collective-permute-start.2 = (bf16[128,3072]{1,0:T(8,128)(2,1)S(1)}, bf16[128,3072]{1,0:T(8,128)(2,1)}, u32[]{:S(2)}, u32[]{:S(2)}) collective-permute-start(bf16[128,3072]{1,0:T(8,128)(2,1)S(1)} %copy-done.6), channel_id=1, source_target_pairs={{0,2},{2,0},{1,3},{3,1},{4,6},{6,4},{5,7},{7,5},{8,10},{10,8},{9,1... | collective-permute-start | bytes 2359304 | tf_op jit(solution)/shard_map/ppermute | solution.py:57
  33.7 10.1 %collective-permute-done.9.refs_2_ = bf16[32,3072]{1,0:T(8,128)(2,1)S(1)} collective-permute-done((bf16[32,3072]{1,0:T(8,128)(2,1)S(1)}, bf16[32,3072]{1,0:T(8,128)(2,1)S(1)}, u32[]{:S(2)}, u32[]{:S(2)}) %collective-permute-start.9) | collective-permute-done | bytes 196640 | tf_op jit(solution)/shard_map/ppermute | solution.py:57
  43.7 1.7 %collective-permute-start.3 = (bf16[128,3072]{1,0:T(8,128)(2,1)S(1)}, bf16[128,3072]{1,0:T(8,128)(2,1)}, u32[]{:S(2)}, u32[]{:S(2)}) collective-permute-start(bf16[128,3072]{1,0:T(8,128)(2,1)S(1)} %copy-done.7), channel_id=1, source_target_pairs={{0,2},{2,0},{1,3},{3,1},{4,6},{6,4},{5,7},{7,5},{8,10},{10,8},{9,1... | collective-permute-start | bytes 2359304 | tf_op jit(solution)/shard_map/ppermute | solution.py:57
  45.4 1.2 collective-permute-start.10
  46.6 4.0 %collective-permute-done.10.refs_3_ = bf16[32,3072]{1,0:T(8,128)(2,1)S(1)} collective-permute-done((bf16[32,3072]{1,0:T(8,128)(2,1)S(1)}, bf16[32,3072]{1,0:T(8,128)(2,1)S(1)}, u32[]{:S(2)}, u32[]{:S(2)}) %collective-permute-start.10) | collective-permute-done | bytes 196640 | tf_op jit(solution)/shard_map/ppermute | solution.py:57
  50.6 2.5 %collective-permute-start.14 = (bf16[32,3072]{1,0:T(8,128)(2,1)S(1)}, bf16[32,3072]{1,0:T(8,128)(2,1)S(1)}, u32[]{:S(2)}, u32[]{:S(2)}) collective-permute-start(bf16[32,3072]{1,0:T(8,128)(2,1)S(1)} %collective-permute-done.13.refs_7_), channel_id=1, source_target_pairs={{0,4},{4,8},{8,12},{12,16},{16,20},{20,24},{24,28},{28,0},{1,5},{5... | collective-permute-start | bytes 589832 | tf_op jit(solution)/shard_map/ppermute | solution.py:57
  53.1 3.3 %collective-permute-done.14.refs_6_ = bf16[32,3072]{1,0:T(8,128)(2,1)S(1)} collective-permute-done((bf16[32,3072]{1,0:T(8,128)(2,1)S(1)}, bf16[32,3072]{1,0:T(8,128)(2,1)S(1)}, u32[]{:S(2)}, u32[]{:S(2)}) %collective-permute-start.14) | collective-permute-done | bytes 196640 | tf_op jit(solution)/shard_map/ppermute | solution.py:57
  56.4 0.4 collective-permute-start.16
  56.8 1.1 collective-permute-start.17
  57.9 0.8 collective-permute-start.18
  58.9 1.2 collective-permute-start.11
  60.2 1.5 %collective-permute-start.15 = (bf16[16,3072]{1,0:T(8,128)(2,1)S(1)}, bf16[16,3072]{1,0:T(8,128)(2,1)S(1)}, u32[]{:S(2)}, u32[]{:S(2)}) collective-permute-start(bf16[16,3072]{1,0:T(8,128)(2,1)S(1)} %slice.37), channel_id=1, source_target_pairs={{0,4},{4,8},{8,12},{12,16},{16,20},{20,24},{24,28},{28,0},{1,5},{5... | collective-permute-start | bytes 294920 | tf_op jit(solution)/shard_map/ppermute | solution.py:57
  61.6 0.7 pad_maximum_fusion.3
  62.3 4.3 %shard_map.148 = (bf16[256,1536]{1,0:T(8,128)(2,1)}, bf16[256,1536]{1,0:T(8,128)(2,1)}, bf16[256,1536]{1,0:T(8,128)(2,1)}, bf16[256,1536]{1,0:T(8,128)(2,1)}) custom-call(s32[12]{0:T(128)} %stack.45.sc, bf16[128,3072]{1,0:T(8,128)(2,1)} %q0.1, bf16[128,3072]{1,0:T(8,128)(2,1)} %collective-permute-done.q1, bf16[128,3072]{1,0:T(8,128)(2,1)} %k0.1, ...), custom_call_target="tpu_custom_call" | custom-call | tf_op jit(solution)/shard_map/pallas_call | solution.py:235
  66.6 0.6 copy-done.20
  67.3 8.4 %shard_map.149 = (bf16[64,3072]{1,0:T(8,128)(2,1)}, bf16[64,3072]{1,0:T(8,128)(2,1)}, bf16[64,3072]{1,0:T(8,128)(2,1)}, bf16[64,3072]{1,0:T(8,128)(2,1)}) custom-call(s32[12]{0:T(128)} %stack.45.sc, bf16[256,1536]{1,0:T(8,128)(2,1)} %get-tuple-element.33.q, bf16[256,1536]{1,0:T(8,128)(2,1)} %get-tuple-element.34.d, bf16[32,3072]{1,0:T(8,128)(2,1)} %copy-done.8, ...), custom_call_target="tpu_custom_call" | custom-call | tf_op jit(solution)/shard_map/pallas_call | solution.py:235
  75.7 0.9 collective-permute-start.24
  76.6 2.2 %collective-permute-start.25 = (bf16[64,3072]{1,0:T(8,128)(2,1)}, bf16[64,3072]{1,0:T(8,128)(2,1)S(1)}, u32[]{:S(2)}, u32[]{:S(2)}) collective-permute-start(bf16[64,3072]{1,0:T(8,128)(2,1)} %get-tuple-element.37), channel_id=1, source_target_pairs={{0,32},{1,33},{32,0},{33,1},{2,34},{3,35},{34,2},{35,3},{4,36},{5,... | collective-permute-start | bytes 1179656 | tf_op jit(solution)/shard_map/ppermute | solution.py:57
  78.8 2.0 %collective-permute-start.26 = (bf16[64,3072]{1,0:T(8,128)(2,1)}, bf16[64,3072]{1,0:T(8,128)(2,1)S(1)}, u32[]{:S(2)}, u32[]{:S(2)}) collective-permute-start(bf16[64,3072]{1,0:T(8,128)(2,1)} %get-tuple-element.38), channel_id=1, source_target_pairs={{0,33},{1,0},{32,1},{33,32},{2,35},{3,2},{34,3},{35,34},{4,37},{5,... | collective-permute-start | bytes 1179656 | tf_op jit(solution)/shard_map/ppermute | solution.py:57
  80.8 0.7 copy-done.4
  81.7 4.7 %shard_map.150 = f32[24,256]{1,0:T(8,128)} custom-call(s32[12]{0:T(128)} %stack.45.sc, bf16[256,1536]{1,0:T(8,128)(2,1)} %get-tuple-element.39.k, bf16[256,1536]{1,0:T(8,128)(2,1)} %get-tuple-element.40.v, bf16[64,3072]{1,0:T(8,128)(2,1)} %bitcast.37, bf16[64,3072]{1,0:T(8,128)(2,1)} %copy-done.3, bf16[64,3072]{1,0:T(8,128)(2,1)} %copy-done.4, ...), custom_call_target="tpu_custom_call" | custom-call | tf_op jit(solution)/shard_map/pallas_call | solution.py:235
  86.3 1.4 %broadcast_in_dim.5 = f32[8,24,256]{2,1,0:T(8,128)} broadcast(f32[24,256]{1,0:T(8,128)} %shard_map.150), dimensions={1,2} | broadcast | bytes 221184 | tf_op jit(solution)/shard_map/broadcast_in_dim | solution.py:343
  87.8 7.8 %all-to-all-start.1 = ((f32[8,24,256]{2,1,0:T(8,128)}), f32[8,24,256]{2,1,0:T(8,128)S(1)}, u32[]{:S(2)}, u32[]{:S(2)}) async-start(f32[8,24,256]{2,1,0:T(8,128)} %broadcast_in_dim.5), calls=%async_computation.1 | async-start | bytes 393216 | tf_op jit(solution)/shard_map/all_to_all | solution.py:344
  95.6 0.7 copy-done.11
  96.5 0.7 copy-done.15
  97.2 3.0 %shard_map.155 = bf16[64,3072]{1,0:T(8,128)(2,1)} custom-call(s32[12]{0:T(128)} %stack.45.sc, bf16[64,3072]{1,0:T(8,128)(2,1)} %get-tuple-element.35.p0, bf16[64,3072]{1,0:T(8,128)(2,1)} %copy-done.11, bf16[64,3072]{1,0:T(8,128)(2,1)} %copy-done.13, bf16[64,3072]{1,0:T(8,128)(2,1)} %copy-done.15), custom_call_target="tpu_custom_call" | custom-call | tf_op jit(solution)/shard_map/pallas_call | solution.py:235
  100.3 4.0 %all-to-all-done.1.refs_0_ = f32[8,24,256]{2,1,0:T(8,128)S(1)} async-done(((f32[8,24,256]{2,1,0:T(8,128)}), f32[8,24,256]{2,1,0:T(8,128)S(1)}, u32[]{:S(2)}, u32[]{:S(2)}) %all-to-all-start.1) | async-done | bytes 196640 | tf_op jit(solution)/shard_map/all_to_all | solution.py:344
  104.2 3.5 %all-to-all-start.2 = ((bf16[8,8,3072]{2,1,0:T(8,128)(2,1)}), bf16[8,8,3072]{2,1,0:T(8,128)(2,1)S(1)}, u32[]{:S(2)}, u32[]{:S(2)}) async-start(bf16[8,8,3072]{2,1,0:T(8,128)(2,1)} %bitcast.39), calls=%async_computation.2 | async-start | bytes 786432 | tf_op jit(solution)/shard_map/all_to_all | solution.py:395
  107.8 0.5 copy-done.1
  108.3 0.6 shard_map.151.refs_0_
  108.9 2.6 %collective-permute-start.19 = (f32[24,256]{1,0:T(8,128)S(1)}, f32[24,256]{1,0:T(8,128)S(1)}, u32[]{:S(2)}, u32[]{:S(2)}) collective-permute-start(f32[24,256]{1,0:T(8,128)S(1)} %shard_map.151.refs_0_), channel_id=1, source_target_pairs={{0,33},{1,0},{32,1},{33,32},{2,35},{3,2},{34,3},{35,34},{4,37},{5,... | collective-permute-start | bytes 73736 | tf_op jit(solution)/shard_map/ppermute | solution.py:57
  111.5 0.8 collective-permute-start.20
  112.5 3.2 %collective-permute-done.20.refs_2_ = f32[24,256]{1,0:T(8,128)S(1)} collective-permute-done((f32[24,256]{1,0:T(8,128)S(1)}, f32[24,256]{1,0:T(8,128)S(1)}, u32[]{:S(2)}, u32[]{:S(2)}) %collective-permute-start.20) | collective-permute-done | bytes 24608 | tf_op jit(solution)/shard_map/ppermute | solution.py:57
  115.7 0.5 collective-permute-done.21.refs_3_
  116.2 0.6 shard_map.152.stats
  116.9 0.6 copy-done
  117.5 6.3 %shard_map.153 = (bf16[128,1536]{1,0:T(8,128)(2,1)}, bf16[128,1536]{1,0:T(8,128)(2,1)}, bf16[128,1536]{1,0:T(8,128)(2,1)}, bf16[128,1536]{1,0:T(8,128)(2,1)}) custom-call(s32[12]{0:T(128)} %stack.45.sc, bf16[256,1536]{1,0:T(8,128)(2,1)} %get-tuple-element.39.k, bf16[256,1536]{1,0:T(8,128)(2,1)} %get-tuple-element.40.v, f32[24,256]{1,0:T(8,128)} %copy-done, ...), custom_call_target="tpu_custom_call" | custom-call | tf_op jit(solution)/shard_map/pallas_call | solution.py:235
  123.8 5.2 %collective-permute-start.22 = (bf16[128,1536]{1,0:T(8,128)(2,1)}, bf16[128,1536]{1,0:T(8,128)(2,1)S(1)}, u32[]{:S(2)}, u32[]{:S(2)}) collective-permute-start(bf16[128,1536]{1,0:T(8,128)(2,1)} %get-tuple-element.42), channel_id=1, source_target_pairs={{0,2},{2,0},{1,3},{3,1},{4,6},{6,4},{5,7},{7,5},{8,10},{10,8},{9,1... | collective-permute-start | bytes 1179656 | tf_op jit(solution)/shard_map/ppermute | solution.py:57
  129.1 0.5 collective-permute-start.27
  129.6 0.9 collective-permute-done.22.k1
  130.5 0.6 collective-permute-done.23.v1
  131.1 0.2 copy-done.12
  131.3 0.6 copy-done.14
  131.8 3.3 %shard_map.154 = (bf16[128,3072]{1,0:T(8,128)(2,1)}, bf16[128,3072]{1,0:T(8,128)(2,1)}) custom-call(s32[12]{0:T(128)} %stack.45.sc, bf16[128,1536]{1,0:T(8,128)(2,1)} %get-tuple-element.41.k0, bf16[128,1536]{1,0:T(8,128)(2,1)} %copy-done.12, bf16[128,1536]{1,0:T(8,128)(2,1)} %get-tuple-element.43.v0, bf16[128,1536]{1,0:T(8,128)(2,1)} %copy-done.14), custom_call_target="tpu_custom_call" | custom-call | tf_op jit(solution)/shard_map/pallas_call | solution.py:235
  135.6 0.2 rev.3
  136.0 0.6 convert_element_type.28
  136.6 0.6 fusion.2
  (86 shorter events, 1.7 us)
Async XLA Ops:
  1.9 0.7 copy-start.22
  5.4 4.3 %collective-permute-start.4 = (bf16[4,6144]{1,0:T(4,128)(2,1)}, bf16[4,6144]{1,0:T(4,128)(2,1)S(1)}, u32[]{:S(2)}, u32[]{:S(2)}) collective-permute-start(bf16[4,6144]{1,0:T(4,128)(2,1)} %get-tuple-element.27), channel_id=1, source_target_pairs={{0,2},{2,0},{1,3},{3,1},{4,6},{6,4},{5,7},{7,5},{8,10},{10,8},{9,1... | collective-permute-start | bytes 147464 | tf_op jit(solution)/shard_map/ppermute | solution.py:57
  10.5 21.7 %copy-start.6 = (bf16[128,3072]{1,0:T(8,128)(2,1)S(1)}, bf16[128,3072]{1,0:T(8,128)(2,1)}, u32[]{:S(2)}) copy-start(bf16[128,3072]{1,0:T(8,128)(2,1)} %v0.1) | copy-start | bytes 2359300
  10.5 33.2 %copy-start.7 = (bf16[128,3072]{1,0:T(8,128)(2,1)S(1)}, bf16[128,3072]{1,0:T(8,128)(2,1)}, u32[]{:S(2)}) copy-start(bf16[128,3072]{1,0:T(8,128)(2,1)} %d0.1) | copy-start | bytes 2359300
  10.5 3.0 %collective-permute-start.5 = (bf16[8,3072]{1,0:T(8,128)(2,1)S(1)}, bf16[8,3072]{1,0:T(8,128)(2,1)S(1)}, u32[]{:S(2)}, u32[]{:S(2)}) collective-permute-start(bf16[8,3072]{1,0:T(8,128)(2,1)S(1)} %get-tuple-element.50), channel_id=1, source_target_pairs={{0,33},{1,0},{32,1},{33,32},{2,35},{3,2},{34,3},{35,34},{4,37},{5,... | collective-permute-start | bytes 147464 | tf_op jit(solution)/shard_map/ppermute | solution.py:57
  11.6 4.5 %collective-permute-start.6 = (bf16[8,3072]{1,0:T(8,128)(2,1)S(1)}, bf16[8,3072]{1,0:T(8,128)(2,1)S(1)}, u32[]{:S(2)}, u32[]{:S(2)}) collective-permute-start(bf16[8,3072]{1,0:T(8,128)(2,1)S(1)} %get-tuple-element.50), channel_id=1, source_target_pairs={{0,32},{1,33},{32,0},{33,1},{2,34},{3,35},{34,2},{35,3},{4,36},{5,... | collective-permute-start | bytes 147464 | tf_op jit(solution)/shard_map/ppermute | solution.py:57
  12.0 4.6 %collective-permute-start.7 = (bf16[8,3072]{1,0:T(8,128)(2,1)S(1)}, bf16[8,3072]{1,0:T(8,128)(2,1)S(1)}, u32[]{:S(2)}, u32[]{:S(2)}) collective-permute-start(bf16[8,3072]{1,0:T(8,128)(2,1)S(1)} %get-tuple-element.50), channel_id=1, source_target_pairs={{0,1},{1,32},{32,33},{33,0},{2,3},{3,34},{34,35},{35,2},{4,5},{5,3... | collective-permute-start | bytes 147464 | tf_op jit(solution)/shard_map/ppermute | solution.py:57
  16.6 8.5 %copy-start.8 = (bf16[32,3072]{1,0:T(8,128)(2,1)}, bf16[32,3072]{1,0:T(8,128)(2,1)S(1)}, u32[]{:S(2)}) copy-start(bf16[32,3072]{1,0:T(8,128)(2,1)S(1)} %pad_maximum_fusion.refs_0_) | copy-start | bytes 589828
  16.6 12.9 %collective-permute-start.8 = (bf16[32,3072]{1,0:T(8,128)(2,1)S(1)}, bf16[32,3072]{1,0:T(8,128)(2,1)S(1)}, u32[]{:S(2)}, u32[]{:S(2)}) collective-permute-start(bf16[32,3072]{1,0:T(8,128)(2,1)S(1)} %pad_maximum_fusion.refs_0_), channel_id=1, source_target_pairs={{0,28},{4,0},{8,4},{12,8},{16,12},{20,16},{24,20},{28,24},{1,29},{... | collective-permute-start | bytes 589832 | tf_op jit(solution)/shard_map/ppermute | solution.py:57
  22.3 10.0 %collective-permute-start.12 = (bf16[32,3072]{1,0:T(8,128)(2,1)S(1)}, bf16[32,3072]{1,0:T(8,128)(2,1)S(1)}, u32[]{:S(2)}, u32[]{:S(2)}) collective-permute-start(bf16[32,3072]{1,0:T(8,128)(2,1)S(1)} %pad_maximum_fusion.refs_0_), channel_id=1, source_target_pairs={{0,4},{4,8},{8,12},{12,16},{16,20},{20,24},{24,28},{28,0},{1,5},{5... | collective-permute-start | bytes 589832 | tf_op jit(solution)/shard_map/ppermute | solution.py:57
  22.3 34.5 %collective-permute-start = (bf16[128,3072]{1,0:T(8,128)(2,1)}, bf16[128,3072]{1,0:T(8,128)(2,1)}, u32[]{:S(2)}, u32[]{:S(2)}) collective-permute-start(bf16[128,3072]{1,0:T(8,128)(2,1)} %q0.1), channel_id=1, source_target_pairs={{0,2},{2,0},{1,3},{3,1},{4,6},{6,4},{5,7},{7,5},{8,10},{10,8},{9,1... | collective-permute-start | bytes 2359304 | tf_op jit(solution)/shard_map/ppermute | solution.py:57
  24.3 33.5 %collective-permute-start.1 = (bf16[128,3072]{1,0:T(8,128)(2,1)}, bf16[128,3072]{1,0:T(8,128)(2,1)}, u32[]{:S(2)}, u32[]{:S(2)}) collective-permute-start(bf16[128,3072]{1,0:T(8,128)(2,1)} %k0.1), channel_id=1, source_target_pairs={{0,2},{2,0},{1,3},{3,1},{4,6},{6,4},{5,7},{7,5},{8,10},{10,8},{9,1... | collective-permute-start | bytes 2359304 | tf_op jit(solution)/shard_map/ppermute | solution.py:57
  25.1 31.3 %all-to-all-start = ((bf16[8,8,3072]{2,1,0:T(8,128)(2,1)}), bf16[8,8,3072]{2,1,0:T(8,128)(2,1)S(1)}, u32[]{:S(2)}, u32[]{:S(2)}) async-start(bf16[8,8,3072]{2,1,0:T(8,128)(2,1)} %broadcast_in_dim.4), calls=%async_computation | async-start | bytes 786432 | tf_op jit(solution)/shard_map/all_to_all | solution.py:277
  29.5 26.9 %copy-start.16 = (bf16[32,3072]{1,0:T(8,128)(2,1)}, bf16[32,3072]{1,0:T(8,128)(2,1)S(1)}, u32[]{:S(2)}) copy-start(bf16[32,3072]{1,0:T(8,128)(2,1)S(1)} %collective-permute-done.8.refs_1_) | copy-start | bytes 589828
  29.5 14.3 %collective-permute-start.9 = (bf16[32,3072]{1,0:T(8,128)(2,1)S(1)}, bf16[32,3072]{1,0:T(8,128)(2,1)S(1)}, u32[]{:S(2)}, u32[]{:S(2)}) collective-permute-start(bf16[32,3072]{1,0:T(8,128)(2,1)S(1)} %collective-permute-done.8.refs_1_), channel_id=1, source_target_pairs={{0,28},{4,0},{8,4},{12,8},{16,12},{20,16},{24,20},{28,24},{1,29},{... | collective-permute-start | bytes 589832 | tf_op jit(solution)/shard_map/ppermute | solution.py:57
  32.2 24.2 %copy-start.17 = (bf16[32,3072]{1,0:T(8,128)(2,1)}, bf16[32,3072]{1,0:T(8,128)(2,1)S(1)}, u32[]{:S(2)}) copy-start(bf16[32,3072]{1,0:T(8,128)(2,1)S(1)} %collective-permute-done.12.refs_8_) | copy-start | bytes 589828
  32.2 13.2 %collective-permute-start.13 = (bf16[32,3072]{1,0:T(8,128)(2,1)S(1)}, bf16[32,3072]{1,0:T(8,128)(2,1)S(1)}, u32[]{:S(2)}, u32[]{:S(2)}) collective-permute-start(bf16[32,3072]{1,0:T(8,128)(2,1)S(1)} %collective-permute-done.12.refs_8_), channel_id=1, source_target_pairs={{0,4},{4,8},{8,12},{12,16},{16,20},{20,24},{24,28},{28,0},{1,5},{5... | collective-permute-start | bytes 589832 | tf_op jit(solution)/shard_map/ppermute | solution.py:57
  32.2 26.7 %collective-permute-start.2 = (bf16[128,3072]{1,0:T(8,128)(2,1)S(1)}, bf16[128,3072]{1,0:T(8,128)(2,1)}, u32[]{:S(2)}, u32[]{:S(2)}) collective-permute-start(bf16[128,3072]{1,0:T(8,128)(2,1)S(1)} %copy-done.6), channel_id=1, source_target_pairs={{0,2},{2,0},{1,3},{3,1},{4,6},{6,4},{5,7},{7,5},{8,10},{10,8},{9,1... | collective-permute-start | bytes 2359304 | tf_op jit(solution)/shard_map/ppermute | solution.py:57
  43.7 13.1 %copy-start.18 = (bf16[32,3072]{1,0:T(8,128)(2,1)}, bf16[32,3072]{1,0:T(8,128)(2,1)S(1)}, u32[]{:S(2)}) copy-start(bf16[32,3072]{1,0:T(8,128)(2,1)S(1)} %collective-permute-done.9.refs_2_) | copy-start | bytes 589828
  43.7 16.4 %collective-permute-start.3 = (bf16[128,3072]{1,0:T(8,128)(2,1)S(1)}, bf16[128,3072]{1,0:T(8,128)(2,1)}, u32[]{:S(2)}, u32[]{:S(2)}) collective-permute-start(bf16[128,3072]{1,0:T(8,128)(2,1)S(1)} %copy-done.7), channel_id=1, source_target_pairs={{0,2},{2,0},{1,3},{3,1},{4,6},{6,4},{5,7},{7,5},{8,10},{10,8},{9,1... | collective-permute-start | bytes 2359304 | tf_op jit(solution)/shard_map/ppermute | solution.py:57
  45.4 11.4 %copy-start.19 = (bf16[32,3072]{1,0:T(8,128)(2,1)}, bf16[32,3072]{1,0:T(8,128)(2,1)S(1)}, u32[]{:S(2)}) copy-start(bf16[32,3072]{1,0:T(8,128)(2,1)S(1)} %collective-permute-done.13.refs_7_) | copy-start | bytes 589828
  45.4 5.2 %collective-permute-start.10 = (bf16[32,3072]{1,0:T(8,128)(2,1)S(1)}, bf16[32,3072]{1,0:T(8,128)(2,1)S(1)}, u32[]{:S(2)}, u32[]{:S(2)}) collective-permute-start(bf16[32,3072]{1,0:T(8,128)(2,1)S(1)} %collective-permute-done.9.refs_2_), channel_id=1, source_target_pairs={{0,28},{4,0},{8,4},{12,8},{16,12},{20,16},{24,20},{28,24},{1,29},{... | collective-permute-start | bytes 589832 | tf_op jit(solution)/shard_map/ppermute | solution.py:57
  50.6 8.3 %copy-start.9 = (bf16[32,3072]{1,0:T(8,128)(2,1)}, bf16[32,3072]{1,0:T(8,128)(2,1)S(1)}, u32[]{:S(2)}) copy-start(bf16[32,3072]{1,0:T(8,128)(2,1)S(1)} %collective-permute-done.10.refs_3_) | copy-start | bytes 589828
  50.6 5.8 %collective-permute-start.14 = (bf16[32,3072]{1,0:T(8,128)(2,1)S(1)}, bf16[32,3072]{1,0:T(8,128)(2,1)S(1)}, u32[]{:S(2)}, u32[]{:S(2)}) collective-permute-start(bf16[32,3072]{1,0:T(8,128)(2,1)S(1)} %collective-permute-done.13.refs_7_), channel_id=1, source_target_pairs={{0,4},{4,8},{8,12},{12,16},{16,20},{20,24},{24,28},{28,0},{1,5},{5... | collective-permute-start | bytes 589832 | tf_op jit(solution)/shard_map/ppermute | solution.py:57
  56.4 2.5 %copy-start.10 = (bf16[32,3072]{1,0:T(8,128)(2,1)}, bf16[32,3072]{1,0:T(8,128)(2,1)S(1)}, u32[]{:S(2)}) copy-start(bf16[32,3072]{1,0:T(8,128)(2,1)S(1)} %collective-permute-done.14.refs_6_) | copy-start | bytes 589828
  56.4 10.2 %copy-start.2 = (bf16[8,8,3072]{2,1,0:T(8,128)(2,1)}, bf16[8,8,3072]{2,1,0:T(8,128)(2,1)S(1)}, u32[]{:S(2)}) copy-start(bf16[8,8,3072]{2,1,0:T(8,128)(2,1)S(1)} %all-to-all-done) | copy-start | bytes 1179652
  56.4 22.4 %collective-permute-start.16 = (bf16[64,3072]{1,0:T(8,128)(2,1)S(1)}, bf16[64,3072]{1,0:T(8,128)(2,1)S(1)}, u32[]{:S(2)}, u32[]{:S(2)}) collective-permute-start(bf16[64,3072]{1,0:T(8,128)(2,1)S(1)} %bitcast.34), channel_id=1, source_target_pairs={{0,33},{1,0},{32,1},{33,32},{2,35},{3,2},{34,3},{35,34},{4,37},{5,... | collective-permute-start | bytes 1179656 | tf_op jit(solution)/shard_map/ppermute | solution.py:57
  56.8 24.0 %collective-permute-start.17 = (bf16[64,3072]{1,0:T(8,128)(2,1)S(1)}, bf16[64,3072]{1,0:T(8,128)(2,1)S(1)}, u32[]{:S(2)}, u32[]{:S(2)}) collective-permute-start(bf16[64,3072]{1,0:T(8,128)(2,1)S(1)} %bitcast.35), channel_id=1, source_target_pairs={{0,32},{1,33},{32,0},{33,1},{2,34},{3,35},{34,2},{35,3},{4,36},{5,... | collective-permute-start | bytes 1179656 | tf_op jit(solution)/shard_map/ppermute | solution.py:57
  57.9 22.9 %collective-permute-start.18 = (bf16[64,3072]{1,0:T(8,128)(2,1)S(1)}, bf16[64,3072]{1,0:T(8,128)(2,1)S(1)}, u32[]{:S(2)}, u32[]{:S(2)}) collective-permute-start(bf16[64,3072]{1,0:T(8,128)(2,1)S(1)} %bitcast.36), channel_id=1, source_target_pairs={{0,1},{1,32},{32,33},{33,0},{2,3},{3,34},{34,35},{35,2},{4,5},{5,3... | collective-permute-start | bytes 1179656 | tf_op jit(solution)/shard_map/ppermute | solution.py:57
  58.9 7.7 %collective-permute-start.11 = (bf16[16,3072]{1,0:T(8,128)(2,1)S(1)}, bf16[16,3072]{1,0:T(8,128)(2,1)S(1)}, u32[]{:S(2)}, u32[]{:S(2)}) collective-permute-start(bf16[16,3072]{1,0:T(8,128)(2,1)S(1)} %slice.36), channel_id=1, source_target_pairs={{0,28},{4,0},{8,4},{12,8},{16,12},{20,16},{24,20},{28,24},{1,29},{... | collective-permute-start | bytes 294920 | tf_op jit(solution)/shard_map/ppermute | solution.py:57
  60.2 6.5 %collective-permute-start.15 = (bf16[16,3072]{1,0:T(8,128)(2,1)S(1)}, bf16[16,3072]{1,0:T(8,128)(2,1)S(1)}, u32[]{:S(2)}, u32[]{:S(2)}) collective-permute-start(bf16[16,3072]{1,0:T(8,128)(2,1)S(1)} %slice.37), channel_id=1, source_target_pairs={{0,4},{4,8},{8,12},{12,16},{16,20},{20,24},{24,28},{28,0},{1,5},{5... | collective-permute-start | bytes 294920 | tf_op jit(solution)/shard_map/ppermute | solution.py:57
  66.6 0.6 copy-start.20
  66.6 0.6 copy-start.21
  75.7 19.9 %collective-permute-start.24 = (bf16[64,3072]{1,0:T(8,128)(2,1)}, bf16[64,3072]{1,0:T(8,128)(2,1)S(1)}, u32[]{:S(2)}, u32[]{:S(2)}) collective-permute-start(bf16[64,3072]{1,0:T(8,128)(2,1)} %get-tuple-element.36), channel_id=1, source_target_pairs={{0,1},{1,32},{32,33},{33,0},{2,3},{3,34},{34,35},{35,2},{4,5},{5,3... | collective-permute-start | bytes 1179656 | tf_op jit(solution)/shard_map/ppermute | solution.py:57
  76.6 19.0 %collective-permute-start.25 = (bf16[64,3072]{1,0:T(8,128)(2,1)}, bf16[64,3072]{1,0:T(8,128)(2,1)S(1)}, u32[]{:S(2)}, u32[]{:S(2)}) collective-permute-start(bf16[64,3072]{1,0:T(8,128)(2,1)} %get-tuple-element.37), channel_id=1, source_target_pairs={{0,32},{1,33},{32,0},{33,1},{2,34},{3,35},{34,2},{35,3},{4,36},{5,... | collective-permute-start | bytes 1179656 | tf_op jit(solution)/shard_map/ppermute | solution.py:57
  78.8 2.0 %copy-start.3 = (bf16[64,3072]{1,0:T(8,128)(2,1)}, bf16[64,3072]{1,0:T(8,128)(2,1)S(1)}, u32[]{:S(2)}) copy-start(bf16[64,3072]{1,0:T(8,128)(2,1)S(1)} %collective-permute-done.16.a1) | copy-start | bytes 1179652
  78.8 16.8 %collective-permute-start.26 = (bf16[64,3072]{1,0:T(8,128)(2,1)}, bf16[64,3072]{1,0:T(8,128)(2,1)S(1)}, u32[]{:S(2)}, u32[]{:S(2)}) collective-permute-start(bf16[64,3072]{1,0:T(8,128)(2,1)} %get-tuple-element.38), channel_id=1, source_target_pairs={{0,33},{1,0},{32,1},{33,32},{2,35},{3,2},{34,3},{35,34},{4,37},{5,... | collective-permute-start | bytes 1179656 | tf_op jit(solution)/shard_map/ppermute | solution.py:57
  80.8 0.7 copy-start.4
  80.8 0.9 copy-start.5
  87.8 16.4 %all-to-all-start.1 = ((f32[8,24,256]{2,1,0:T(8,128)}), f32[8,24,256]{2,1,0:T(8,128)S(1)}, u32[]{:S(2)}, u32[]{:S(2)}) async-start(f32[8,24,256]{2,1,0:T(8,128)} %broadcast_in_dim.5), calls=%async_computation.1 | async-start | bytes 393216 | tf_op jit(solution)/shard_map/all_to_all | solution.py:344
  95.6 0.8 copy-start.11
  95.6 0.9 copy-start.13
  96.5 0.7 copy-start.15
  104.2 24.9 %all-to-all-start.2 = ((bf16[8,8,3072]{2,1,0:T(8,128)(2,1)}), bf16[8,8,3072]{2,1,0:T(8,128)(2,1)S(1)}, u32[]{:S(2)}, u32[]{:S(2)}) async-start(bf16[8,8,3072]{2,1,0:T(8,128)(2,1)} %bitcast.39), calls=%async_computation.2 | async-start | bytes 786432 | tf_op jit(solution)/shard_map/all_to_all | solution.py:395
  107.7 0.6 copy-start.1
  108.9 3.6 %collective-permute-start.19 = (f32[24,256]{1,0:T(8,128)S(1)}, f32[24,256]{1,0:T(8,128)S(1)}, u32[]{:S(2)}, u32[]{:S(2)}) collective-permute-start(f32[24,256]{1,0:T(8,128)S(1)} %shard_map.151.refs_0_), channel_id=1, source_target_pairs={{0,33},{1,0},{32,1},{33,32},{2,35},{3,2},{34,3},{35,34},{4,37},{5,... | collective-permute-start | bytes 73736 | tf_op jit(solution)/shard_map/ppermute | solution.py:57
  111.5 4.2 %collective-permute-start.20 = (f32[24,256]{1,0:T(8,128)S(1)}, f32[24,256]{1,0:T(8,128)S(1)}, u32[]{:S(2)}, u32[]{:S(2)}) collective-permute-start(f32[24,256]{1,0:T(8,128)S(1)} %shard_map.151.refs_0_), channel_id=1, source_target_pairs={{0,32},{1,33},{32,0},{33,1},{2,34},{3,35},{34,2},{35,3},{4,36},{5,... | collective-permute-start | bytes 73736 | tf_op jit(solution)/shard_map/ppermute | solution.py:57
  112.4 3.9 %collective-permute-start.21 = (f32[24,256]{1,0:T(8,128)S(1)}, f32[24,256]{1,0:T(8,128)S(1)}, u32[]{:S(2)}, u32[]{:S(2)}) collective-permute-start(f32[24,256]{1,0:T(8,128)S(1)} %shard_map.151.refs_0_), channel_id=1, source_target_pairs={{0,1},{1,32},{32,33},{33,0},{2,3},{3,34},{34,35},{35,2},{4,5},{5,3... | collective-permute-start | bytes 73736 | tf_op jit(solution)/shard_map/ppermute | solution.py:57
  116.9 0.6 copy-start
  123.8 6.7 %collective-permute-start.22 = (bf16[128,1536]{1,0:T(8,128)(2,1)}, bf16[128,1536]{1,0:T(8,128)(2,1)S(1)}, u32[]{:S(2)}, u32[]{:S(2)}) collective-permute-start(bf16[128,1536]{1,0:T(8,128)(2,1)} %get-tuple-element.42), channel_id=1, source_target_pairs={{0,2},{2,0},{1,3},{3,1},{4,6},{6,4},{5,7},{7,5},{8,10},{10,8},{9,1... | collective-permute-start | bytes 1179656 | tf_op jit(solution)/shard_map/ppermute | solution.py:57
  129.0 2.1 %collective-permute-start.23 = (bf16[128,1536]{1,0:T(8,128)(2,1)}, bf16[128,1536]{1,0:T(8,128)(2,1)S(1)}, u32[]{:S(2)}, u32[]{:S(2)}) collective-permute-start(bf16[128,1536]{1,0:T(8,128)(2,1)} %get-tuple-element.44), channel_id=1, source_target_pairs={{0,2},{2,0},{1,3},{3,1},{4,6},{6,4},{5,7},{7,5},{8,10},{10,8},{9,1... | collective-permute-start | bytes 1179656 | tf_op jit(solution)/shard_map/ppermute | solution.py:57
  129.1 6.0 %collective-permute-start.27 = (f32[4,3072]{1,0:T(4,128)S(1)}, f32[4,3072]{1,0:T(4,128)S(1)}, u32[]{:S(2)}, u32[]{:S(2)}) collective-permute-start(f32[4,3072]{1,0:T(4,128)S(1)} %slice.39), channel_id=1, source_target_pairs={{0,2},{2,0},{1,3},{3,1},{4,6},{6,4},{5,7},{7,5},{8,10},{10,8},{9,1... | collective-permute-start | bytes 147464 | tf_op jit(solution)/shard_map/ppermute | solution.py:57
  130.5 0.8 copy-start.12
  131.1 0.8 copy-start.14

commit v4 on v3

v4 whole, which is shorter than its diff:
```python
import functools
import math

import jax
import jax.numpy as jnp
import numpy as np
from jax import lax
from jax.experimental import pallas as pl
from jax.experimental.pallas import tpu as pltpu
from jax.sharding import Mesh
from jax.sharding import PartitionSpec as P

HD = 128
VFRAME = 512
ROPE_BASE = 10000.0
NEG = -1e30
SCALE = HD ** (-0.5)
LOG2E = math.log2(math.e)

NY, NZ, NC = 4, 8, 2
HEADS = 12
GROUPS = 2
HPG = HEADS // GROUPS
GW = HPG * HD
CW = HEADS * HD
VT = 128
AR = 4
CR = NC * AR
ZR = NZ * CR
YR = NY * CR
AUDIO = NY * ZR

ALL = ("dp", "yh", "z", "core", "yl")
Y = ("yh", "yl")
f32 = jnp.float32
bf16 = jnp.bfloat16


def frequencies():
    half = HD // 2
    return ROPE_BASE ** (-(jnp.arange(half, dtype=f32) / half))


def turn_tables(where_at):
    angle = where_at.astype(f32)[:, None] * frequencies()[None, :]
    cosine, sine = jnp.cos(angle), jnp.sin(angle)
    return jnp.concatenate([cosine, cosine], 1), jnp.concatenate([-sine, sine], 1)


def shift(x, axis, size, step):
    return lax.ppermute(x, axis, [(i, (i + step) % size) for i in range(size)])


def nt(a, b):
    return lax.dot_general(a, b, (((1,), (1,)), ((), ())), preferred_element_type=f32)


def nn(a, b):
    return lax.dot_general(a, b, (((1,), (0,)), ((), ())), preferred_element_type=f32)


def ahead(first, second):
    later = first(0)
    for i in range(HPG):
        now = later
        if i + 1 < HPG:
            later = first(i + 1)
        second(i, *now)


def head(i):
    return slice(i * HD, (i + 1) * HD)


def prepare_kernel(sc, q0, q1, k0, k1, v0, v1, d0, d1, cos, sin, qr, kr, vr, dr):
    limit = sc[3]
    for block, (q, k, v, d) in enumerate(((q0, k0, v0, d0), (q1, k1, v1, d1))):
        rows = slice(block * VT, (block + 1) * VT)
        cosine, sine = cos[block : block + 1, :], sin[block : block + 1, :]
        for i in range(HPG):
            for src, dst in ((q, qr), (k, kr)):
                x = src[:, head(i)].astype(f32)
                dst[rows, head(i)] = (
                    x * cosine + pltpu.roll(x, HD // 2, 1) * sine
                ).astype(bf16)
        vr[rows, :] = v[...]
        token = sc[4 + block] + lax.broadcasted_iota(jnp.int32, (VT, GW), 0)
        dr[rows, :] = jnp.where(token < limit, d[...].astype(f32), 0.0).astype(bf16)


def video_to_audio_kernel(sc, q, d, *refs):
    blocks, outs = refs[:NY], refs[NY:]
    core, y, limit = sc[0], sc[1], sc[2]
    row = lax.broadcasted_iota(jnp.int32, (AUDIO, HD), 0)
    yy = (row // ZR + y) % NY
    zz = (row // CR) % NZ
    r = row % CR
    cc = jnp.where(r < AR, core, 1 - core)
    own = ((yy // 2 * NZ + zz) * NC + cc) * 2 + yy % 2
    bias = jnp.where(own * AR + r % AR < limit, 0.0, NEG)
    bias = jnp.concatenate([bias, bias], 1)

    def scores(i):
        key = jnp.concatenate([a[:, head(i)] for a in blocks], 0)
        value = jnp.concatenate([a[:, head(HPG + i)] for a in blocks], 0)
        return nt(key, q[:, head(i)]), nt(value, d[:, head(i)])

    def gradients(i, s, dp):
        query, grad = q[:, head(i)], d[:, head(i)]
        s = s * (SCALE * LOG2E) + bias
        e = jnp.exp2(s - jnp.max(s, axis=0, keepdims=True))
        p = e * (1.0 / jnp.sum(e, axis=0, keepdims=True))
        pb = p.astype(bf16)
        delta = jnp.sum(p * dp, axis=0, keepdims=True)
        ds = (p * (dp - delta)).astype(bf16)
        dk = (nn(ds, query) * SCALE).astype(bf16)
        dv = nn(pb, grad).astype(bf16)
        for n, o in enumerate(outs):
            o[:, head(i)] = dk[n * ZR : (n + 1) * ZR]
            o[:, head(HPG + i)] = dv[n * ZR : (n + 1) * ZR]

    ahead(scores, gradients)


def sum_kernel(sc, p0, p1, p2, p3, out):
    out[...] = sum(p[...].astype(f32) for p in (p0, p1, p2, p3)).astype(bf16)


def pack_kernel(sc, keep, got, qd, copies):
    both = jnp.concatenate([keep[...].astype(f32), got[...].astype(f32)], 0)
    qd[...] = both[:, : 2 * CW].astype(bf16)
    kv = both[:, 2 * CW :]
    kv = jnp.concatenate([kv, kv], 0).astype(bf16)
    for n in range(NZ // 2):
        copies[n * 2 * CR : (n + 1) * 2 * CR, :] = kv


def audio_turn(sc, freq):
    row = lax.broadcasted_iota(jnp.int32, (AR, HD), 0)
    lane = lax.broadcasted_iota(jnp.int32, (AR, HD), 1)
    pos = functools.reduce(lambda a, n: jnp.where(row == n, sc[8 + n], a), range(1, AR), sc[8])
    angle = pos.astype(f32) * freq[...]
    cosine = jnp.cos(angle)
    sine = jnp.where(lane < HD // 2, -jnp.sin(angle), jnp.sin(angle))
    return cosine, sine


def audio_kernel(sc, q, k, v, d, freq, keep, give):
    core, own = sc[0], sc[7]
    cosine, sine = audio_turn(sc, freq)
    row = lax.broadcasted_iota(jnp.int32, (AR, HD), 0)
    ours = own * AR + row < sc[2]

    def turn(x):
        x = x.astype(f32)
        swapped = jnp.concatenate([x[:, HD // 2 :], x[:, : HD // 2]], 1)
        return x * cosine + swapped * sine

    def pair(ref, n, change):
        return [change(ref[:, head(c * HEADS + n)]) for c in range(NC)]

    same = lambda x: x.astype(f32)
    clear = lambda x: jnp.where(ours, x.astype(f32), 0.0)
    for n in range(HEADS):
        base = n // HPG * 2 * GW + n % HPG * HD
        for at, ref, change in ((base, q, turn), (base + GW, d, clear), (2 * CW + base, k, turn), (2 * CW + base + GW, v, same)):
            a, b = pair(ref, n, change)
            lanes = slice(at, at + HD)
            keep[:, lanes] = jnp.where(core == 0, a, b).astype(bf16)
            give[:, lanes] = jnp.where(core == 0, b, a).astype(bf16)


def video_token(sc, row):
    return jnp.where(row < VT, sc[4] + row, sc[5] + row - VT)


def statistics_kernel(sc, k, v, qd, copies, out):
    g = pl.program_id(0)
    row = lax.broadcasted_iota(jnp.int32, (2 * VT, HD), 0)
    bias = jnp.where(video_token(sc, row) < sc[3], 0.0, NEG)
    bias = jnp.concatenate([bias, bias], 1)
    some = jnp.minimum(sc[4], sc[5]) < sc[3]

    def scores(i):
        return nt(k[:, head(i)], qd[:, head(i)]), nt(v[:, head(i)], qd[:, head(HPG + i)])

    def sums(i, s, dp):
        s = s * (SCALE * LOG2E) + bias
        m = jnp.max(s, axis=0, keepdims=True)
        e = jnp.exp2(s - m)
        c = jnp.sum(e, axis=0, keepdims=True)
        t = jnp.sum(e * dp, axis=0, keepdims=True)
        out[pl.ds(g * HPG + i, 1), :] = jnp.where(some, m + jnp.log2(c), NEG)
        out[pl.ds(HEADS + g * HPG + i, 1), :] = jnp.where(some, t / c, 0.0)

    ahead(scores, sums)

    @pl.when(g == GROUPS - 1)
    def _():
        for n in range(NZ):
            copies[n] = out[...]


def merge(lses, deltas):
    top = functools.reduce(jnp.maximum, lses)
    weights = [jnp.exp2(x - top) for x in lses]
    total = sum(weights)
    delta = sum(w * x for w, x in zip(weights, deltas)) / total
    return top + jnp.log2(total), delta


def merge_kernel(sc, *refs, count, turn):
    *parts, out = refs
    if count > 1:
        (part,) = parts
        parts = [part.at[n] for n in range(count)]
    lse, delta = merge([p[:HEADS] for p in parts], [p[HEADS:] for p in parts])
    both = jnp.concatenate([lse, delta], 0)
    place = lax.broadcasted_iota(jnp.int32, both.shape, 1) // CR % NY
    if turn > 0:
        a = pltpu.roll(both, sc[1] * CR, 1)
        b = pltpu.roll(both, AUDIO - YR + sc[1] * CR, 1)
        out[...] = jnp.where(place >= sc[1], a, b)
    else:
        a = pltpu.roll(both, lax.rem(AUDIO - sc[1] * CR, AUDIO), 1)
        b = pltpu.roll(both, YR - sc[1] * CR, 1)
        out[...] = jnp.where(place < NY - sc[1], a, b)


def audio_to_video_kernel(sc, k, v, stats, cos, sin, qd, dk0, dk1, dv0, dv1):
    g = pl.program_id(0)
    row = lax.broadcasted_iota(jnp.int32, (2 * VT, HD), 0)
    valid = video_token(sc, row) < sc[3]

    def scores(i):
        query, grad = qd[:, head(i)], qd[:, head(HPG + i)]
        return query, grad, nt(k[:, head(i)], query), nt(v[:, head(i)], grad)

    def gradients(i, query, grad, s, dp):
        lse = stats[pl.ds(g * HPG + i, 1), :]
        delta = stats[pl.ds(HEADS + g * HPG + i, 1), :]
        p = jnp.exp2(s * (SCALE * LOG2E) - lse)
        ds = (p * (dp - delta)).astype(bf16)
        dv = jnp.where(valid, nn(p.astype(bf16), grad), 0.0).astype(bf16)
        dk = jnp.where(valid, nn(ds, query) * SCALE, 0.0)
        for block, (dko, dvo) in enumerate(((dk0, dv0), (dk1, dv1))):
            rows = slice(block * VT, (block + 1) * VT)
            x = dk[rows]
            dko[:, head(i)] = (
                x * cos[block : block + 1, :]
                - pltpu.roll(x, HD // 2, 1) * sin[block : block + 1, :]
            ).astype(bf16)
            dvo[:, head(i)] = dv[rows]

    ahead(scores, gradients)


def finish_kernel(sc, total, other, freq, dk, dv):
    core = sc[0]
    cosine, sine = audio_turn(sc, freq)
    for c in range(NC):
        mine = core == c
        for n in range(HEADS):
            base = n // HPG * 2 * GW + n % HPG * HD
            lanes = head(c * HEADS + n)
            x, w = (
                jnp.where(mine, total[:AR, at : at + HD], other[:, at : at + HD])
                for at in (base, base + GW)
            )
            swapped = jnp.concatenate([x[:, HD // 2 :], x[:, : HD // 2]], 1)
            dk[:, lanes] = (x * cosine - swapped * sine).astype(bf16)
            dv[:, lanes] = w.astype(bf16)


def join_kernel(sc, k1, v1, k, v, dk, dv):
    dk[...] = k1[...]
    dv[...] = v1[...]


def call(kernel, scalars, args, specs, outs, out_specs, grid=(GROUPS,), limit=16, scratch=(), aliases={}):
    return pl.pallas_call(
        kernel,
        grid_spec=pltpu.PrefetchScalarGridSpec(
            num_scalar_prefetch=1, grid=grid, in_specs=specs, out_specs=out_specs, scratch_shapes=scratch
        ),
        out_shape=outs,
        input_output_aliases=aliases,
        compiler_params=pltpu.CompilerParams(vmem_limit_bytes=limit * 1024 * 1024),
        cost_estimate=pl.CostEstimate(flops=0, bytes_accessed=0, transcendentals=0),
    )(scalars, *args)


def local(q_video, k_video, v_video, d_video, q_audio, k_audio, v_audio, d_audio, audio_pos, video_len, audio_len):
    yh, z, core, yl = (lax.axis_index(a) for a in ("yh", "z", "core", "yl"))
    y = yh * 2 + yl
    own = ((yh * NZ + z) * NC + core) * 2 + yl
    pair = ((yh * NZ + z) * NC + 1 - core) * 2 + yl
    scalars = jnp.stack(
        [core, y, audio_len[0], video_len[0], own * VT, pair * VT, z, own, *audio_pos]
    ).astype(jnp.int32)

    frequency = np.tile(ROPE_BASE ** (-np.arange(HD // 2) / (HD // 2)), 2).astype(np.float32)
    whole = pl.BlockSpec((AR, NC * CW), lambda g, sc: (0, 0))
    wide = pl.BlockSpec((AR, 4 * CW), lambda g, sc: (0, 0))
    keep, give = call(
        audio_kernel,
        scalars,
        (q_audio, k_audio, v_audio, d_audio, frequency[None]),
        [whole] * 4 + [pl.BlockSpec((1, HD), lambda g, sc: (0, 0))],
        [jax.ShapeDtypeStruct((AR, 4 * CW), bf16)] * 2,
        [wide] * 2,
        grid=(1,),
        limit=56,
    )
    chip = pl.BlockSpec((CR, 2 * CW), lambda g, sc: (0, 0))
    along = pl.BlockSpec((ZR, 2 * CW), lambda g, sc: (0, 0))
    qd, copies = call(
        pack_kernel,
        scalars,
        (keep, shift(give, "core", NC, 1)),
        [wide] * 2,
        [jax.ShapeDtypeStruct((CR, 2 * CW), bf16), jax.ShapeDtypeStruct((ZR, 2 * CW), bf16)],
        [chip, along],
        grid=(1,),
        limit=16,
    )
    kv_z = lax.all_to_all(copies, "z", split_axis=0, concat_axis=0, tiled=True)

    def along_y(x):
        return [x] + [shift(x, Y, NY, NY - n) for n in range(1, NY)]

    q_pair, k_pair, v_pair, d_pair = (
        shift(x, "core", NC, 1) for x in (q_video, k_video, v_video, d_video)
    )
    cos, sin = turn_tables(jnp.stack([own * VT // VFRAME, pair * VT // VFRAME]))
    half = pl.BlockSpec((VT, GW), lambda g, sc: (0, sc[0] * GROUPS + g))
    table = pl.BlockSpec((2, HD), lambda g, sc: (0, 0))
    video_in = pl.BlockSpec((2 * VT, GW), lambda g, sc: (0, g))
    all_in = pl.BlockSpec((AUDIO, 2 * GW), lambda g, sc: (0, g))
    audio_in = pl.BlockSpec((ZR, 2 * GW), lambda g, sc: (0, g))
    video = pl.BlockSpec((2 * VT, GW), lambda g, sc: (0, g))
    audio = pl.BlockSpec((ZR, 2 * GW), lambda g, sc: (0, g))
    rows = pl.BlockSpec((2 * HEADS, AUDIO), lambda g, sc: (0, 0))
    mine = pl.BlockSpec((VT, GW), lambda g, sc: (0, g))
    video_shape = jax.ShapeDtypeStruct((2 * VT, CW), bf16)
    rows_shape = jax.ShapeDtypeStruct((2 * HEADS, AUDIO), f32)
    full_shape = jax.ShapeDtypeStruct((VT, NC * CW), bf16)
    mine_shape = jax.ShapeDtypeStruct((VT, CW), bf16)
    audio_shape = jax.ShapeDtypeStruct((ZR, 2 * CW), bf16)

    qr, kr, vr, dr = call(
        prepare_kernel,
        scalars,
        (q_video, q_pair, k_video, k_pair, v_video, v_pair, d_video, d_pair, cos, sin),
        [half] * 8 + [table] * 2,
        [video_shape] * 4,
        [video] * 4,
    )


    home = jnp.concatenate(along_y(qd), 0)
    copies = jnp.broadcast_to(home[None], (NZ,) + home.shape).reshape(AUDIO, 2 * CW)
    copies, kv_z = lax.optimization_barrier((copies, kv_z))
    qd_all = lax.all_to_all(copies, "z", split_axis=0, concat_axis=0, tiled=True)
    kv_all = along_y(kv_z)

    parts = call(
        video_to_audio_kernel,
        scalars,
        (qr, dr, *kv_all),
        [video_in] * 2 + [audio_in] * NY,
        [audio_shape] * NY,
        [audio] * NY,
    )
    parts_y = [parts[0]] + [shift(parts[n], Y, NY, n) for n in range(1, NY)]

    kr, parts = lax.optimization_barrier((kr, parts))
    every = pl.BlockSpec((NZ, 2 * HEADS, AUDIO), lambda g, sc: (0, 0, 0))
    copies = call(
        statistics_kernel,
        scalars,
        (kr, vr, qd_all),
        [video_in] * 2 + [all_in],
        jax.ShapeDtypeStruct((NZ, 2 * HEADS, AUDIO), f32),
        every,
        scratch=[pltpu.VMEM((2 * HEADS, AUDIO), f32)],
    )
    stats = lax.all_to_all(copies, "z", split_axis=0, concat_axis=0, tiled=True)
    stats = call(
        functools.partial(merge_kernel, count=NZ, turn=1),
        scalars,
        (stats,),
        [every],
        rows_shape,
        rows,
        grid=(1,),
        limit=16,
    )
    sums = call(
        sum_kernel,
        scalars,
        parts_y,
        [audio_in] * NY,
        audio_shape,
        audio,
    )
    stats = call(
        functools.partial(merge_kernel, count=1, turn=-1),
        scalars,
        along_y(stats),
        [rows] * NY,
        rows_shape,
        rows,
        grid=(1,),
        limit=16,
    )
    dk0, dk1, dv0, dv1 = call(
        audio_to_video_kernel,
        scalars,
        (kr, vr, stats, cos, sin, qd_all),
        [video_in] * 2 + [rows] + [table] * 2 + [all_in],
        [full_shape, mine_shape] * 2,
        [half, mine] * 2,
    )

    dk_there = dk1
    dk1, dv1 = shift(dk1, "core", NC, 1), shift(dv1, "core", NC, 1)
    sums = lax.all_to_all(sums, "z", split_axis=0, concat_axis=0, tiled=True)
    sums, _ = lax.optimization_barrier((sums, dk_there))
    sums = jnp.sum(sums.reshape(NZ, CR, 2 * CW).astype(f32), 0)
    few = pl.BlockSpec((AR, NC * CW), lambda g, sc: (0, 0))
    dk_audio, dv_audio = call(
        finish_kernel,
        scalars,
        (sums, shift(sums[AR:], "core", NC, 1), frequency[None]),
        [chip, few, pl.BlockSpec((1, HD), lambda g, sc: (0, 0))],
        [jax.ShapeDtypeStruct((AR, NC * CW), bf16)] * 2,
        [few] * 2,
        grid=(1,),
        limit=16,
    )
    dk1, dv1, dk_audio, dv_audio = lax.optimization_barrier((dk1, dv1, dk_audio, dv_audio))
    place = pl.BlockSpec(memory_space=pl.ANY)
    other = pl.BlockSpec((VT, GW), lambda g, sc: (0, (1 - sc[0]) * GROUPS + g))
    dk_video, dv_video = call(
        join_kernel,
        scalars,
        (dk1, dv1, dk0, dv0),
        [mine] * 2 + [place] * 2,
        [full_shape] * 2,
        [other] * 2,
        aliases={3: 0, 4: 1},
        limit=16,
    )
    return dk_video, dv_video, dk_audio, dv_audio


def solution(mesh):
    fine = Mesh(mesh.devices.reshape(mesh.shape["dp"], 2, NZ, NC, 2), ALL)
    rows = P(ALL, None)
    return jax.shard_map(
        local,
        mesh=fine,
        in_specs=(rows,) * 8 + (P(ALL), P("dp"), P("dp")),
        out_specs=(rows,) * 4,
        check_vma=False,
    )
```

time: 138 us -> 122 us (0.88)
  starting transfers between devices: 57.5 us -> 47.6 us
  Pallas kernels: 33.4 us -> 26.1 us
  waiting for transfers between devices: 31.6 us -> 33.5 us
    ppermute x28 -> x20, starting transfers between devices: 41.9 us -> 26.7 us  [shift(): return lax.ppermute(x, axis, [(i, (i + step) % size) for i in range(size)])]
    all_to_all x1 -> x2, waiting for transfers between devices: 0.01 us -> 12.8 us  [the longest x1 7.98 us: local(): kv_z = lax.all_to_all(copies, 'z', split_axis=0, concat_axis=0, tiled=True)]
    pallas_call x9 -> x11, Pallas kernels: 33.4 us -> 26.1 us  [call(): pl.pallas_call(kernel, grid_spec=pltpu.PrefetchScalarGridSpec(num_scalar_...]
    ppermute x28 -> x20, waiting for transfers between devices: 27.7 us -> 20.7 us  [shift(): return lax.ppermute(x, axis, [(i, (i + step) % size) for i in range(size)])]
    all_to_all x1 -> x2, starting transfers between devices: 4.36 us -> 10.2 us  [the longest x1 6.45 us: local(): kv_z = lax.all_to_all(copies, 'z', split_axis=0, concat_axis=0, tiled=True)]
    all_to_all x1, waiting for transfers between devices: 3.95 us -> 0.01 us  [local(): stats = lax.all_to_all(copies, 'z', split_axis=0, concat_axis=0, tiled=True)]
    all_to_all x1, starting transfers between devices: 7.79 us -> 4.02 us  [local(): stats = lax.all_to_all(copies, 'z', split_axis=0, concat_axis=0, tiled=True)]
    all_to_all x1, starting transfers between devices: 3.45 us -> 6.74 us  [local(): sums = lax.all_to_all(sums, 'z', split_axis=0, concat_axis=0, tiled=True)]
  transfers between devices with their start and end apart: 31 -> 24, of which waited for: 12 -> 13; matrix products, arithmetic and copies ran while one was open for 2% -> 1% of each run, Pallas kernels for 23% -> 17%
where the time goes in v4:
time: 122 us; the launch traced here: 121 us
  starting transfers between devices  47.6 us (39%)
  waiting for transfers between devices  33.5 us (27%)
  Pallas kernels  26.1 us (21%)
  local copies, waits for them, and re-layouts  10.4 us (9%)
  between operations  2.07 us (2%)
  other arithmetic  1.35 us (1%)
    ppermute x20, starting transfers between devices, shift(): return lax.ppermute(x, axis, [(i, (i + step) % size) for i in range(size)])  26.7 us
    pallas_call x11, Pallas kernels, call(): pl.pallas_call(kernel, grid_spec=pltpu.PrefetchScalarGridSpec(num_scalar_...  26.1 us
    ppermute x20, waiting for transfers between devices, shift(): return lax.ppermute(x, axis, [(i, (i + step) % size) for i in range(size)])  20.7 us
    all_to_all x1, waiting for transfers between devices, local(): kv_z = lax.all_to_all(copies, 'z', split_axis=0, concat_axis=0, tiled=True)  7.98 us
    unnamed x24, local copies, waits for them, and re-layouts  7.76 us
    all_to_all x1, starting transfers between devices, local(): sums = lax.all_to_all(sums, 'z', split_axis=0, concat_axis=0, tiled=True)  6.74 us
    all_to_all x1, starting transfers between devices, local(): kv_z = lax.all_to_all(copies, 'z', split_axis=0, concat_axis=0, tiled=True)  6.45 us
    all_to_all x1, waiting for transfers between devices, local(): lax.all_to_all(copies, 'z', split_axis=0, concat_axis=0, tiled=True)  4.83 us
  transfers between devices with their start and end apart: 24, of which 13 were waited for; matrix products, arithmetic and copies ran while one was open for 1% of the time, Pallas kernels for 17%

profile of v4, /device:TPU:1, one launch (start us, length us, event | category | flops | bytes accessed | tf_op | source)
XLA Modules:
  0.0 121.1 jit_solution(4536572653836427834)
XLA Ops:
  1.9 1.3 %stack.36.sc = s32[12]{0:T(128)} concatenate(s32[1]{0:T(128)} %bitcast, s32[1]{0:T(128)} %bitcast.1, s32[1]{0:T(128)S(6)} %copy.22, s32[1]{0:T(128)S(6)} %copy.21, s32[1]{0:T(128)} %bitcast.2, s32[1]{0:T(128)} %bitcast.3, s32[1]{0:T(128)} %bitcast.4, s32[1]{0:T(128)} %bitcast.5, s32[4]{0:T(128)} %param.21), dimensions={0} | concatenate | bytes 96 | tf_op jit(solution)/shard_map/stack | solution.py:298
  3.3 2.2 %shard_map.157 = (bf16[4,6144]{1,0:T(4,128)(2,1)}, bf16[4,6144]{1,0:T(4,128)(2,1)}) custom-call(s32[12]{0:T(128)} %stack.36.sc, bf16[4,3072]{1,0:T(4,128)(2,1)} %q.1, bf16[4,3072]{1,0:T(4,128)(2,1)} %k.1, bf16[4,3072]{1,0:T(4,128)(2,1)} %v.1, bf16[4,3072]{1,0:T(4,128)(2,1)} %d.1, f32[1,128]{1,0:T(1,128)} %constant.55.clone.freq), custom_call_target="tpu_custom_call" | custom-call | tf_op jit(solution)/shard_map/pallas_call | solution.py:281
  5.5 3.2 %collective-permute-start.4 = (bf16[4,6144]{1,0:T(4,128)(2,1)}, bf16[4,6144]{1,0:T(4,128)(2,1)S(1)}, u32[]{:S(2)}, u32[]{:S(2)}) collective-permute-start(bf16[4,6144]{1,0:T(4,128)(2,1)} %get-tuple-element.36), channel_id=1, source_target_pairs={{0,2},{2,0},{1,3},{3,1},{4,6},{6,4},{5,7},{7,5},{8,10},{10,8},{9,1... | collective-permute-start | bytes 147464 | tf_op jit(solution)/shard_map/ppermute | solution.py:51
  8.7 1.1 collective-permute-done.4.got
  9.8 0.7 copy-done.8
  10.5 0.8 copy-done.10
  11.3 1.3 %shard_map.158 = (bf16[8,3072]{1,0:T(8,128)(2,1)S(1)}, bf16[64,3072]{1,0:T(8,128)(2,1)}) custom-call(s32[12]{0:T(128)S(1)} %copy-done.8, bf16[4,6144]{1,0:T(4,128)(2,1)S(1)} %copy-done.10, bf16[4,6144]{1,0:T(4,128)(2,1)S(1)} %collective-permute-done.4.got), custom_call_target="tpu_custom_call" | custom-call | tf_op jit(solution)/shard_map/pallas_call | solution.py:281
  12.6 6.4 %all-to-all-start = ((bf16[8,8,3072]{2,1,0:T(8,128)(2,1)}), bf16[8,8,3072]{2,1,0:T(8,128)(2,1)S(1)}, u32[]{:S(2)}, u32[]{:S(2)}) async-start(bf16[8,8,3072]{2,1,0:T(8,128)(2,1)} %bitcast.9), calls=%async_computation | async-start | bytes 786432 | tf_op jit(solution)/shard_map/all_to_all | solution.py:327
  19.0 1.3 %collective-permute-start.7 = (bf16[8,3072]{1,0:T(8,128)(2,1)S(1)}, bf16[8,3072]{1,0:T(8,128)(2,1)S(1)}, u32[]{:S(2)}, u32[]{:S(2)}) collective-permute-start(bf16[8,3072]{1,0:T(8,128)(2,1)S(1)} %get-tuple-element.37), channel_id=1, source_target_pairs={{0,1},{1,32},{32,33},{33,0},{2,3},{3,34},{34,35},{35,2},{4,5},{5,3... | collective-permute-start | bytes 147464 | tf_op jit(solution)/shard_map/ppermute | solution.py:51
  20.3 2.6 %collective-permute-start.6 = (bf16[8,3072]{1,0:T(8,128)(2,1)S(1)}, bf16[8,3072]{1,0:T(8,128)(2,1)S(1)}, u32[]{:S(2)}, u32[]{:S(2)}) collective-permute-start(bf16[8,3072]{1,0:T(8,128)(2,1)S(1)} %get-tuple-element.37), channel_id=1, source_target_pairs={{0,32},{1,33},{32,0},{33,1},{2,34},{3,35},{34,2},{35,3},{4,36},{5,... | collective-permute-start | bytes 147464 | tf_op jit(solution)/shard_map/ppermute | solution.py:51
  22.9 1.1 collective-permute-start.5
  24.0 0.9 collective-permute-done.6
  24.9 1.2 %collective-permute-done.5 = bf16[8,3072]{1,0:T(8,128)(2,1)S(1)} collective-permute-done((bf16[8,3072]{1,0:T(8,128)(2,1)S(1)}, bf16[8,3072]{1,0:T(8,128)(2,1)S(1)}, u32[]{:S(2)}, u32[]{:S(2)}) %collective-permute-start.5) | collective-permute-done | bytes 49184 | tf_op jit(solution)/shard_map/ppermute | solution.py:51
  26.2 8.0 %all-to-all-done = bf16[8,8,3072]{2,1,0:T(8,128)(2,1)S(1)} async-done(((bf16[8,8,3072]{2,1,0:T(8,128)(2,1)}), bf16[8,8,3072]{2,1,0:T(8,128)(2,1)S(1)}, u32[]{:S(2)}, u32[]{:S(2)}) %all-to-all-start) | async-done | bytes 393248 | tf_op jit(solution)/shard_map/all_to_all | solution.py:327
  34.2 1.4 %broadcast_in_dim.2 = bf16[8,32,3072]{2,1,0:T(8,128)(2,1)} broadcast(bf16[32,3072]{1,0:T(8,128)(2,1)S(1)} %pad_maximum_fusion), dimensions={1,2} | broadcast | bytes 1769472 | tf_op jit(solution)/shard_map/broadcast_in_dim | solution.py:362
  35.5 3.7 %all-to-all-start.1 = ((bf16[8,32,3072]{2,1,0:T(8,128)(2,1)}), bf16[8,32,3072]{2,1,0:T(8,128)(2,1)S(1)}, u32[]{:S(2)}, u32[]{:S(2)}) async-start(bf16[8,32,3072]{2,1,0:T(8,128)(2,1)} %broadcast_in_dim.2), calls=%async_computation.1 | async-start | bytes 3145728 | tf_op jit(solution)/shard_map/all_to_all | solution.py:364
  39.3 0.6 collective-permute-start
  39.9 0.1 collective-permute-start.1
  40.0 0.4 collective-permute-start.2
  40.4 0.1 collective-permute-start.3
  40.5 1.3 %collective-permute-start.10 = (bf16[64,3072]{1,0:T(8,128)(2,1)S(1)}, bf16[64,3072]{1,0:T(8,128)(2,1)S(1)}, u32[]{:S(2)}, u32[]{:S(2)}) collective-permute-start(bf16[64,3072]{1,0:T(8,128)(2,1)S(1)} %bitcast.20), channel_id=1, source_target_pairs={{0,1},{1,32},{32,33},{33,0},{2,3},{3,34},{34,35},{35,2},{4,5},{5,3... | collective-permute-start | bytes 1179656 | tf_op jit(solution)/shard_map/ppermute | solution.py:51
  41.8 0.1 collective-permute-done.q1
  41.9 2.9 %collective-permute-start.9 = (bf16[64,3072]{1,0:T(8,128)(2,1)S(1)}, bf16[64,3072]{1,0:T(8,128)(2,1)S(1)}, u32[]{:S(2)}, u32[]{:S(2)}) collective-permute-start(bf16[64,3072]{1,0:T(8,128)(2,1)S(1)} %bitcast.21), channel_id=1, source_target_pairs={{0,32},{1,33},{32,0},{33,1},{2,34},{3,35},{34,2},{35,3},{4,36},{5,... | collective-permute-start | bytes 1179656 | tf_op jit(solution)/shard_map/ppermute | solution.py:51
  44.8 0.0 collective-permute-done.1.k1
  44.8 2.1 %collective-permute-start.8 = (bf16[64,3072]{1,0:T(8,128)(2,1)S(1)}, bf16[64,3072]{1,0:T(8,128)(2,1)S(1)}, u32[]{:S(2)}, u32[]{:S(2)}) collective-permute-start(bf16[64,3072]{1,0:T(8,128)(2,1)S(1)} %bitcast.22), channel_id=1, source_target_pairs={{0,33},{1,0},{32,1},{33,32},{2,35},{3,2},{34,3},{35,34},{4,37},{5,... | collective-permute-start | bytes 1179656 | tf_op jit(solution)/shard_map/ppermute | solution.py:51
  46.9 0.1 add_convert_fusion
  47.0 0.1 fusion
  47.1 0.1 pad_maximum_fusion.1
  47.2 0.0 copy-done.9
  47.2 0.0 copy-start.1
  47.2 1.1 copy-done.1
  48.3 1.1 copy-done.3
  49.4 1.1 copy-done.4
  50.6 1.1 copy-done.5
  51.7 3.1 %shard_map.156 = (bf16[256,1536]{1,0:T(8,128)(2,1)S(1)}, bf16[256,1536]{1,0:T(8,128)(2,1)S(1)}, bf16[256,1536]{1,0:T(8,128)(2,1)S(1)}, bf16[256,1536]{1,0:T(8,128)(2,1)S(1)}) custom-call(s32[12]{0:T(128)S(1)} %copy-done.9, bf16[128,3072]{1,0:T(8,128)(2,1)S(1)} %copy-done.1, bf16[128,3072]{1,0:T(8,128)(2,1)} %collective-permute-done.q1, ...), custom_call_target="tpu_custom_call" | custom-call | tf_op jit(solution)/shard_map/pallas_call | solution.py:281
  54.9 6.8 %collective-permute-done.9.refs_2_ = bf16[64,3072]{1,0:T(8,128)(2,1)S(1)} collective-permute-done((bf16[64,3072]{1,0:T(8,128)(2,1)S(1)}, bf16[64,3072]{1,0:T(8,128)(2,1)S(1)}, u32[]{:S(2)}, u32[]{:S(2)}) %collective-permute-start.9) | collective-permute-done | bytes 393248 | tf_op jit(solution)/shard_map/ppermute | solution.py:51
  61.7 0.9 collective-permute-done.8.refs_1_
  62.5 5.0 %shard_map.159 = (bf16[64,3072]{1,0:T(8,128)(2,1)S(1)}, bf16[64,3072]{1,0:T(8,128)(2,1)}, bf16[64,3072]{1,0:T(8,128)(2,1)}, bf16[64,3072]{1,0:T(8,128)(2,1)}) custom-call(s32[12]{0:T(128)S(1)} %copy-done.9, bf16[256,1536]{1,0:T(8,128)(2,1)S(1)} %get-tuple-element.33.q, bf16[256,1536]{1,0:T(8,128)(2,1)S(1)} %get-tuple-element.34.d, ...), custom_call_target="tpu_custom_call" | custom-call | tf_op jit(solution)/shard_map/pallas_call | solution.py:281
  67.6 0.7 copy-done.6
  68.3 1.6 %collective-permute-start.16 = (bf16[64,3072]{1,0:T(8,128)(2,1)}, bf16[64,3072]{1,0:T(8,128)(2,1)}, u32[]{:S(2)}, u32[]{:S(2)}) collective-permute-start(bf16[64,3072]{1,0:T(8,128)(2,1)} %get-tuple-element.41), channel_id=1, source_target_pairs={{0,1},{1,32},{32,33},{33,0},{2,3},{3,34},{34,35},{35,2},{4,5},{5,3... | collective-permute-start | bytes 1179656 | tf_op jit(solution)/shard_map/ppermute | solution.py:51
  70.0 2.6 %collective-permute-start.17 = (bf16[64,3072]{1,0:T(8,128)(2,1)}, bf16[64,3072]{1,0:T(8,128)(2,1)}, u32[]{:S(2)}, u32[]{:S(2)}) collective-permute-start(bf16[64,3072]{1,0:T(8,128)(2,1)} %get-tuple-element.42), channel_id=1, source_target_pairs={{0,32},{1,33},{32,0},{33,1},{2,34},{3,35},{34,2},{35,3},{4,36},{5,... | collective-permute-start | bytes 1179656 | tf_op jit(solution)/shard_map/ppermute | solution.py:51
  72.6 0.0 collective-permute-start.18
  72.6 4.8 %all-to-all-done.1 = bf16[8,32,3072]{2,1,0:T(8,128)(2,1)S(1)} async-done(((bf16[8,32,3072]{2,1,0:T(8,128)(2,1)}), bf16[8,32,3072]{2,1,0:T(8,128)(2,1)S(1)}, u32[]{:S(2)}, u32[]{:S(2)}) %all-to-all-start.1) | async-done | bytes 1572896 | tf_op jit(solution)/shard_map/all_to_all | solution.py:364
  77.4 2.9 %shard_map.160 = f32[8,24,256]{2,1,0:T(8,128)} custom-call(s32[12]{0:T(128)S(1)} %copy-done.9, bf16[256,1536]{1,0:T(8,128)(2,1)S(1)} %get-tuple-element.44.k, bf16[256,1536]{1,0:T(8,128)(2,1)S(1)} %get-tuple-element.45.v, bf16[256,3072]{1,0:T(8,128)(2,1)S(1)} %bitcast.18), custom_call_target="tpu_custom_call" | custom-call | tf_op jit(solution)/shard_map/pallas_call | solution.py:281
  80.3 4.0 %all-to-all-start.2 = ((f32[8,24,256]{2,1,0:T(8,128)}), f32[8,24,256]{2,1,0:T(8,128)}, u32[]{:S(2)}, u32[]{:S(2)}) async-start(f32[8,24,256]{2,1,0:T(8,128)} %shard_map.160), calls=%async_computation.2 | async-start | bytes 393216 | tf_op jit(solution)/shard_map/all_to_all | solution.py:388
  84.4 5.7 %collective-permute-done.17.p2 = bf16[64,3072]{1,0:T(8,128)(2,1)} collective-permute-done((bf16[64,3072]{1,0:T(8,128)(2,1)}, bf16[64,3072]{1,0:T(8,128)(2,1)}, u32[]{:S(2)}, u32[]{:S(2)}) %collective-permute-start.17) | collective-permute-done | bytes 393248 | tf_op jit(solution)/shard_map/ppermute | solution.py:51
  90.1 1.0 copy-done.7
  91.1 2.7 %shard_map.164 = bf16[64,3072]{1,0:T(8,128)(2,1)} custom-call(s32[12]{0:T(128)S(1)} %copy-done.9, bf16[64,3072]{1,0:T(8,128)(2,1)S(1)} %copy-done.7, bf16[64,3072]{1,0:T(8,128)(2,1)} %collective-permute-done.16.p1, bf16[64,3072]{1,0:T(8,128)(2,1)} %collective-permute-done.17.p2, bf16[64,3072]{1,0:T(8,128)(2,1)} %collective-permute-done.18.p3), custom_call_target="tpu_custom_call" | custom-call | tf_op jit(solution)/shard_map/pallas_call | solution.py:281
  93.8 6.7 %all-to-all-start.3 = ((bf16[8,8,3072]{2,1,0:T(8,128)(2,1)}), bf16[8,8,3072]{2,1,0:T(8,128)(2,1)}, u32[]{:S(2)}, u32[]{:S(2)}) async-start(bf16[8,8,3072]{2,1,0:T(8,128)(2,1)} %bitcast.13), calls=%async_computation.3 | async-start | bytes 786432 | tf_op jit(solution)/shard_map/all_to_all | solution.py:428
  100.5 1.6 %shard_map.161.refs_0_ = f32[24,256]{1,0:T(8,128)S(1)} custom-call(s32[12]{0:T(128)S(1)} %copy-done.9, f32[8,24,256]{2,1,0:T(8,128)} %all-to-all-done.2.refs_0_), custom_call_target="tpu_custom_call" | custom-call | tf_op jit(solution)/shard_map/pallas_call | solution.py:281
  102.1 1.3 %collective-permute-start.13 = (f32[24,256]{1,0:T(8,128)S(1)}, f32[24,256]{1,0:T(8,128)S(1)}, u32[]{:S(2)}, u32[]{:S(2)}) collective-permute-start(f32[24,256]{1,0:T(8,128)S(1)} %shard_map.161.refs_0_), channel_id=1, source_target_pairs={{0,1},{1,32},{32,33},{33,0},{2,3},{3,34},{34,35},{35,2},{4,5},{5,3... | collective-permute-start | bytes 73736 | tf_op jit(solution)/shard_map/ppermute | solution.py:51
  103.3 2.6 %collective-permute-start.12 = (f32[24,256]{1,0:T(8,128)S(1)}, f32[24,256]{1,0:T(8,128)S(1)}, u32[]{:S(2)}, u32[]{:S(2)}) collective-permute-start(f32[24,256]{1,0:T(8,128)S(1)} %shard_map.161.refs_0_), channel_id=1, source_target_pairs={{0,32},{1,33},{32,0},{33,1},{2,34},{3,35},{34,2},{35,3},{4,36},{5,... | collective-permute-start | bytes 73736 | tf_op jit(solution)/shard_map/ppermute | solution.py:51
  106.0 0.1 collective-permute-done.13.refs_3_
  106.1 1.5 %collective-permute-done.12.refs_2_ = f32[24,256]{1,0:T(8,128)S(1)} collective-permute-done((f32[24,256]{1,0:T(8,128)S(1)}, f32[24,256]{1,0:T(8,128)S(1)}, u32[]{:S(2)}, u32[]{:S(2)}) %collective-permute-start.12) | collective-permute-done | bytes 24608 | tf_op jit(solution)/shard_map/ppermute | solution.py:51
  107.5 1.5 %collective-permute-done.11.refs_1_ = f32[24,256]{1,0:T(8,128)S(1)} collective-permute-done((f32[24,256]{1,0:T(8,128)S(1)}, f32[24,256]{1,0:T(8,128)S(1)}, u32[]{:S(2)}, u32[]{:S(2)}) %collective-permute-start.11) | collective-permute-done | bytes 24608 | tf_op jit(solution)/shard_map/ppermute | solution.py:51
  109.0 0.6 shard_map.162.stats
  109.7 0.0 copy-start.11
  109.7 3.8 %shard_map.163 = (bf16[128,3072]{1,0:T(8,128)(2,1)}, bf16[128,1536]{1,0:T(8,128)(2,1)S(1)}, bf16[128,3072]{1,0:T(8,128)(2,1)}, bf16[128,1536]{1,0:T(8,128)(2,1)}) custom-call(s32[12]{0:T(128)S(1)} %copy-done.9, bf16[256,1536]{1,0:T(8,128)(2,1)S(1)} %get-tuple-element.44.k, bf16[256,1536]{1,0:T(8,128)(2,1)S(1)} %get-tuple-element.45.v, ...), custom_call_target="tpu_custom_call" | custom-call | tf_op jit(solution)/shard_map/pallas_call | solution.py:281
  113.5 2.1 %collective-permute-start.15 = (bf16[128,1536]{1,0:T(8,128)(2,1)}, bf16[128,1536]{1,0:T(8,128)(2,1)S(1)}, u32[]{:S(2)}, u32[]{:S(2)}) collective-permute-start(bf16[128,1536]{1,0:T(8,128)(2,1)} %get-tuple-element.48), channel_id=1, source_target_pairs={{0,2},{2,0},{1,3},{3,1},{4,6},{6,4},{5,7},{7,5},{8,10},{10,8},{9,1... | collective-permute-start | bytes 1179656 | tf_op jit(solution)/shard_map/ppermute | solution.py:51
  115.6 1.1 convert_reduce_fusion.total
  116.7 0.8 collective-permute-start.19
  117.4 0.9 collective-permute-done.19.other
  118.3 1.2 %shard_map.165 = (bf16[4,3072]{1,0:T(4,128)(2,1)}, bf16[4,3072]{1,0:T(4,128)(2,1)}) custom-call(s32[12]{0:T(128)S(1)} %copy-done.9, f32[8,3072]{1,0:T(8,128)S(1)} %convert_reduce_fusion.total, f32[4,3072]{1,0:T(4,128)S(1)} %collective-permute-done.19.other, f32[1,128]{1,0:T(1,128)S(1)} %copy-done.11), custom_call_target="tpu_custom_call" | custom-call | tf_op jit(solution)/shard_map/pallas_call | solution.py:281
  119.6 1.6 %shard_map.166 = (bf16[128,3072]{1,0:T(8,128)(2,1)}, bf16[128,3072]{1,0:T(8,128)(2,1)}) custom-call(s32[12]{0:T(128)S(1)} %copy-done.9, bf16[128,1536]{1,0:T(8,128)(2,1)S(1)} %collective-permute-done.14.k1, bf16[128,1536]{1,0:T(8,128)(2,1)S(1)} %collective-permute-done.15.v1, ...), custom_call_target="tpu_custom_call", output_to_operand_aliasing={{0}: (3, {}), {1}: (4, {})} | custom-call | tf_op jit(solution)/shard_map/pallas_call | solution.py:281
  (28 shorter events, 0.1 us)
Async XLA Ops:
  5.5 4.3 %collective-permute-start.4 = (bf16[4,6144]{1,0:T(4,128)(2,1)}, bf16[4,6144]{1,0:T(4,128)(2,1)S(1)}, u32[]{:S(2)}, u32[]{:S(2)}) collective-permute-start(bf16[4,6144]{1,0:T(4,128)(2,1)} %get-tuple-element.36), channel_id=1, source_target_pairs={{0,2},{2,0},{1,3},{3,1},{4,6},{6,4},{5,7},{7,5},{8,10},{10,8},{9,1... | collective-permute-start | bytes 147464 | tf_op jit(solution)/shard_map/ppermute | solution.py:51
  9.8 0.7 copy-start.8
  10.5 0.8 copy-start.10
  12.6 21.6 %all-to-all-start = ((bf16[8,8,3072]{2,1,0:T(8,128)(2,1)}), bf16[8,8,3072]{2,1,0:T(8,128)(2,1)S(1)}, u32[]{:S(2)}, u32[]{:S(2)}) async-start(bf16[8,8,3072]{2,1,0:T(8,128)(2,1)} %bitcast.9), calls=%async_computation | async-start | bytes 786432 | tf_op jit(solution)/shard_map/all_to_all | solution.py:327
  19.0 5.0 %collective-permute-start.7 = (bf16[8,3072]{1,0:T(8,128)(2,1)S(1)}, bf16[8,3072]{1,0:T(8,128)(2,1)S(1)}, u32[]{:S(2)}, u32[]{:S(2)}) collective-permute-start(bf16[8,3072]{1,0:T(8,128)(2,1)S(1)} %get-tuple-element.37), channel_id=1, source_target_pairs={{0,1},{1,32},{32,33},{33,0},{2,3},{3,34},{34,35},{35,2},{4,5},{5,3... | collective-permute-start | bytes 147464 | tf_op jit(solution)/shard_map/ppermute | solution.py:51
  20.3 4.6 %collective-permute-start.6 = (bf16[8,3072]{1,0:T(8,128)(2,1)S(1)}, bf16[8,3072]{1,0:T(8,128)(2,1)S(1)}, u32[]{:S(2)}, u32[]{:S(2)}) collective-permute-start(bf16[8,3072]{1,0:T(8,128)(2,1)S(1)} %get-tuple-element.37), channel_id=1, source_target_pairs={{0,32},{1,33},{32,0},{33,1},{2,34},{3,35},{34,2},{35,3},{4,36},{5,... | collective-permute-start | bytes 147464 | tf_op jit(solution)/shard_map/ppermute | solution.py:51
  22.9 3.2 %collective-permute-start.5 = (bf16[8,3072]{1,0:T(8,128)(2,1)S(1)}, bf16[8,3072]{1,0:T(8,128)(2,1)S(1)}, u32[]{:S(2)}, u32[]{:S(2)}) collective-permute-start(bf16[8,3072]{1,0:T(8,128)(2,1)S(1)} %get-tuple-element.37), channel_id=1, source_target_pairs={{0,33},{1,0},{32,1},{33,32},{2,35},{3,2},{34,3},{35,34},{4,37},{5,... | collective-permute-start | bytes 147464 | tf_op jit(solution)/shard_map/ppermute | solution.py:51
  35.5 3.7 %copy-start = (bf16[128,3072]{1,0:T(8,128)(2,1)S(1)}, bf16[128,3072]{1,0:T(8,128)(2,1)}, u32[]{:S(2)}) copy-start(bf16[128,3072]{1,0:T(8,128)(2,1)} %q0.1) | copy-start | bytes 2359300
  35.5 4.3 %copy-start.2 = (bf16[128,3072]{1,0:T(8,128)(2,1)S(1)}, bf16[128,3072]{1,0:T(8,128)(2,1)}, u32[]{:S(2)}) copy-start(bf16[128,3072]{1,0:T(8,128)(2,1)} %k0.1) | copy-start | bytes 2359300
  35.5 11.6 %copy-start.9 = (s32[12]{0:T(128)S(1)}, s32[12]{0:T(128)}, u32[]{:S(2)}) copy-start(s32[12]{0:T(128)} %stack.36.sc) | copy-start | bytes 148
  35.5 41.9 %all-to-all-start.1 = ((bf16[8,32,3072]{2,1,0:T(8,128)(2,1)}), bf16[8,32,3072]{2,1,0:T(8,128)(2,1)S(1)}, u32[]{:S(2)}, u32[]{:S(2)}) async-start(bf16[8,32,3072]{2,1,0:T(8,128)(2,1)} %broadcast_in_dim.2), calls=%async_computation.1 | async-start | bytes 3145728 | tf_op jit(solution)/shard_map/all_to_all | solution.py:364
  39.3 2.6 %collective-permute-start = (bf16[128,3072]{1,0:T(8,128)(2,1)S(1)}, bf16[128,3072]{1,0:T(8,128)(2,1)}, u32[]{:S(2)}, u32[]{:S(2)}) collective-permute-start(bf16[128,3072]{1,0:T(8,128)(2,1)S(1)} %copy-done), channel_id=1, source_target_pairs={{0,2},{2,0},{1,3},{3,1},{4,6},{6,4},{5,7},{7,5},{8,10},{10,8},{9,1... | collective-permute-start | bytes 2359304 | tf_op jit(solution)/shard_map/ppermute | solution.py:51
  39.9 5.0 %collective-permute-start.1 = (bf16[128,3072]{1,0:T(8,128)(2,1)S(1)}, bf16[128,3072]{1,0:T(8,128)(2,1)}, u32[]{:S(2)}, u32[]{:S(2)}) collective-permute-start(bf16[128,3072]{1,0:T(8,128)(2,1)S(1)} %copy-done.2), channel_id=1, source_target_pairs={{0,2},{2,0},{1,3},{3,1},{4,6},{6,4},{5,7},{7,5},{8,10},{10,8},{9,1... | collective-permute-start | bytes 2359304 | tf_op jit(solution)/shard_map/ppermute | solution.py:51
  40.0 7.2 %collective-permute-start.2 = (bf16[128,3072]{1,0:T(8,128)(2,1)}, bf16[128,3072]{1,0:T(8,128)(2,1)}, u32[]{:S(2)}, u32[]{:S(2)}) collective-permute-start(bf16[128,3072]{1,0:T(8,128)(2,1)} %v0.1), channel_id=1, source_target_pairs={{0,2},{2,0},{1,3},{3,1},{4,6},{6,4},{5,7},{7,5},{8,10},{10,8},{9,1... | collective-permute-start | bytes 2359304 | tf_op jit(solution)/shard_map/ppermute | solution.py:51
  40.4 6.8 %collective-permute-start.3 = (bf16[128,3072]{1,0:T(8,128)(2,1)}, bf16[128,3072]{1,0:T(8,128)(2,1)}, u32[]{:S(2)}, u32[]{:S(2)}) collective-permute-start(bf16[128,3072]{1,0:T(8,128)(2,1)} %d0.1), channel_id=1, source_target_pairs={{0,2},{2,0},{1,3},{3,1},{4,6},{6,4},{5,7},{7,5},{8,10},{10,8},{9,1... | collective-permute-start | bytes 2359304 | tf_op jit(solution)/shard_map/ppermute | solution.py:51
  40.5 14.4 %collective-permute-start.10 = (bf16[64,3072]{1,0:T(8,128)(2,1)S(1)}, bf16[64,3072]{1,0:T(8,128)(2,1)S(1)}, u32[]{:S(2)}, u32[]{:S(2)}) collective-permute-start(bf16[64,3072]{1,0:T(8,128)(2,1)S(1)} %bitcast.20), channel_id=1, source_target_pairs={{0,1},{1,32},{32,33},{33,0},{2,3},{3,34},{34,35},{35,2},{4,5},{5,3... | collective-permute-start | bytes 1179656 | tf_op jit(solution)/shard_map/ppermute | solution.py:51
  41.9 19.8 %collective-permute-start.9 = (bf16[64,3072]{1,0:T(8,128)(2,1)S(1)}, bf16[64,3072]{1,0:T(8,128)(2,1)S(1)}, u32[]{:S(2)}, u32[]{:S(2)}) collective-permute-start(bf16[64,3072]{1,0:T(8,128)(2,1)S(1)} %bitcast.21), channel_id=1, source_target_pairs={{0,32},{1,33},{32,0},{33,1},{2,34},{3,35},{34,2},{35,3},{4,36},{5,... | collective-permute-start | bytes 1179656 | tf_op jit(solution)/shard_map/ppermute | solution.py:51
  44.8 17.7 %collective-permute-start.8 = (bf16[64,3072]{1,0:T(8,128)(2,1)S(1)}, bf16[64,3072]{1,0:T(8,128)(2,1)S(1)}, u32[]{:S(2)}, u32[]{:S(2)}) collective-permute-start(bf16[64,3072]{1,0:T(8,128)(2,1)S(1)} %bitcast.22), channel_id=1, source_target_pairs={{0,33},{1,0},{32,1},{33,32},{2,35},{3,2},{34,3},{35,34},{4,37},{5,... | collective-permute-start | bytes 1179656 | tf_op jit(solution)/shard_map/ppermute | solution.py:51
  47.2 1.1 copy-start.1
  48.3 1.1 copy-start.3
  49.4 1.1 copy-start.4
  50.6 1.1 copy-start.5
  67.6 0.8 copy-start.6
  68.3 16.0 %collective-permute-start.16 = (bf16[64,3072]{1,0:T(8,128)(2,1)}, bf16[64,3072]{1,0:T(8,128)(2,1)}, u32[]{:S(2)}, u32[]{:S(2)}) collective-permute-start(bf16[64,3072]{1,0:T(8,128)(2,1)} %get-tuple-element.41), channel_id=1, source_target_pairs={{0,1},{1,32},{32,33},{33,0},{2,3},{3,34},{34,35},{35,2},{4,5},{5,3... | collective-permute-start | bytes 1179656 | tf_op jit(solution)/shard_map/ppermute | solution.py:51
  70.0 20.1 %collective-permute-start.17 = (bf16[64,3072]{1,0:T(8,128)(2,1)}, bf16[64,3072]{1,0:T(8,128)(2,1)}, u32[]{:S(2)}, u32[]{:S(2)}) collective-permute-start(bf16[64,3072]{1,0:T(8,128)(2,1)} %get-tuple-element.42), channel_id=1, source_target_pairs={{0,32},{1,33},{32,0},{33,1},{2,34},{3,35},{34,2},{35,3},{4,36},{5,... | collective-permute-start | bytes 1179656 | tf_op jit(solution)/shard_map/ppermute | solution.py:51
  72.6 17.5 %collective-permute-start.18 = (bf16[64,3072]{1,0:T(8,128)(2,1)}, bf16[64,3072]{1,0:T(8,128)(2,1)}, u32[]{:S(2)}, u32[]{:S(2)}) collective-permute-start(bf16[64,3072]{1,0:T(8,128)(2,1)} %get-tuple-element.43), channel_id=1, source_target_pairs={{0,33},{1,0},{32,1},{33,32},{2,35},{3,2},{34,3},{35,34},{4,37},{5,... | collective-permute-start | bytes 1179656 | tf_op jit(solution)/shard_map/ppermute | solution.py:51
  80.3 13.4 %all-to-all-start.2 = ((f32[8,24,256]{2,1,0:T(8,128)}), f32[8,24,256]{2,1,0:T(8,128)}, u32[]{:S(2)}, u32[]{:S(2)}) async-start(f32[8,24,256]{2,1,0:T(8,128)} %shard_map.160), calls=%async_computation.2 | async-start | bytes 393216 | tf_op jit(solution)/shard_map/all_to_all | solution.py:388
  90.1 1.0 copy-start.7
  93.8 21.8 %all-to-all-start.3 = ((bf16[8,8,3072]{2,1,0:T(8,128)(2,1)}), bf16[8,8,3072]{2,1,0:T(8,128)(2,1)}, u32[]{:S(2)}, u32[]{:S(2)}) async-start(bf16[8,8,3072]{2,1,0:T(8,128)(2,1)} %bitcast.13), calls=%async_computation.3 | async-start | bytes 786432 | tf_op jit(solution)/shard_map/all_to_all | solution.py:428
  102.1 4.0 %collective-permute-start.13 = (f32[24,256]{1,0:T(8,128)S(1)}, f32[24,256]{1,0:T(8,128)S(1)}, u32[]{:S(2)}, u32[]{:S(2)}) collective-permute-start(f32[24,256]{1,0:T(8,128)S(1)} %shard_map.161.refs_0_), channel_id=1, source_target_pairs={{0,1},{1,32},{32,33},{33,0},{2,3},{3,34},{34,35},{35,2},{4,5},{5,3... | collective-permute-start | bytes 73736 | tf_op jit(solution)/shard_map/ppermute | solution.py:51
  103.3 4.2 %collective-permute-start.12 = (f32[24,256]{1,0:T(8,128)S(1)}, f32[24,256]{1,0:T(8,128)S(1)}, u32[]{:S(2)}, u32[]{:S(2)}) collective-permute-start(f32[24,256]{1,0:T(8,128)S(1)} %shard_map.161.refs_0_), channel_id=1, source_target_pairs={{0,32},{1,33},{32,0},{33,1},{2,34},{3,35},{34,2},{35,3},{4,36},{5,... | collective-permute-start | bytes 73736 | tf_op jit(solution)/shard_map/ppermute | solution.py:51
  106.0 3.1 %collective-permute-start.11 = (f32[24,256]{1,0:T(8,128)S(1)}, f32[24,256]{1,0:T(8,128)S(1)}, u32[]{:S(2)}, u32[]{:S(2)}) collective-permute-start(f32[24,256]{1,0:T(8,128)S(1)} %shard_map.161.refs_0_), channel_id=1, source_target_pairs={{0,33},{1,0},{32,1},{33,32},{2,35},{3,2},{34,3},{35,34},{4,37},{5,... | collective-permute-start | bytes 73736 | tf_op jit(solution)/shard_map/ppermute | solution.py:51
  109.7 8.6 %copy-start.11 = (f32[1,128]{1,0:T(1,128)S(1)}, f32[1,128]{1,0:T(1,128)}, u32[]{:S(2)}) copy-start(f32[1,128]{1,0:T(1,128)} %constant.55.clone.freq) | copy-start | bytes 1540
  113.5 6.1 %collective-permute-start.15 = (bf16[128,1536]{1,0:T(8,128)(2,1)}, bf16[128,1536]{1,0:T(8,128)(2,1)S(1)}, u32[]{:S(2)}, u32[]{:S(2)}) collective-permute-start(bf16[128,1536]{1,0:T(8,128)(2,1)} %get-tuple-element.48), channel_id=1, source_target_pairs={{0,2},{2,0},{1,3},{3,1},{4,6},{6,4},{5,7},{7,5},{8,10},{10,8},{9,1... | collective-permute-start | bytes 1179656 | tf_op jit(solution)/shard_map/ppermute | solution.py:51
  115.6 4.0 %collective-permute-start.14 = (bf16[128,1536]{1,0:T(8,128)(2,1)S(1)}, bf16[128,1536]{1,0:T(8,128)(2,1)S(1)}, u32[]{:S(2)}, u32[]{:S(2)}) collective-permute-start(bf16[128,1536]{1,0:T(8,128)(2,1)S(1)} %get-tuple-element.47), channel_id=1, source_target_pairs={{0,2},{2,0},{1,3},{3,1},{4,6},{6,4},{5,7},{7,5},{8,10},{10,8},{9,1... | collective-permute-start | bytes 1179656 | tf_op jit(solution)/shard_map/ppermute | solution.py:51
  116.7 1.6 %collective-permute-start.19 = (f32[4,3072]{1,0:T(4,128)S(1)}, f32[4,3072]{1,0:T(4,128)S(1)}, u32[]{:S(2)}, u32[]{:S(2)}) collective-permute-start(f32[4,3072]{1,0:T(4,128)S(1)} %slice.5), channel_id=1, source_target_pairs={{0,2},{2,0},{1,3},{3,1},{4,6},{6,4},{5,7},{7,5},{8,10},{10,8},{9,1... | collective-permute-start | bytes 147464 | tf_op jit(solution)/shard_map/ppermute | solution.py:51

commit v5 on v4

--- a/solution.py
+++ b/solution.py
@@ -174,7 +174,8 @@
     return jnp.where(row < VT, sc[4] + row, sc[5] + row - VT)
 
 
-def statistics_kernel(sc, k, v, qd, copies, out):
+def statistics_kernel(sc, k, v, *refs):
+    *blocks, copies, out = refs
     g = pl.program_id(0)
     row = lax.broadcasted_iota(jnp.int32, (2 * VT, HD), 0)
     bias = jnp.where(video_token(sc, row) < sc[3], 0.0, NEG)
@@ -182,7 +183,9 @@
     some = jnp.minimum(sc[4], sc[5]) < sc[3]
 
     def scores(i):
-        return nt(k[:, head(i)], qd[:, head(i)]), nt(v[:, head(i)], qd[:, head(HPG + i)])
+        query = jnp.concatenate([a[:, head(i)] for a in blocks], 0)
+        grad = jnp.concatenate([a[:, head(HPG + i)] for a in blocks], 0)
+        return nt(k[:, head(i)], query), nt(v[:, head(i)], grad)
 
     def sums(i, s, dp):
         s = s * (SCALE * LOG2E) + bias
@@ -197,8 +200,9 @@
 
     @pl.when(g == GROUPS - 1)
     def _():
+        stats = pltpu.roll(out[...], sc[6] * YR, 1)
         for n in range(NZ):
-            copies[n] = out[...]
+            copies[n] = stats
 
 
 def merge(lses, deltas):
@@ -224,16 +228,19 @@
     else:
         a = pltpu.roll(both, lax.rem(AUDIO - sc[1] * CR, AUDIO), 1)
         b = pltpu.roll(both, YR - sc[1] * CR, 1)
-        out[...] = jnp.where(place < NY - sc[1], a, b)
-
-
-def audio_to_video_kernel(sc, k, v, stats, cos, sin, qd, dk0, dk1, dv0, dv1):
+        both = jnp.where(place < NY - sc[1], a, b)
+        out[...] = pltpu.roll(both, lax.rem(AUDIO - sc[6] * YR, AUDIO), 1)
+
+
+def audio_to_video_kernel(sc, k, v, stats, cos, sin, *refs):
+    *blocks, dk0, dk1, dv0, dv1 = refs
     g = pl.program_id(0)
     row = lax.broadcasted_iota(jnp.int32, (2 * VT, HD), 0)
     valid = video_token(sc, row) < sc[3]
 
     def scores(i):
-        query, grad = qd[:, head(i)], qd[:, head(HPG + i)]
+        query = jnp.concatenate([a[:, head(i)] for a in blocks], 0)
+        grad = jnp.concatenate([a[:, head(HPG + i)] for a in blocks], 0)
         return query, grad, nt(k[:, head(i)], query), nt(v[:, head(i)], grad)
 
     def gradients(i, query, grad, s, dp):
@@ -336,7 +343,6 @@
     half = pl.BlockSpec((VT, GW), lambda g, sc: (0, sc[0] * GROUPS + g))
     table = pl.BlockSpec((2, HD), lambda g, sc: (0, 0))
     video_in = pl.BlockSpec((2 * VT, GW), lambda g, sc: (0, g))
-    all_in = pl.BlockSpec((AUDIO, 2 * GW), lambda g, sc: (0, g))
     audio_in = pl.BlockSpec((ZR, 2 * GW), lambda g, sc: (0, g))
     video = pl.BlockSpec((2 * VT, GW), lambda g, sc: (0, g))
     audio = pl.BlockSpec((ZR, 2 * GW), lambda g, sc: (0, g))
@@ -355,14 +361,22 @@
         [half] * 8 + [table] * 2,
         [video_shape] * 4,
         [video] * 4,
-    )
-
-
+        limit=56,
+    )
+
+
+    qd, qr, kr, vr, dr = lax.optimization_barrier((qd, qr, kr, vr, dr))
     home = jnp.concatenate(along_y(qd), 0)
-    copies = jnp.broadcast_to(home[None], (NZ,) + home.shape).reshape(AUDIO, 2 * CW)
-    copies, kv_z = lax.optimization_barrier((copies, kv_z))
-    qd_all = lax.all_to_all(copies, "z", split_axis=0, concat_axis=0, tiled=True)
+    home, kv_z = lax.optimization_barrier((home, kv_z))
     kv_all = along_y(kv_z)
+    up, down = [home], [home]
+    for _ in range(3):
+        up.append(shift(up[-1], "z", NZ, NZ - 1))
+        down.append(shift(down[-1], "z", NZ, 1))
+    up[3], down[3], *kv_all = lax.optimization_barrier((up[3], down[3], *kv_all))
+    far = [shift(up[-1][: YR // 2], "z", NZ, NZ - 1), shift(down[-1][YR // 2 :], "z", NZ, 1)]
+    qd_all = up + far + down[:0:-1]
+    ring_in = [pl.BlockSpec((x.shape[0], 2 * GW), lambda g, sc: (0, g)) for x in qd_all]
 
     parts = call(
         video_to_audio_kernel,
@@ -379,8 +393,8 @@
     copies = call(
         statistics_kernel,
         scalars,
-        (kr, vr, qd_all),
-        [video_in] * 2 + [all_in],
+        (kr, vr, *qd_all),
+        [video_in] * 2 + ring_in,
         jax.ShapeDtypeStruct((NZ, 2 * HEADS, AUDIO), f32),
         every,
         scratch=[pltpu.VMEM((2 * HEADS, AUDIO), f32)],
@@ -417,8 +431,8 @@
     dk0, dk1, dv0, dv1 = call(
         audio_to_video_kernel,
         scalars,
-        (kr, vr, stats, cos, sin, qd_all),
-        [video_in] * 2 + [rows] + [table] * 2 + [all_in],
+        (kr, vr, stats, cos, sin, *qd_all),
+        [video_in] * 2 + [rows] + [table] * 2 + ring_in,
         [full_shape, mine_shape] * 2,
         [half, mine] * 2,
     )
@@ -439,7 +453,6 @@
         grid=(1,),
         limit=16,
     )
-    dk1, dv1, dk_audio, dv_audio = lax.optimization_barrier((dk1, dv1, dk_audio, dv_audio))
     place = pl.BlockSpec(memory_space=pl.ANY)
     other = pl.BlockSpec((VT, GW), lambda g, sc: (0, (1 - sc[0]) * GROUPS + g))
     dk_video, dv_video = call(

time: 122 us -> 119 us (0.975)
  waiting for transfers between devices: 33.5 us -> 26.2 us
  starting transfers between devices: 47.6 us -> 54.3 us
  local copies, waits for them, and re-layouts: 10.4 us -> 6.75 us
    ppermute x20 -> x28, starting transfers between devices: 26.7 us -> 37.1 us  [shift(): return lax.ppermute(x, axis, [(i, (i + step) % size) for i in range(size)])]
    all_to_all x1, waiting for transfers between devices: 7.98 us -> 1.35 us  [local(): kv_z = lax.all_to_all(copies, 'z', split_axis=0, concat_axis=0, tiled=True)]
    all_to_all x1 -> x0, waiting for transfers between devices: 4.83 us -> none  [local(): lax.all_to_all(copies, 'z', split_axis=0, concat_axis=0, tiled=True)]
    ppermute x20 -> x28, waiting for transfers between devices: 20.7 us -> 24.9 us  [shift(): return lax.ppermute(x, axis, [(i, (i + step) % size) for i in range(size)])]
    all_to_all x1 -> x0, starting transfers between devices: 3.71 us -> none  [local(): lax.all_to_all(copies, 'z', split_axis=0, concat_axis=0, tiled=True)]
    unnamed x24 -> x32, local copies, waits for them, and re-layouts: 7.76 us -> 6.09 us
    all_to_all x1, starting transfers between devices: 6.74 us -> 5.38 us  [local(): sums = lax.all_to_all(sums, 'z', split_axis=0, concat_axis=0, tiled=True)]
    broadcast_in_dim x1 -> x0, local copies, waits for them, and re-layouts: 1.36 us -> none  [local(): jnp.broadcast_to(home[None], (NZ,) + home.shape).reshape(AUDIO, 2 * CW)]
  transfers between devices with their start and end apart: 24 -> 31, of which waited for: 13 -> 10; matrix products, arithmetic and copies ran while one was open for 1% -> 2% of each run, Pallas kernels for 17% -> 22%
where the time goes in v5:
time: 119 us; the launch traced here: 118 us
  starting transfers between devices  54.3 us (46%)
  Pallas kernels  26.7 us (22%)
  waiting for transfers between devices  26.2 us (22%)
  local copies, waits for them, and re-layouts  6.75 us (6%)
  between operations  2.13 us (2%)
  other arithmetic  1.92 us (2%)
    ppermute x28, starting transfers between devices, shift(): return lax.ppermute(x, axis, [(i, (i + step) % size) for i in range(size)])  37.1 us
    pallas_call x11, Pallas kernels, call(): pl.pallas_call(kernel, grid_spec=pltpu.PrefetchScalarGridSpec(num_scalar_...  26.7 us
    ppermute x28, waiting for transfers between devices, shift(): return lax.ppermute(x, axis, [(i, (i + step) % size) for i in range(size)])  24.9 us
    all_to_all x1, starting transfers between devices, local(): kv_z = lax.all_to_all(copies, 'z', split_axis=0, concat_axis=0, tiled=True)  6.45 us
    unnamed x32, local copies, waits for them, and re-layouts  6.09 us
    all_to_all x1, starting transfers between devices, local(): sums = lax.all_to_all(sums, 'z', split_axis=0, concat_axis=0, tiled=True)  5.38 us
    all_to_all x1, starting transfers between devices, local(): stats = lax.all_to_all(copies, 'z', split_axis=0, concat_axis=0, tiled=True)  5.36 us
  transfers between devices with their start and end apart: 31, of which 10 were waited for; matrix products, arithmetic and copies ran while one was open for 2% of the time, Pallas kernels for 22%

profile of v5, /device:TPU:1, one launch (start us, length us, event | category | flops | bytes accessed | tf_op | source)
XLA Modules:
  0.0 118.0 jit_solution(3965187957071155393)
XLA Ops:
  0.6 3.3 %collective-permute-start.1 = (bf16[128,3072]{1,0:T(8,128)(2,1)}, bf16[128,3072]{1,0:T(8,128)(2,1)S(1)}, u32[]{:S(2)}, u32[]{:S(2)}) collective-permute-start(bf16[128,3072]{1,0:T(8,128)(2,1)} %q0.1), channel_id=1, source_target_pairs={{0,2},{2,0},{1,3},{3,1},{4,6},{6,4},{5,7},{7,5},{8,10},{10,8},{9,1... | collective-permute-start | bytes 2359304 | tf_op jit(solution)/shard_map/ppermute | solution.py:51
  4.0 0.1 collective-permute-start.2
  4.1 0.4 collective-permute-start.3
  4.5 0.1 collective-permute-start.4
  5.9 0.6 copy-done.15
  6.5 0.6 stack.36.sc
  7.2 2.2 %shard_map.156 = (bf16[4,6144]{1,0:T(4,128)(2,1)}, bf16[4,6144]{1,0:T(4,128)(2,1)}) custom-call(s32[12]{0:T(128)} %stack.36.sc, bf16[4,3072]{1,0:T(4,128)(2,1)} %q.1, bf16[4,3072]{1,0:T(4,128)(2,1)} %k.1, bf16[4,3072]{1,0:T(4,128)(2,1)} %v.1, bf16[4,3072]{1,0:T(4,128)(2,1)} %d.1, f32[1,128]{1,0:T(1,128)} %constant.55.clone.freq), custom_call_target="tpu_custom_call" | custom-call | tf_op jit(solution)/shard_map/pallas_call | solution.py:288
  9.4 0.4 collective-permute-start
  9.8 0.1 add_convert_fusion
  9.9 1.0 collective-permute-done.got
  10.9 1.3 %shard_map.157 = (bf16[8,3072]{1,0:T(8,128)(2,1)S(1)}, bf16[64,3072]{1,0:T(8,128)(2,1)}) custom-call(s32[12]{0:T(128)S(1)} %copy-done.6, bf16[4,6144]{1,0:T(4,128)(2,1)S(1)} %copy-done.8, bf16[4,6144]{1,0:T(4,128)(2,1)S(1)} %collective-permute-done.got), custom_call_target="tpu_custom_call" | custom-call | tf_op jit(solution)/shard_map/pallas_call | solution.py:288
  12.2 6.5 %all-to-all-start = ((bf16[8,8,3072]{2,1,0:T(8,128)(2,1)}), bf16[8,8,3072]{2,1,0:T(8,128)(2,1)S(1)}, u32[]{:S(2)}, u32[]{:S(2)}) async-start(bf16[8,8,3072]{2,1,0:T(8,128)(2,1)} %bitcast.8), calls=%async_computation | async-start | bytes 786432 | tf_op jit(solution)/shard_map/all_to_all | solution.py:334
  18.6 0.1 fusion
  18.8 0.6 pad_maximum_fusion.1
  19.4 0.0 copy-start.13
  19.5 0.8 copy-done.12
  20.3 0.3 copy-done.13
  20.5 0.3 copy-done.14
  20.9 4.3 %shard_map.158 = (bf16[256,1536]{1,0:T(8,128)(2,1)}, bf16[256,1536]{1,0:T(8,128)(2,1)}, bf16[256,1536]{1,0:T(8,128)(2,1)}, bf16[256,1536]{1,0:T(8,128)(2,1)}) custom-call(s32[12]{0:T(128)} %stack.36.sc, bf16[128,3072]{1,0:T(8,128)(2,1)} %q0.1, bf16[128,3072]{1,0:T(8,128)(2,1)} %copy-done.12, bf16[128,3072]{1,0:T(8,128)(2,1)} %k0.1, ...), custom_call_target="tpu_custom_call" | custom-call | tf_op jit(solution)/shard_map/pallas_call | solution.py:288
  25.2 1.4 %collective-permute-start.7 = (bf16[8,3072]{1,0:T(8,128)(2,1)S(1)}, bf16[8,3072]{1,0:T(8,128)(2,1)S(1)}, u32[]{:S(2)}, u32[]{:S(2)}) collective-permute-start(bf16[8,3072]{1,0:T(8,128)(2,1)S(1)} %get-tuple-element.49), channel_id=1, source_target_pairs={{0,1},{1,32},{32,33},{33,0},{2,3},{3,34},{34,35},{35,2},{4,5},{5,3... | collective-permute-start | bytes 147464 | tf_op jit(solution)/shard_map/ppermute | solution.py:51
  26.6 2.6 %collective-permute-start.6 = (bf16[8,3072]{1,0:T(8,128)(2,1)S(1)}, bf16[8,3072]{1,0:T(8,128)(2,1)S(1)}, u32[]{:S(2)}, u32[]{:S(2)}) collective-permute-start(bf16[8,3072]{1,0:T(8,128)(2,1)S(1)} %get-tuple-element.49), channel_id=1, source_target_pairs={{0,32},{1,33},{32,0},{33,1},{2,34},{3,35},{34,2},{35,3},{4,36},{5,... | collective-permute-start | bytes 147464 | tf_op jit(solution)/shard_map/ppermute | solution.py:51
  29.2 1.1 collective-permute-start.5
  30.3 0.9 collective-permute-done.6
  31.2 1.2 %collective-permute-done.5 = bf16[8,3072]{1,0:T(8,128)(2,1)S(1)} collective-permute-done((bf16[8,3072]{1,0:T(8,128)(2,1)S(1)}, bf16[8,3072]{1,0:T(8,128)(2,1)S(1)}, u32[]{:S(2)}, u32[]{:S(2)}) %collective-permute-start.5) | collective-permute-done | bytes 49184 | tf_op jit(solution)/shard_map/ppermute | solution.py:51
  32.4 1.3 %all-to-all-done = bf16[8,8,3072]{2,1,0:T(8,128)(2,1)S(1)} async-done(((bf16[8,8,3072]{2,1,0:T(8,128)(2,1)}), bf16[8,8,3072]{2,1,0:T(8,128)(2,1)S(1)}, u32[]{:S(2)}, u32[]{:S(2)}) %all-to-all-start) | async-done | bytes 393248 | tf_op jit(solution)/shard_map/all_to_all | solution.py:334
  33.8 0.2 collective-permute-start.11
  34.0 2.4 %collective-permute-start.8 = (bf16[32,3072]{1,0:T(8,128)(2,1)S(1)}, bf16[32,3072]{1,0:T(8,128)(2,1)S(1)}, u32[]{:S(2)}, u32[]{:S(2)}) collective-permute-start(bf16[32,3072]{1,0:T(8,128)(2,1)S(1)} %pad_maximum_fusion.refs_0_), channel_id=1, source_target_pairs={{0,28},{4,0},{8,4},{12,8},{16,12},{20,16},{24,20},{28,24},{1,29},{... | collective-permute-start | bytes 589832 | tf_op jit(solution)/shard_map/ppermute | solution.py:51
  36.5 1.3 %collective-permute-start.16 = (bf16[64,3072]{1,0:T(8,128)(2,1)S(1)}, bf16[64,3072]{1,0:T(8,128)(2,1)S(1)}, u32[]{:S(2)}, u32[]{:S(2)}) collective-permute-start(bf16[64,3072]{1,0:T(8,128)(2,1)S(1)} %bitcast.15), channel_id=1, source_target_pairs={{0,1},{1,32},{32,33},{33,0},{2,3},{3,34},{34,35},{35,2},{4,5},{5,3... | collective-permute-start | bytes 1179656 | tf_op jit(solution)/shard_map/ppermute | solution.py:51
  37.8 2.6 %collective-permute-start.15 = (bf16[64,3072]{1,0:T(8,128)(2,1)S(1)}, bf16[64,3072]{1,0:T(8,128)(2,1)S(1)}, u32[]{:S(2)}, u32[]{:S(2)}) collective-permute-start(bf16[64,3072]{1,0:T(8,128)(2,1)S(1)} %bitcast.16), channel_id=1, source_target_pairs={{0,32},{1,33},{32,0},{33,1},{2,34},{3,35},{34,2},{35,3},{4,36},{5,... | collective-permute-start | bytes 1179656 | tf_op jit(solution)/shard_map/ppermute | solution.py:51
  40.4 1.1 collective-permute-start.14
  41.5 2.7 %collective-permute-start.9 = (bf16[32,3072]{1,0:T(8,128)(2,1)S(1)}, bf16[32,3072]{1,0:T(8,128)(2,1)S(1)}, u32[]{:S(2)}, u32[]{:S(2)}) collective-permute-start(bf16[32,3072]{1,0:T(8,128)(2,1)S(1)} %collective-permute-done.8.refs_1_), channel_id=1, source_target_pairs={{0,28},{4,0},{8,4},{12,8},{16,12},{20,16},{24,20},{28,24},{1,29},{... | collective-permute-start | bytes 589832 | tf_op jit(solution)/shard_map/ppermute | solution.py:51
  44.1 3.3 %collective-permute-done.12.refs_7_ = bf16[32,3072]{1,0:T(8,128)(2,1)S(1)} collective-permute-done((bf16[32,3072]{1,0:T(8,128)(2,1)S(1)}, bf16[32,3072]{1,0:T(8,128)(2,1)S(1)}, u32[]{:S(2)}, u32[]{:S(2)}) %collective-permute-start.12) | collective-permute-done | bytes 196640 | tf_op jit(solution)/shard_map/ppermute | solution.py:51
  47.5 2.7 %collective-permute-start.10 = (bf16[32,3072]{1,0:T(8,128)(2,1)S(1)}, bf16[32,3072]{1,0:T(8,128)(2,1)S(1)}, u32[]{:S(2)}, u32[]{:S(2)}) collective-permute-start(bf16[32,3072]{1,0:T(8,128)(2,1)S(1)} %collective-permute-done.9.refs_2_), channel_id=1, source_target_pairs={{0,28},{4,0},{8,4},{12,8},{16,12},{20,16},{24,20},{28,24},{1,29},{... | collective-permute-start | bytes 589832 | tf_op jit(solution)/shard_map/ppermute | solution.py:51
  50.2 6.7 %collective-permute-done.15.refs_2_ = bf16[64,3072]{1,0:T(8,128)(2,1)S(1)} collective-permute-done((bf16[64,3072]{1,0:T(8,128)(2,1)S(1)}, bf16[64,3072]{1,0:T(8,128)(2,1)S(1)}, u32[]{:S(2)}, u32[]{:S(2)}) %collective-permute-start.15) | collective-permute-done | bytes 393248 | tf_op jit(solution)/shard_map/ppermute | solution.py:51
  57.0 0.1 collective-permute-start.18
  57.1 2.7 %collective-permute-start.17 = (bf16[16,3072]{1,0:T(8,128)(2,1)S(1)}, bf16[16,3072]{1,0:T(8,128)(2,1)S(1)}, u32[]{:S(2)}, u32[]{:S(2)}) collective-permute-start(bf16[16,3072]{1,0:T(8,128)(2,1)S(1)} %slice.10), channel_id=1, source_target_pairs={{0,28},{4,0},{8,4},{12,8},{16,12},{20,16},{24,20},{28,24},{1,29},{... | collective-permute-start | bytes 294920 | tf_op jit(solution)/shard_map/ppermute | solution.py:51
  59.7 1.1 copy-done.2
  60.9 1.1 copy-done.3
  62.0 5.0 %shard_map.159 = (bf16[64,3072]{1,0:T(8,128)(2,1)S(1)}, bf16[64,3072]{1,0:T(8,128)(2,1)}, bf16[64,3072]{1,0:T(8,128)(2,1)}, bf16[64,3072]{1,0:T(8,128)(2,1)}) custom-call(s32[12]{0:T(128)S(1)} %copy-done.7, bf16[256,1536]{1,0:T(8,128)(2,1)S(1)} %copy-done.2, bf16[256,1536]{1,0:T(8,128)(2,1)S(1)} %copy-done.3, bf16[64,3072]{1,0:T(8,128)(2,1)S(1)} %bitcast.18, ...), custom_call_target="tpu_custom_call" | custom-call | tf_op jit(solution)/shard_map/pallas_call | solution.py:288
  67.0 0.7 copy-done.4
  67.7 1.5 %collective-permute-start.24 = (bf16[64,3072]{1,0:T(8,128)(2,1)}, bf16[64,3072]{1,0:T(8,128)(2,1)}, u32[]{:S(2)}, u32[]{:S(2)}) collective-permute-start(bf16[64,3072]{1,0:T(8,128)(2,1)} %get-tuple-element.58), channel_id=1, source_target_pairs={{0,1},{1,32},{32,33},{33,0},{2,3},{3,34},{34,35},{35,2},{4,5},{5,3... | collective-permute-start | bytes 1179656 | tf_op jit(solution)/shard_map/ppermute | solution.py:51
  69.2 3.0 %collective-permute-start.25 = (bf16[64,3072]{1,0:T(8,128)(2,1)}, bf16[64,3072]{1,0:T(8,128)(2,1)}, u32[]{:S(2)}, u32[]{:S(2)}) collective-permute-start(bf16[64,3072]{1,0:T(8,128)(2,1)} %get-tuple-element.59), channel_id=1, source_target_pairs={{0,32},{1,33},{32,0},{33,1},{2,34},{3,35},{34,2},{35,3},{4,36},{5,... | collective-permute-start | bytes 1179656 | tf_op jit(solution)/shard_map/ppermute | solution.py:51
  72.2 3.1 %shard_map.160 = f32[8,24,256]{2,1,0:T(8,128)} custom-call(s32[12]{0:T(128)S(1)} %copy-done.7, bf16[256,1536]{1,0:T(8,128)(2,1)S(1)} %copy-done, bf16[256,1536]{1,0:T(8,128)(2,1)S(1)} %copy-done.1, bf16[32,3072]{1,0:T(8,128)(2,1)S(1)} %pad_maximum_fusion.refs_0_, bf16[32,3072]{1,0:T(8,128)(2,1)S(1)} %collective-permute-done.8.refs_1_, ...), custom_call_target="tpu_custom_call" | custom-call | tf_op jit(solution)/shard_map/pallas_call | solution.py:288
  75.3 5.4 %all-to-all-start.1 = ((f32[8,24,256]{2,1,0:T(8,128)}), f32[8,24,256]{2,1,0:T(8,128)S(1)}, u32[]{:S(2)}, u32[]{:S(2)}) async-start(f32[8,24,256]{2,1,0:T(8,128)} %shard_map.160), calls=%async_computation.1 | async-start | bytes 393216 | tf_op jit(solution)/shard_map/all_to_all | solution.py:402
  80.7 8.3 %collective-permute-done.25.p2 = bf16[64,3072]{1,0:T(8,128)(2,1)} collective-permute-done((bf16[64,3072]{1,0:T(8,128)(2,1)}, bf16[64,3072]{1,0:T(8,128)(2,1)}, u32[]{:S(2)}, u32[]{:S(2)}) %collective-permute-start.25) | collective-permute-done | bytes 393248 | tf_op jit(solution)/shard_map/ppermute | solution.py:51
  89.0 1.0 copy-done.5
  90.0 2.7 %shard_map.165 = bf16[64,3072]{1,0:T(8,128)(2,1)} custom-call(s32[12]{0:T(128)S(1)} %copy-done.7, bf16[64,3072]{1,0:T(8,128)(2,1)S(1)} %copy-done.5, bf16[64,3072]{1,0:T(8,128)(2,1)} %collective-permute-done.24.p1, bf16[64,3072]{1,0:T(8,128)(2,1)} %collective-permute-done.25.p2, bf16[64,3072]{1,0:T(8,128)(2,1)} %collective-permute-done.26.p3), custom_call_target="tpu_custom_call" | custom-call | tf_op jit(solution)/shard_map/pallas_call | solution.py:288
  92.7 5.4 %all-to-all-start.2 = ((bf16[8,8,3072]{2,1,0:T(8,128)(2,1)}), bf16[8,8,3072]{2,1,0:T(8,128)(2,1)}, u32[]{:S(2)}, u32[]{:S(2)}) async-start(bf16[8,8,3072]{2,1,0:T(8,128)(2,1)} %bitcast.10), calls=%async_computation.2 | async-start | bytes 786432 | tf_op jit(solution)/shard_map/all_to_all | solution.py:442
  98.1 0.7 shard_map.161.refs_0_
  98.8 0.0 copy-start.10
  98.8 1.5 %collective-permute-start.21 = (f32[24,256]{1,0:T(8,128)S(1)}, f32[24,256]{1,0:T(8,128)S(1)}, u32[]{:S(2)}, u32[]{:S(2)}) collective-permute-start(f32[24,256]{1,0:T(8,128)S(1)} %shard_map.161.refs_0_), channel_id=1, source_target_pairs={{0,1},{1,32},{32,33},{33,0},{2,3},{3,34},{34,35},{35,2},{4,5},{5,3... | collective-permute-start | bytes 73736 | tf_op jit(solution)/shard_map/ppermute | solution.py:51
  100.3 3.0 %collective-permute-start.20 = (f32[24,256]{1,0:T(8,128)S(1)}, f32[24,256]{1,0:T(8,128)S(1)}, u32[]{:S(2)}, u32[]{:S(2)}) collective-permute-start(f32[24,256]{1,0:T(8,128)S(1)} %shard_map.161.refs_0_), channel_id=1, source_target_pairs={{0,32},{1,33},{32,0},{33,1},{2,34},{3,35},{34,2},{35,3},{4,36},{5,... | collective-permute-start | bytes 73736 | tf_op jit(solution)/shard_map/ppermute | solution.py:51
  103.3 0.0 collective-permute-done.21.refs_3_
  103.4 1.4 %collective-permute-done.20.refs_2_ = f32[24,256]{1,0:T(8,128)S(1)} collective-permute-done((f32[24,256]{1,0:T(8,128)S(1)}, f32[24,256]{1,0:T(8,128)S(1)}, u32[]{:S(2)}, u32[]{:S(2)}) %collective-permute-start.20) | collective-permute-done | bytes 24608 | tf_op jit(solution)/shard_map/ppermute | solution.py:51
  104.8 1.6 %collective-permute-done.19.refs_1_ = f32[24,256]{1,0:T(8,128)S(1)} collective-permute-done((f32[24,256]{1,0:T(8,128)S(1)}, f32[24,256]{1,0:T(8,128)S(1)}, u32[]{:S(2)}, u32[]{:S(2)}) %collective-permute-start.19) | collective-permute-done | bytes 24608 | tf_op jit(solution)/shard_map/ppermute | solution.py:51
  106.4 0.7 shard_map.162.stats
  107.1 3.9 %shard_map.163 = (bf16[128,3072]{1,0:T(8,128)(2,1)}, bf16[128,1536]{1,0:T(8,128)(2,1)}, bf16[128,3072]{1,0:T(8,128)(2,1)}, bf16[128,1536]{1,0:T(8,128)(2,1)}) custom-call(s32[12]{0:T(128)S(1)} %copy-done.7, bf16[256,1536]{1,0:T(8,128)(2,1)S(1)} %copy-done, bf16[256,1536]{1,0:T(8,128)(2,1)S(1)} %copy-done.1, f32[24,256]{1,0:T(8,128)S(1)} %shard_map.162.stats, ...), custom_call_target="tpu_custom_call" | custom-call | tf_op jit(solution)/shard_map/pallas_call | solution.py:288
  111.0 2.1 %collective-permute-start.23 = (bf16[128,1536]{1,0:T(8,128)(2,1)}, bf16[128,1536]{1,0:T(8,128)(2,1)S(1)}, u32[]{:S(2)}, u32[]{:S(2)}) collective-permute-start(bf16[128,1536]{1,0:T(8,128)(2,1)} %get-tuple-element.66), channel_id=1, source_target_pairs={{0,2},{2,0},{1,3},{3,1},{4,6},{6,4},{5,7},{7,5},{8,10},{10,8},{9,1... | collective-permute-start | bytes 1179656 | tf_op jit(solution)/shard_map/ppermute | solution.py:51
  113.1 0.1 collective-permute-start.22
  113.2 1.1 convert_reduce_fusion.total
  114.3 0.8 collective-permute-start.27
  115.0 0.2 collective-permute-done.22.k1
  115.2 1.5 %shard_map.164 = (bf16[128,3072]{1,0:T(8,128)(2,1)}, bf16[128,3072]{1,0:T(8,128)(2,1)}) custom-call(s32[12]{0:T(128)S(1)} %copy-done.7, bf16[128,1536]{1,0:T(8,128)(2,1)S(1)} %collective-permute-done.22.k1, bf16[128,1536]{1,0:T(8,128)(2,1)S(1)} %collective-permute-done.23.v1, ...), custom_call_target="tpu_custom_call", output_to_operand_aliasing={{0}: (3, {}), {1}: (4, {})} | custom-call | tf_op jit(solution)/shard_map/pallas_call | solution.py:288
  116.8 1.3 %shard_map.166 = (bf16[4,3072]{1,0:T(4,128)(2,1)}, bf16[4,3072]{1,0:T(4,128)(2,1)}) custom-call(s32[12]{0:T(128)S(1)} %copy-done.7, f32[8,3072]{1,0:T(8,128)S(1)} %convert_reduce_fusion.total, f32[4,3072]{1,0:T(4,128)S(1)} %collective-permute-done.27.other, f32[1,128]{1,0:T(1,128)S(1)} %copy-done.11), custom_call_target="tpu_custom_call" | custom-call | tf_op jit(solution)/shard_map/pallas_call | solution.py:288
  (51 shorter events, 0.2 us)
Async XLA Ops:
  0.6 18.8 %collective-permute-start.1 = (bf16[128,3072]{1,0:T(8,128)(2,1)}, bf16[128,3072]{1,0:T(8,128)(2,1)S(1)}, u32[]{:S(2)}, u32[]{:S(2)}) collective-permute-start(bf16[128,3072]{1,0:T(8,128)(2,1)} %q0.1), channel_id=1, source_target_pairs={{0,2},{2,0},{1,3},{3,1},{4,6},{6,4},{5,7},{7,5},{8,10},{10,8},{9,1... | collective-permute-start | bytes 2359304 | tf_op jit(solution)/shard_map/ppermute | solution.py:51
  4.0 15.5 %collective-permute-start.2 = (bf16[128,3072]{1,0:T(8,128)(2,1)}, bf16[128,3072]{1,0:T(8,128)(2,1)S(1)}, u32[]{:S(2)}, u32[]{:S(2)}) collective-permute-start(bf16[128,3072]{1,0:T(8,128)(2,1)} %k0.1), channel_id=1, source_target_pairs={{0,2},{2,0},{1,3},{3,1},{4,6},{6,4},{5,7},{7,5},{8,10},{10,8},{9,1... | collective-permute-start | bytes 2359304 | tf_op jit(solution)/shard_map/ppermute | solution.py:51
  4.1 15.4 %collective-permute-start.3 = (bf16[128,3072]{1,0:T(8,128)(2,1)}, bf16[128,3072]{1,0:T(8,128)(2,1)S(1)}, u32[]{:S(2)}, u32[]{:S(2)}) collective-permute-start(bf16[128,3072]{1,0:T(8,128)(2,1)} %v0.1), channel_id=1, source_target_pairs={{0,2},{2,0},{1,3},{3,1},{4,6},{6,4},{5,7},{7,5},{8,10},{10,8},{9,1... | collective-permute-start | bytes 2359304 | tf_op jit(solution)/shard_map/ppermute | solution.py:51
  4.5 15.0 %collective-permute-start.4 = (bf16[128,3072]{1,0:T(8,128)(2,1)}, bf16[128,3072]{1,0:T(8,128)(2,1)}, u32[]{:S(2)}, u32[]{:S(2)}) collective-permute-start(bf16[128,3072]{1,0:T(8,128)(2,1)} %d0.1), channel_id=1, source_target_pairs={{0,2},{2,0},{1,3},{3,1},{4,6},{6,4},{5,7},{7,5},{8,10},{10,8},{9,1... | collective-permute-start | bytes 2359304 | tf_op jit(solution)/shard_map/ppermute | solution.py:51
  5.9 0.7 copy-start.15
  9.4 1.5 %copy-start.8 = (bf16[4,6144]{1,0:T(4,128)(2,1)S(1)}, bf16[4,6144]{1,0:T(4,128)(2,1)}, u32[]{:S(2)}) copy-start(bf16[4,6144]{1,0:T(4,128)(2,1)} %get-tuple-element.39.keep) | copy-start | bytes 147460
  9.4 1.5 %collective-permute-start = (bf16[4,6144]{1,0:T(4,128)(2,1)}, bf16[4,6144]{1,0:T(4,128)(2,1)S(1)}, u32[]{:S(2)}, u32[]{:S(2)}) collective-permute-start(bf16[4,6144]{1,0:T(4,128)(2,1)} %get-tuple-element.40), channel_id=1, source_target_pairs={{0,2},{2,0},{1,3},{3,1},{4,6},{6,4},{5,7},{7,5},{8,10},{10,8},{9,1... | collective-permute-start | bytes 147464 | tf_op jit(solution)/shard_map/ppermute | solution.py:51
  9.8 1.0 copy-start.6
  12.2 21.6 %all-to-all-start = ((bf16[8,8,3072]{2,1,0:T(8,128)(2,1)}), bf16[8,8,3072]{2,1,0:T(8,128)(2,1)S(1)}, u32[]{:S(2)}, u32[]{:S(2)}) async-start(bf16[8,8,3072]{2,1,0:T(8,128)(2,1)} %bitcast.8), calls=%async_computation | async-start | bytes 786432 | tf_op jit(solution)/shard_map/all_to_all | solution.py:334
  19.4 0.9 copy-start.12
  19.4 1.1 copy-start.13
  19.4 1.4 %copy-start.14 = (bf16[128,3072]{1,0:T(8,128)(2,1)}, bf16[128,3072]{1,0:T(8,128)(2,1)S(1)}, u32[]{:S(2)}) copy-start(bf16[128,3072]{1,0:T(8,128)(2,1)S(1)} %collective-permute-done.3.v1) | copy-start | bytes 2359300
  25.2 5.1 %collective-permute-start.7 = (bf16[8,3072]{1,0:T(8,128)(2,1)S(1)}, bf16[8,3072]{1,0:T(8,128)(2,1)S(1)}, u32[]{:S(2)}, u32[]{:S(2)}) collective-permute-start(bf16[8,3072]{1,0:T(8,128)(2,1)S(1)} %get-tuple-element.49), channel_id=1, source_target_pairs={{0,1},{1,32},{32,33},{33,0},{2,3},{3,34},{34,35},{35,2},{4,5},{5,3... | collective-permute-start | bytes 147464 | tf_op jit(solution)/shard_map/ppermute | solution.py:51
  26.6 4.6 %collective-permute-start.6 = (bf16[8,3072]{1,0:T(8,128)(2,1)S(1)}, bf16[8,3072]{1,0:T(8,128)(2,1)S(1)}, u32[]{:S(2)}, u32[]{:S(2)}) collective-permute-start(bf16[8,3072]{1,0:T(8,128)(2,1)S(1)} %get-tuple-element.49), channel_id=1, source_target_pairs={{0,32},{1,33},{32,0},{33,1},{2,34},{3,35},{34,2},{35,3},{4,36},{5,... | collective-permute-start | bytes 147464 | tf_op jit(solution)/shard_map/ppermute | solution.py:51
  29.2 3.2 %collective-permute-start.5 = (bf16[8,3072]{1,0:T(8,128)(2,1)S(1)}, bf16[8,3072]{1,0:T(8,128)(2,1)S(1)}, u32[]{:S(2)}, u32[]{:S(2)}) collective-permute-start(bf16[8,3072]{1,0:T(8,128)(2,1)S(1)} %get-tuple-element.49), channel_id=1, source_target_pairs={{0,33},{1,0},{32,1},{33,32},{2,35},{3,2},{34,3},{35,34},{4,37},{5,... | collective-permute-start | bytes 147464 | tf_op jit(solution)/shard_map/ppermute | solution.py:51
  33.8 7.7 %collective-permute-start.11 = (bf16[32,3072]{1,0:T(8,128)(2,1)S(1)}, bf16[32,3072]{1,0:T(8,128)(2,1)S(1)}, u32[]{:S(2)}, u32[]{:S(2)}) collective-permute-start(bf16[32,3072]{1,0:T(8,128)(2,1)S(1)} %pad_maximum_fusion.refs_0_), channel_id=1, source_target_pairs={{0,4},{4,8},{8,12},{12,16},{16,20},{20,24},{24,28},{28,0},{1,5},{5... | collective-permute-start | bytes 589832 | tf_op jit(solution)/shard_map/ppermute | solution.py:51
  34.0 7.4 %collective-permute-start.8 = (bf16[32,3072]{1,0:T(8,128)(2,1)S(1)}, bf16[32,3072]{1,0:T(8,128)(2,1)S(1)}, u32[]{:S(2)}, u32[]{:S(2)}) collective-permute-start(bf16[32,3072]{1,0:T(8,128)(2,1)S(1)} %pad_maximum_fusion.refs_0_), channel_id=1, source_target_pairs={{0,28},{4,0},{8,4},{12,8},{16,12},{20,16},{24,20},{28,24},{1,29},{... | collective-permute-start | bytes 589832 | tf_op jit(solution)/shard_map/ppermute | solution.py:51
  36.5 13.7 %collective-permute-start.16 = (bf16[64,3072]{1,0:T(8,128)(2,1)S(1)}, bf16[64,3072]{1,0:T(8,128)(2,1)S(1)}, u32[]{:S(2)}, u32[]{:S(2)}) collective-permute-start(bf16[64,3072]{1,0:T(8,128)(2,1)S(1)} %bitcast.15), channel_id=1, source_target_pairs={{0,1},{1,32},{32,33},{33,0},{2,3},{3,34},{34,35},{35,2},{4,5},{5,3... | collective-permute-start | bytes 1179656 | tf_op jit(solution)/shard_map/ppermute | solution.py:51
  37.8 19.1 %collective-permute-start.15 = (bf16[64,3072]{1,0:T(8,128)(2,1)S(1)}, bf16[64,3072]{1,0:T(8,128)(2,1)S(1)}, u32[]{:S(2)}, u32[]{:S(2)}) collective-permute-start(bf16[64,3072]{1,0:T(8,128)(2,1)S(1)} %bitcast.16), channel_id=1, source_target_pairs={{0,32},{1,33},{32,0},{33,1},{2,34},{3,35},{34,2},{35,3},{4,36},{5,... | collective-permute-start | bytes 1179656 | tf_op jit(solution)/shard_map/ppermute | solution.py:51
  40.4 16.5 %collective-permute-start.14 = (bf16[64,3072]{1,0:T(8,128)(2,1)S(1)}, bf16[64,3072]{1,0:T(8,128)(2,1)S(1)}, u32[]{:S(2)}, u32[]{:S(2)}) collective-permute-start(bf16[64,3072]{1,0:T(8,128)(2,1)S(1)} %bitcast.17), channel_id=1, source_target_pairs={{0,33},{1,0},{32,1},{33,32},{2,35},{3,2},{34,3},{35,34},{4,37},{5,... | collective-permute-start | bytes 1179656 | tf_op jit(solution)/shard_map/ppermute | solution.py:51
  41.5 6.0 %collective-permute-start.12 = (bf16[32,3072]{1,0:T(8,128)(2,1)S(1)}, bf16[32,3072]{1,0:T(8,128)(2,1)S(1)}, u32[]{:S(2)}, u32[]{:S(2)}) collective-permute-start(bf16[32,3072]{1,0:T(8,128)(2,1)S(1)} %collective-permute-done.11.refs_8_), channel_id=1, source_target_pairs={{0,4},{4,8},{8,12},{12,16},{16,20},{20,24},{24,28},{28,0},{1,5},{5... | collective-permute-start | bytes 589832 | tf_op jit(solution)/shard_map/ppermute | solution.py:51
  41.5 6.0 %collective-permute-start.9 = (bf16[32,3072]{1,0:T(8,128)(2,1)S(1)}, bf16[32,3072]{1,0:T(8,128)(2,1)S(1)}, u32[]{:S(2)}, u32[]{:S(2)}) collective-permute-start(bf16[32,3072]{1,0:T(8,128)(2,1)S(1)} %collective-permute-done.8.refs_1_), channel_id=1, source_target_pairs={{0,28},{4,0},{8,4},{12,8},{16,12},{20,16},{24,20},{28,24},{1,29},{... | collective-permute-start | bytes 589832 | tf_op jit(solution)/shard_map/ppermute | solution.py:51
  47.5 9.4 %collective-permute-start.13 = (bf16[32,3072]{1,0:T(8,128)(2,1)S(1)}, bf16[32,3072]{1,0:T(8,128)(2,1)S(1)}, u32[]{:S(2)}, u32[]{:S(2)}) collective-permute-start(bf16[32,3072]{1,0:T(8,128)(2,1)S(1)} %collective-permute-done.12.refs_7_), channel_id=1, source_target_pairs={{0,4},{4,8},{8,12},{12,16},{16,20},{20,24},{24,28},{28,0},{1,5},{5... | collective-permute-start | bytes 589832 | tf_op jit(solution)/shard_map/ppermute | solution.py:51
  47.5 9.4 %collective-permute-start.10 = (bf16[32,3072]{1,0:T(8,128)(2,1)S(1)}, bf16[32,3072]{1,0:T(8,128)(2,1)S(1)}, u32[]{:S(2)}, u32[]{:S(2)}) collective-permute-start(bf16[32,3072]{1,0:T(8,128)(2,1)S(1)} %collective-permute-done.9.refs_2_), channel_id=1, source_target_pairs={{0,28},{4,0},{8,4},{12,8},{16,12},{20,16},{24,20},{28,24},{1,29},{... | collective-permute-start | bytes 589832 | tf_op jit(solution)/shard_map/ppermute | solution.py:51
  56.9 2.8 %copy-start.7 = (s32[12]{0:T(128)S(1)}, s32[12]{0:T(128)}, u32[]{:S(2)}) copy-start(s32[12]{0:T(128)} %stack.36.sc) | copy-start | bytes 148
  57.0 15.2 %copy-start = (bf16[256,1536]{1,0:T(8,128)(2,1)S(1)}, bf16[256,1536]{1,0:T(8,128)(2,1)}, u32[]{:S(2)}) copy-start(bf16[256,1536]{1,0:T(8,128)(2,1)} %get-tuple-element.61.k) | copy-start | bytes 2359300
  57.0 15.2 %copy-start.1 = (bf16[256,1536]{1,0:T(8,128)(2,1)S(1)}, bf16[256,1536]{1,0:T(8,128)(2,1)}, u32[]{:S(2)}) copy-start(bf16[256,1536]{1,0:T(8,128)(2,1)} %get-tuple-element.62.v) | copy-start | bytes 2359300
  57.0 15.2 %collective-permute-start.18 = (bf16[16,3072]{1,0:T(8,128)(2,1)S(1)}, bf16[16,3072]{1,0:T(8,128)(2,1)S(1)}, u32[]{:S(2)}, u32[]{:S(2)}) collective-permute-start(bf16[16,3072]{1,0:T(8,128)(2,1)S(1)} %slice.11), channel_id=1, source_target_pairs={{0,4},{4,8},{8,12},{12,16},{16,20},{20,24},{24,28},{28,0},{1,5},{5... | collective-permute-start | bytes 294920 | tf_op jit(solution)/shard_map/ppermute | solution.py:51
  57.1 15.1 %collective-permute-start.17 = (bf16[16,3072]{1,0:T(8,128)(2,1)S(1)}, bf16[16,3072]{1,0:T(8,128)(2,1)S(1)}, u32[]{:S(2)}, u32[]{:S(2)}) collective-permute-start(bf16[16,3072]{1,0:T(8,128)(2,1)S(1)} %slice.10), channel_id=1, source_target_pairs={{0,28},{4,0},{8,4},{12,8},{16,12},{20,16},{24,20},{28,24},{1,29},{... | collective-permute-start | bytes 294920 | tf_op jit(solution)/shard_map/ppermute | solution.py:51
  59.7 1.1 copy-start.2
  60.9 1.1 copy-start.3
  67.0 0.7 copy-start.4
  67.7 12.9 %collective-permute-start.24 = (bf16[64,3072]{1,0:T(8,128)(2,1)}, bf16[64,3072]{1,0:T(8,128)(2,1)}, u32[]{:S(2)}, u32[]{:S(2)}) collective-permute-start(bf16[64,3072]{1,0:T(8,128)(2,1)} %get-tuple-element.58), channel_id=1, source_target_pairs={{0,1},{1,32},{32,33},{33,0},{2,3},{3,34},{34,35},{35,2},{4,5},{5,3... | collective-permute-start | bytes 1179656 | tf_op jit(solution)/shard_map/ppermute | solution.py:51
  69.2 19.8 %collective-permute-start.25 = (bf16[64,3072]{1,0:T(8,128)(2,1)}, bf16[64,3072]{1,0:T(8,128)(2,1)}, u32[]{:S(2)}, u32[]{:S(2)}) collective-permute-start(bf16[64,3072]{1,0:T(8,128)(2,1)} %get-tuple-element.59), channel_id=1, source_target_pairs={{0,32},{1,33},{32,0},{33,1},{2,34},{3,35},{34,2},{35,3},{4,36},{5,... | collective-permute-start | bytes 1179656 | tf_op jit(solution)/shard_map/ppermute | solution.py:51
  72.2 16.8 %collective-permute-start.26 = (bf16[64,3072]{1,0:T(8,128)(2,1)}, bf16[64,3072]{1,0:T(8,128)(2,1)}, u32[]{:S(2)}, u32[]{:S(2)}) collective-permute-start(bf16[64,3072]{1,0:T(8,128)(2,1)} %get-tuple-element.60), channel_id=1, source_target_pairs={{0,33},{1,0},{32,1},{33,32},{2,35},{3,2},{34,3},{35,34},{4,37},{5,... | collective-permute-start | bytes 1179656 | tf_op jit(solution)/shard_map/ppermute | solution.py:51
  75.3 17.4 %all-to-all-start.1 = ((f32[8,24,256]{2,1,0:T(8,128)}), f32[8,24,256]{2,1,0:T(8,128)S(1)}, u32[]{:S(2)}, u32[]{:S(2)}) async-start(f32[8,24,256]{2,1,0:T(8,128)} %shard_map.160), calls=%async_computation.1 | async-start | bytes 393216 | tf_op jit(solution)/shard_map/all_to_all | solution.py:402
  89.0 1.0 copy-start.5
  92.7 20.5 %all-to-all-start.2 = ((bf16[8,8,3072]{2,1,0:T(8,128)(2,1)}), bf16[8,8,3072]{2,1,0:T(8,128)(2,1)}, u32[]{:S(2)}, u32[]{:S(2)}) async-start(bf16[8,8,3072]{2,1,0:T(8,128)(2,1)} %bitcast.10), calls=%async_computation.2 | async-start | bytes 786432 | tf_op jit(solution)/shard_map/all_to_all | solution.py:442
  98.8 8.3 %copy-start.9 = (f32[2,128]{1,0:T(2,128)S(1)}, f32[2,128]{1,0:T(2,128)}, u32[]{:S(2)}) copy-start(f32[2,128]{1,0:T(2,128)} %get-tuple-element.77.cos) | copy-start | bytes 3076
  98.8 8.3 %copy-start.10 = (f32[2,128]{1,0:T(2,128)S(1)}, f32[2,128]{1,0:T(2,128)}, u32[]{:S(2)}) copy-start(f32[2,128]{1,0:T(2,128)} %get-tuple-element.78.sin) | copy-start | bytes 3076
  98.8 4.6 %collective-permute-start.21 = (f32[24,256]{1,0:T(8,128)S(1)}, f32[24,256]{1,0:T(8,128)S(1)}, u32[]{:S(2)}, u32[]{:S(2)}) collective-permute-start(f32[24,256]{1,0:T(8,128)S(1)} %shard_map.161.refs_0_), channel_id=1, source_target_pairs={{0,1},{1,32},{32,33},{33,0},{2,3},{3,34},{34,35},{35,2},{4,5},{5,3... | collective-permute-start | bytes 73736 | tf_op jit(solution)/shard_map/ppermute | solution.py:51
  100.3 4.5 %collective-permute-start.20 = (f32[24,256]{1,0:T(8,128)S(1)}, f32[24,256]{1,0:T(8,128)S(1)}, u32[]{:S(2)}, u32[]{:S(2)}) collective-permute-start(f32[24,256]{1,0:T(8,128)S(1)} %shard_map.161.refs_0_), channel_id=1, source_target_pairs={{0,32},{1,33},{32,0},{33,1},{2,34},{3,35},{34,2},{35,3},{4,36},{5,... | collective-permute-start | bytes 73736 | tf_op jit(solution)/shard_map/ppermute | solution.py:51
  103.3 3.1 %collective-permute-start.19 = (f32[24,256]{1,0:T(8,128)S(1)}, f32[24,256]{1,0:T(8,128)S(1)}, u32[]{:S(2)}, u32[]{:S(2)}) collective-permute-start(f32[24,256]{1,0:T(8,128)S(1)} %shard_map.161.refs_0_), channel_id=1, source_target_pairs={{0,33},{1,0},{32,1},{33,32},{2,35},{3,2},{34,3},{35,34},{4,37},{5,... | collective-permute-start | bytes 73736 | tf_op jit(solution)/shard_map/ppermute | solution.py:51
  111.0 4.0 %collective-permute-start.23 = (bf16[128,1536]{1,0:T(8,128)(2,1)}, bf16[128,1536]{1,0:T(8,128)(2,1)S(1)}, u32[]{:S(2)}, u32[]{:S(2)}) collective-permute-start(bf16[128,1536]{1,0:T(8,128)(2,1)} %get-tuple-element.66), channel_id=1, source_target_pairs={{0,2},{2,0},{1,3},{3,1},{4,6},{6,4},{5,7},{7,5},{8,10},{10,8},{9,1... | collective-permute-start | bytes 1179656 | tf_op jit(solution)/shard_map/ppermute | solution.py:51
  113.1 2.1 %collective-permute-start.22 = (bf16[128,1536]{1,0:T(8,128)(2,1)}, bf16[128,1536]{1,0:T(8,128)(2,1)S(1)}, u32[]{:S(2)}, u32[]{:S(2)}) collective-permute-start(bf16[128,1536]{1,0:T(8,128)(2,1)} %get-tuple-element.65), channel_id=1, source_target_pairs={{0,2},{2,0},{1,3},{3,1},{4,6},{6,4},{5,7},{7,5},{8,10},{10,8},{9,1... | collective-permute-start | bytes 1179656 | tf_op jit(solution)/shard_map/ppermute | solution.py:51
  114.3 2.5 %collective-permute-start.27 = (f32[4,3072]{1,0:T(4,128)S(1)}, f32[4,3072]{1,0:T(4,128)S(1)}, u32[]{:S(2)}, u32[]{:S(2)}) collective-permute-start(f32[4,3072]{1,0:T(4,128)S(1)} %slice.13), channel_id=1, source_target_pairs={{0,2},{2,0},{1,3},{3,1},{4,6},{6,4},{5,7},{7,5},{8,10},{10,8},{9,1... | collective-permute-start | bytes 147464 | tf_op jit(solution)/shard_map/ppermute | solution.py:51
  115.2 1.6 %copy-start.11 = (f32[1,128]{1,0:T(1,128)S(1)}, f32[1,128]{1,0:T(1,128)}, u32[]{:S(2)}) copy-start(f32[1,128]{1,0:T(1,128)} %constant.55.clone.freq) | copy-start | bytes 1540

commit v6 on v5

--- a/solution.py
+++ b/solution.py
@@ -88,8 +88,31 @@
         dr[rows, :] = jnp.where(token < limit, d[...].astype(f32), 0.0).astype(bf16)
 
 
-def video_to_audio_kernel(sc, q, d, *refs):
-    blocks, outs = refs[:NY], refs[NY:]
+def video_to_audio_kernel(sc, q_far, d_far, *refs):
+    blocks, outs, (q_near, d_near, sems) = refs[:NY], refs[NY : 2 * NY], refs[2 * NY :]
+    g = pl.program_id(0)
+
+    def moves(n):
+        lanes = slice(n * GW, (n + 1) * GW)
+        return [
+            pltpu.make_async_copy(far.at[:, lanes], near.at[n], sems.at[m, n])
+            for m, (far, near) in enumerate(((q_far, q_near), (d_far, d_near)))
+        ]
+
+    @pl.when(g == 0)
+    def _():
+        for n in range(GROUPS):
+            for move in moves(n):
+                move.start()
+
+    for n in range(GROUPS):
+
+        @pl.when(g == n)
+        def _():
+            for move in moves(n):
+                move.wait()
+
+    q, d = q_near.at[g], d_near.at[g]
     core, y, limit = sc[0], sc[1], sc[2]
     row = lax.broadcasted_iota(jnp.int32, (AUDIO, HD), 0)
     yy = (row // ZR + y) % NY
@@ -213,28 +236,33 @@
     return top + jnp.log2(total), delta
 
 
-def merge_kernel(sc, *refs, count, turn):
-    *parts, out = refs
-    if count > 1:
-        (part,) = parts
-        parts = [part.at[n] for n in range(count)]
+def merge_kernel(sc, parts, out):
+    lse, delta = merge([parts[n, :HEADS] for n in range(NZ)], [parts[n, HEADS:] for n in range(NZ)])
+    both = jnp.concatenate([lse, delta], 0)
+    place = lax.broadcasted_iota(jnp.int32, both.shape, 1) // CR % NY
+    a = pltpu.roll(both, sc[1] * CR, 1)
+    b = pltpu.roll(both, AUDIO - YR + sc[1] * CR, 1)
+    out[...] = jnp.where(place >= sc[1], a, b)
+
+
+def merge_back(sc, parts):
     lse, delta = merge([p[:HEADS] for p in parts], [p[HEADS:] for p in parts])
     both = jnp.concatenate([lse, delta], 0)
     place = lax.broadcasted_iota(jnp.int32, both.shape, 1) // CR % NY
-    if turn > 0:
-        a = pltpu.roll(both, sc[1] * CR, 1)
-        b = pltpu.roll(both, AUDIO - YR + sc[1] * CR, 1)
-        out[...] = jnp.where(place >= sc[1], a, b)
-    else:
-        a = pltpu.roll(both, lax.rem(AUDIO - sc[1] * CR, AUDIO), 1)
-        b = pltpu.roll(both, YR - sc[1] * CR, 1)
-        both = jnp.where(place < NY - sc[1], a, b)
-        out[...] = pltpu.roll(both, lax.rem(AUDIO - sc[6] * YR, AUDIO), 1)
-
-
-def audio_to_video_kernel(sc, k, v, stats, cos, sin, *refs):
-    *blocks, dk0, dk1, dv0, dv1 = refs
+    a = pltpu.roll(both, lax.rem(AUDIO - sc[1] * CR, AUDIO), 1)
+    b = pltpu.roll(both, YR - sc[1] * CR, 1)
+    both = jnp.where(place < NY - sc[1], a, b)
+    return pltpu.roll(both, lax.rem(AUDIO - sc[6] * YR, AUDIO), 1)
+
+
+def audio_to_video_kernel(sc, k, v, s0, s1, s2, s3, cos, sin, *refs):
+    *blocks, dk0, dk1, dv0, dv1, stats = refs
     g = pl.program_id(0)
+
+    @pl.when(g == 0)
+    def _():
+        stats[...] = merge_back(sc, (s0, s1, s2, s3))
+
     row = lax.broadcasted_iota(jnp.int32, (2 * VT, HD), 0)
     valid = video_token(sc, row) < sc[3]
 
@@ -262,7 +290,7 @@
     ahead(scores, gradients)
 
 
-def finish_kernel(sc, total, other, freq, dk, dv):
+def finish_audio(sc, total, other, freq, dk, dv):
     core = sc[0]
     cosine, sine = audio_turn(sc, freq)
     for c in range(NC):
@@ -279,9 +307,13 @@
             dv[:, lanes] = w.astype(bf16)
 
 
-def join_kernel(sc, k1, v1, k, v, dk, dv):
+def last_kernel(sc, k1, v1, k, v, total, other, freq, dk, dv, dk_audio, dv_audio):
     dk[...] = k1[...]
     dv[...] = v1[...]
+
+    @pl.when(pl.program_id(0) == 0)
+    def _():
+        finish_audio(sc, total, other, freq, dk_audio, dv_audio)
 
 
 def call(kernel, scalars, args, specs, outs, out_specs, grid=(GROUPS,), limit=16, scratch=(), aliases={}):
@@ -382,9 +414,12 @@
         video_to_audio_kernel,
         scalars,
         (qr, dr, *kv_all),
-        [video_in] * 2 + [audio_in] * NY,
+        [pl.BlockSpec(memory_space=pltpu.HBM)] * 2 + [audio_in] * NY,
         [audio_shape] * NY,
         [audio] * NY,
+        scratch=[pltpu.VMEM((GROUPS, 2 * VT, GW), bf16)] * 2
+        + [pltpu.SemaphoreType.DMA((2, GROUPS))],
+        limit=58,
     )
     parts_y = [parts[0]] + [shift(parts[n], Y, NY, n) for n in range(1, NY)]
 
@@ -401,7 +436,7 @@
     )
     stats = lax.all_to_all(copies, "z", split_axis=0, concat_axis=0, tiled=True)
     stats = call(
-        functools.partial(merge_kernel, count=NZ, turn=1),
+        merge_kernel,
         scalars,
         (stats,),
         [every],
@@ -418,23 +453,14 @@
         audio_shape,
         audio,
     )
-    stats = call(
-        functools.partial(merge_kernel, count=1, turn=-1),
-        scalars,
-        along_y(stats),
-        [rows] * NY,
-        rows_shape,
-        rows,
-        grid=(1,),
-        limit=16,
-    )
     dk0, dk1, dv0, dv1 = call(
         audio_to_video_kernel,
         scalars,
-        (kr, vr, stats, cos, sin, *qd_all),
-        [video_in] * 2 + [rows] + [table] * 2 + ring_in,
+        (kr, vr, *along_y(stats), cos, sin, *qd_all),
+        [video_in] * 2 + [rows] * NY + [table] * 2 + ring_in,
         [full_shape, mine_shape] * 2,
         [half, mine] * 2,
+        scratch=[pltpu.VMEM((2 * HEADS, AUDIO), f32)],
     )
 
     dk_there = dk1
@@ -443,25 +469,15 @@
     sums, _ = lax.optimization_barrier((sums, dk_there))
     sums = jnp.sum(sums.reshape(NZ, CR, 2 * CW).astype(f32), 0)
     few = pl.BlockSpec((AR, NC * CW), lambda g, sc: (0, 0))
-    dk_audio, dv_audio = call(
-        finish_kernel,
-        scalars,
-        (sums, shift(sums[AR:], "core", NC, 1), frequency[None]),
-        [chip, few, pl.BlockSpec((1, HD), lambda g, sc: (0, 0))],
-        [jax.ShapeDtypeStruct((AR, NC * CW), bf16)] * 2,
-        [few] * 2,
-        grid=(1,),
-        limit=16,
-    )
     place = pl.BlockSpec(memory_space=pl.ANY)
     other = pl.BlockSpec((VT, GW), lambda g, sc: (0, (1 - sc[0]) * GROUPS + g))
-    dk_video, dv_video = call(
-        join_kernel,
-        scalars,
-        (dk1, dv1, dk0, dv0),
-        [mine] * 2 + [place] * 2,
-        [full_shape] * 2,
-        [other] * 2,
+    dk_video, dv_video, dk_audio, dv_audio = call(
+        last_kernel,
+        scalars,
+        (dk1, dv1, dk0, dv0, sums, shift(sums[AR:], "core", NC, 1), frequency[None]),
+        [mine] * 2 + [place] * 2 + [chip, few, pl.BlockSpec((1, HD), lambda g, sc: (0, 0))],
+        [full_shape] * 2 + [jax.ShapeDtypeStruct((AR, NC * CW), bf16)] * 2,
+        [other] * 2 + [few] * 2,
         aliases={3: 0, 4: 1},
         limit=16,
     )

time: 119 us -> 118 us (level)
  local copies, waits for them, and re-layouts: 6.75 us -> 4.86 us
    unnamed x32 -> x34, local copies, waits for them, and re-layouts: 6.09 us -> 4.26 us
    pallas_call x11 -> x9, Pallas kernels: 26.7 us -> 27.5 us  [call(): pl.pallas_call(kernel, grid_spec=pltpu.PrefetchScalarGridSpec(num_scalar_...]
where the time goes in v6:
time: 118 us
  starting transfers between devices  54.8 us (46%)
  Pallas kernels  27.5 us (23%)
  waiting for transfers between devices  26.5 us (22%)
  local copies, waits for them, and re-layouts  4.86 us (4%)
  between operations  2.15 us (2%)
  other arithmetic  1.91 us (2%)
    ppermute x28, starting transfers between devices, shift(): return lax.ppermute(x, axis, [(i, (i + step) % size) for i in range(size)])  37.7 us
    pallas_call x9, Pallas kernels, call(): pl.pallas_call(kernel, grid_spec=pltpu.PrefetchScalarGridSpec(num_scalar_...  27.5 us
    ppermute x28, waiting for transfers between devices, shift(): return lax.ppermute(x, axis, [(i, (i + step) % size) for i in range(size)])  25.1 us
    all_to_all x1, starting transfers between devices, local(): kv_z = lax.all_to_all(copies, 'z', split_axis=0, concat_axis=0, tiled=True)  6.45 us
    all_to_all x1, starting transfers between devices, local(): sums = lax.all_to_all(sums, 'z', split_axis=0, concat_axis=0, tiled=True)  5.36 us
    all_to_all x1, starting transfers between devices, local(): stats = lax.all_to_all(copies, 'z', split_axis=0, concat_axis=0, tiled=True)  5.35 us
    unnamed x34, local copies, waits for them, and re-layouts  4.26 us
  transfers between devices with their start and end apart: 31, of which 10 were waited for; matrix products, arithmetic and copies ran while one was open for 2% of the time, Pallas kernels for 22%

profile of v6, /device:TPU:1, one launch (start us, length us, event | category | flops | bytes accessed | tf_op | source)
XLA Modules:
  0.0 117.7 jit_solution(218114695741437251)
XLA Ops:
  0.6 3.3 %collective-permute-start.1 = (bf16[128,3072]{1,0:T(8,128)(2,1)}, bf16[128,3072]{1,0:T(8,128)(2,1)S(1)}, u32[]{:S(2)}, u32[]{:S(2)}) collective-permute-start(bf16[128,3072]{1,0:T(8,128)(2,1)} %q0.1), channel_id=1, source_target_pairs={{0,2},{2,0},{1,3},{3,1},{4,6},{6,4},{5,7},{7,5},{8,10},{10,8},{9,1... | collective-permute-start | bytes 2359304 | tf_op jit(solution)/shard_map/ppermute | solution.py:51
  4.0 0.1 collective-permute-start.2
  4.1 0.4 collective-permute-start.3
  4.5 0.1 collective-permute-start.4
  5.9 0.6 copy-done.16
  6.5 0.6 stack.36.sc
  7.1 2.2 %shard_map.156 = (bf16[4,6144]{1,0:T(4,128)(2,1)}, bf16[4,6144]{1,0:T(4,128)(2,1)}) custom-call(s32[12]{0:T(128)} %stack.36.sc, bf16[4,3072]{1,0:T(4,128)(2,1)} %q.1, bf16[4,3072]{1,0:T(4,128)(2,1)} %k.1, bf16[4,3072]{1,0:T(4,128)(2,1)} %v.1, bf16[4,3072]{1,0:T(4,128)(2,1)} %d.1, f32[1,128]{1,0:T(1,128)} %constant.55.clone.freq), custom_call_target="tpu_custom_call" | custom-call | tf_op jit(solution)/shard_map/pallas_call | solution.py:320
  9.3 0.4 collective-permute-start
  9.7 0.1 add_convert_fusion
  9.8 1.0 collective-permute-done.got
  10.8 1.3 %shard_map.157 = (bf16[8,3072]{1,0:T(8,128)(2,1)S(1)}, bf16[64,3072]{1,0:T(8,128)(2,1)}) custom-call(s32[12]{0:T(128)S(1)} %copy-done.3, bf16[4,6144]{1,0:T(4,128)(2,1)S(1)} %copy-done.5, bf16[4,6144]{1,0:T(4,128)(2,1)S(1)} %collective-permute-done.got), custom_call_target="tpu_custom_call" | custom-call | tf_op jit(solution)/shard_map/pallas_call | solution.py:320
  12.1 6.5 %all-to-all-start = ((bf16[8,8,3072]{2,1,0:T(8,128)(2,1)}), bf16[8,8,3072]{2,1,0:T(8,128)(2,1)S(1)}, u32[]{:S(2)}, u32[]{:S(2)}) async-start(bf16[8,8,3072]{2,1,0:T(8,128)(2,1)} %bitcast.8), calls=%async_computation | async-start | bytes 786432 | tf_op jit(solution)/shard_map/all_to_all | solution.py:366
  18.6 0.1 fusion
  18.7 0.6 pad_maximum_fusion.1
  19.3 0.0 collective-permute-done.1.q1
  19.4 0.0 collective-permute-done.2.k1
  19.4 0.0 copy-start.11
  19.4 0.0 collective-permute-done.3.v1
  19.4 0.8 copy-done.10
  20.2 0.3 copy-done.11
  20.5 0.3 copy-done.12
  20.8 4.3 %shard_map.158 = (bf16[256,1536]{1,0:T(8,128)(2,1)}, bf16[256,1536]{1,0:T(8,128)(2,1)}, bf16[256,1536]{1,0:T(8,128)(2,1)}, bf16[256,1536]{1,0:T(8,128)(2,1)}) custom-call(s32[12]{0:T(128)} %stack.36.sc, bf16[128,3072]{1,0:T(8,128)(2,1)} %q0.1, bf16[128,3072]{1,0:T(8,128)(2,1)} %copy-done.10, bf16[128,3072]{1,0:T(8,128)(2,1)} %k0.1, ...), custom_call_target="tpu_custom_call" | custom-call | tf_op jit(solution)/shard_map/pallas_call | solution.py:320
  25.1 1.4 %collective-permute-start.7 = (bf16[8,3072]{1,0:T(8,128)(2,1)S(1)}, bf16[8,3072]{1,0:T(8,128)(2,1)S(1)}, u32[]{:S(2)}, u32[]{:S(2)}) collective-permute-start(bf16[8,3072]{1,0:T(8,128)(2,1)S(1)} %get-tuple-element.45), channel_id=1, source_target_pairs={{0,1},{1,32},{32,33},{33,0},{2,3},{3,34},{34,35},{35,2},{4,5},{5,3... | collective-permute-start | bytes 147464 | tf_op jit(solution)/shard_map/ppermute | solution.py:51
  26.5 2.6 %collective-permute-start.6 = (bf16[8,3072]{1,0:T(8,128)(2,1)S(1)}, bf16[8,3072]{1,0:T(8,128)(2,1)S(1)}, u32[]{:S(2)}, u32[]{:S(2)}) collective-permute-start(bf16[8,3072]{1,0:T(8,128)(2,1)S(1)} %get-tuple-element.45), channel_id=1, source_target_pairs={{0,32},{1,33},{32,0},{33,1},{2,34},{3,35},{34,2},{35,3},{4,36},{5,... | collective-permute-start | bytes 147464 | tf_op jit(solution)/shard_map/ppermute | solution.py:51
  29.1 1.1 collective-permute-start.5
  30.2 0.9 collective-permute-done.6
  31.1 1.2 %collective-permute-done.5 = bf16[8,3072]{1,0:T(8,128)(2,1)S(1)} collective-permute-done((bf16[8,3072]{1,0:T(8,128)(2,1)S(1)}, bf16[8,3072]{1,0:T(8,128)(2,1)S(1)}, u32[]{:S(2)}, u32[]{:S(2)}) %collective-permute-start.5) | collective-permute-done | bytes 49184 | tf_op jit(solution)/shard_map/ppermute | solution.py:51
  32.4 1.4 %all-to-all-done = bf16[8,8,3072]{2,1,0:T(8,128)(2,1)S(1)} async-done(((bf16[8,8,3072]{2,1,0:T(8,128)(2,1)}), bf16[8,8,3072]{2,1,0:T(8,128)(2,1)S(1)}, u32[]{:S(2)}, u32[]{:S(2)}) %all-to-all-start) | async-done | bytes 393248 | tf_op jit(solution)/shard_map/all_to_all | solution.py:366
  33.7 0.2 collective-permute-start.11
  34.0 2.5 %collective-permute-start.8 = (bf16[32,3072]{1,0:T(8,128)(2,1)S(1)}, bf16[32,3072]{1,0:T(8,128)(2,1)S(1)}, u32[]{:S(2)}, u32[]{:S(2)}) collective-permute-start(bf16[32,3072]{1,0:T(8,128)(2,1)S(1)} %pad_maximum_fusion.refs_0_), channel_id=1, source_target_pairs={{0,28},{4,0},{8,4},{12,8},{16,12},{20,16},{24,20},{28,24},{1,29},{... | collective-permute-start | bytes 589832 | tf_op jit(solution)/shard_map/ppermute | solution.py:51
  36.4 1.3 %collective-permute-start.16 = (bf16[64,3072]{1,0:T(8,128)(2,1)S(1)}, bf16[64,3072]{1,0:T(8,128)(2,1)S(1)}, u32[]{:S(2)}, u32[]{:S(2)}) collective-permute-start(bf16[64,3072]{1,0:T(8,128)(2,1)S(1)} %bitcast.15), channel_id=1, source_target_pairs={{0,1},{1,32},{32,33},{33,0},{2,3},{3,34},{34,35},{35,2},{4,5},{5,3... | collective-permute-start | bytes 1179656 | tf_op jit(solution)/shard_map/ppermute | solution.py:51
  37.7 2.6 %collective-permute-start.15 = (bf16[64,3072]{1,0:T(8,128)(2,1)S(1)}, bf16[64,3072]{1,0:T(8,128)(2,1)S(1)}, u32[]{:S(2)}, u32[]{:S(2)}) collective-permute-start(bf16[64,3072]{1,0:T(8,128)(2,1)S(1)} %bitcast.16), channel_id=1, source_target_pairs={{0,32},{1,33},{32,0},{33,1},{2,34},{3,35},{34,2},{35,3},{4,36},{5,... | collective-permute-start | bytes 1179656 | tf_op jit(solution)/shard_map/ppermute | solution.py:51
  40.3 1.1 collective-permute-start.14
  41.4 2.7 %collective-permute-start.9 = (bf16[32,3072]{1,0:T(8,128)(2,1)S(1)}, bf16[32,3072]{1,0:T(8,128)(2,1)S(1)}, u32[]{:S(2)}, u32[]{:S(2)}) collective-permute-start(bf16[32,3072]{1,0:T(8,128)(2,1)S(1)} %collective-permute-done.8.refs_1_), channel_id=1, source_target_pairs={{0,28},{4,0},{8,4},{12,8},{16,12},{20,16},{24,20},{28,24},{1,29},{... | collective-permute-start | bytes 589832 | tf_op jit(solution)/shard_map/ppermute | solution.py:51
  44.1 3.3 %collective-permute-done.12.refs_7_ = bf16[32,3072]{1,0:T(8,128)(2,1)S(1)} collective-permute-done((bf16[32,3072]{1,0:T(8,128)(2,1)S(1)}, bf16[32,3072]{1,0:T(8,128)(2,1)S(1)}, u32[]{:S(2)}, u32[]{:S(2)}) %collective-permute-start.12) | collective-permute-done | bytes 196640 | tf_op jit(solution)/shard_map/ppermute | solution.py:51
  47.4 2.7 %collective-permute-start.10 = (bf16[32,3072]{1,0:T(8,128)(2,1)S(1)}, bf16[32,3072]{1,0:T(8,128)(2,1)S(1)}, u32[]{:S(2)}, u32[]{:S(2)}) collective-permute-start(bf16[32,3072]{1,0:T(8,128)(2,1)S(1)} %collective-permute-done.9.refs_2_), channel_id=1, source_target_pairs={{0,28},{4,0},{8,4},{12,8},{16,12},{20,16},{24,20},{28,24},{1,29},{... | collective-permute-start | bytes 589832 | tf_op jit(solution)/shard_map/ppermute | solution.py:51
  50.1 6.7 %collective-permute-done.15.refs_2_ = bf16[64,3072]{1,0:T(8,128)(2,1)S(1)} collective-permute-done((bf16[64,3072]{1,0:T(8,128)(2,1)S(1)}, bf16[64,3072]{1,0:T(8,128)(2,1)S(1)}, u32[]{:S(2)}, u32[]{:S(2)}) %collective-permute-start.15) | collective-permute-done | bytes 393248 | tf_op jit(solution)/shard_map/ppermute | solution.py:51
  56.9 0.1 collective-permute-start.18
  57.0 2.7 %collective-permute-start.17 = (bf16[16,3072]{1,0:T(8,128)(2,1)S(1)}, bf16[16,3072]{1,0:T(8,128)(2,1)S(1)}, u32[]{:S(2)}, u32[]{:S(2)}) collective-permute-start(bf16[16,3072]{1,0:T(8,128)(2,1)S(1)} %slice.10), channel_id=1, source_target_pairs={{0,28},{4,0},{8,4},{12,8},{16,12},{20,16},{24,20},{28,24},{1,29},{... | collective-permute-start | bytes 294920 | tf_op jit(solution)/shard_map/ppermute | solution.py:51
  59.7 7.4 %shard_map.159 = (bf16[64,3072]{1,0:T(8,128)(2,1)}, bf16[64,3072]{1,0:T(8,128)(2,1)}, bf16[64,3072]{1,0:T(8,128)(2,1)}, bf16[64,3072]{1,0:T(8,128)(2,1)}) custom-call(s32[12]{0:T(128)} %stack.36.sc, bf16[256,1536]{1,0:T(8,128)(2,1)} %get-tuple-element.43.q_far, bf16[256,1536]{1,0:T(8,128)(2,1)} %get-tuple-element.44.d_far, bf16[64,3072]{1,0:T(8,128)(2,1)} %bitcast.18, ...), custom_call_target="tpu_custom_call" | custom-call | tf_op jit(solution)/shard_map/pallas_call | solution.py:320
  67.1 1.6 %collective-permute-start.24 = (bf16[64,3072]{1,0:T(8,128)(2,1)}, bf16[64,3072]{1,0:T(8,128)(2,1)}, u32[]{:S(2)}, u32[]{:S(2)}) collective-permute-start(bf16[64,3072]{1,0:T(8,128)(2,1)} %get-tuple-element.54), channel_id=1, source_target_pairs={{0,1},{1,32},{32,33},{33,0},{2,3},{3,34},{34,35},{35,2},{4,5},{5,3... | collective-permute-start | bytes 1179656 | tf_op jit(solution)/shard_map/ppermute | solution.py:51
  68.7 3.0 %collective-permute-start.25 = (bf16[64,3072]{1,0:T(8,128)(2,1)}, bf16[64,3072]{1,0:T(8,128)(2,1)}, u32[]{:S(2)}, u32[]{:S(2)}) collective-permute-start(bf16[64,3072]{1,0:T(8,128)(2,1)} %get-tuple-element.55), channel_id=1, source_target_pairs={{0,32},{1,33},{32,0},{33,1},{2,34},{3,35},{34,2},{35,3},{4,36},{5,... | collective-permute-start | bytes 1179656 | tf_op jit(solution)/shard_map/ppermute | solution.py:51
  71.7 0.5 copy-done.4
  72.2 3.1 %shard_map.160 = f32[8,24,256]{2,1,0:T(8,128)} custom-call(s32[12]{0:T(128)S(1)} %copy-done.4, bf16[256,1536]{1,0:T(8,128)(2,1)S(1)} %copy-done, bf16[256,1536]{1,0:T(8,128)(2,1)S(1)} %copy-done.1, bf16[32,3072]{1,0:T(8,128)(2,1)S(1)} %pad_maximum_fusion.refs_0_, bf16[32,3072]{1,0:T(8,128)(2,1)S(1)} %collective-permute-done.8.refs_1_, ...), custom_call_target="tpu_custom_call" | custom-call | tf_op jit(solution)/shard_map/pallas_call | solution.py:320
  75.3 5.4 %all-to-all-start.1 = ((f32[8,24,256]{2,1,0:T(8,128)}), f32[8,24,256]{2,1,0:T(8,128)S(1)}, u32[]{:S(2)}, u32[]{:S(2)}) async-start(f32[8,24,256]{2,1,0:T(8,128)} %shard_map.160), calls=%async_computation.1 | async-start | bytes 393216 | tf_op jit(solution)/shard_map/all_to_all | solution.py:437
  80.6 7.8 %collective-permute-done.25.p2 = bf16[64,3072]{1,0:T(8,128)(2,1)} collective-permute-done((bf16[64,3072]{1,0:T(8,128)(2,1)}, bf16[64,3072]{1,0:T(8,128)(2,1)}, u32[]{:S(2)}, u32[]{:S(2)}) %collective-permute-start.25) | collective-permute-done | bytes 393248 | tf_op jit(solution)/shard_map/ppermute | solution.py:51
  88.5 1.0 copy-done.2
  89.5 2.7 %shard_map.163 = bf16[64,3072]{1,0:T(8,128)(2,1)} custom-call(s32[12]{0:T(128)S(1)} %copy-done.4, bf16[64,3072]{1,0:T(8,128)(2,1)S(1)} %copy-done.2, bf16[64,3072]{1,0:T(8,128)(2,1)} %collective-permute-done.24.p1, bf16[64,3072]{1,0:T(8,128)(2,1)} %collective-permute-done.25.p2, bf16[64,3072]{1,0:T(8,128)(2,1)} %collective-permute-done.26.p3), custom_call_target="tpu_custom_call" | custom-call | tf_op jit(solution)/shard_map/pallas_call | solution.py:320
  92.2 5.4 %all-to-all-start.2 = ((bf16[8,8,3072]{2,1,0:T(8,128)(2,1)}), bf16[8,8,3072]{2,1,0:T(8,128)(2,1)}, u32[]{:S(2)}, u32[]{:S(2)}) async-start(bf16[8,8,3072]{2,1,0:T(8,128)(2,1)} %bitcast.10), calls=%async_computation.2 | async-start | bytes 786432 | tf_op jit(solution)/shard_map/all_to_all | solution.py:468
  97.5 0.0 copy-start.7
  97.6 0.7 shard_map.161.s0
  98.2 1.6 %collective-permute-start.21 = (f32[24,256]{1,0:T(8,128)S(1)}, f32[24,256]{1,0:T(8,128)S(1)}, u32[]{:S(2)}, u32[]{:S(2)}) collective-permute-start(f32[24,256]{1,0:T(8,128)S(1)} %shard_map.161.s0), channel_id=1, source_target_pairs={{0,1},{1,32},{32,33},{33,0},{2,3},{3,34},{34,35},{35,2},{4,5},{5,3... | collective-permute-start | bytes 73736 | tf_op jit(solution)/shard_map/ppermute | solution.py:51
  99.8 3.0 %collective-permute-start.20 = (f32[24,256]{1,0:T(8,128)S(1)}, f32[24,256]{1,0:T(8,128)S(1)}, u32[]{:S(2)}, u32[]{:S(2)}) collective-permute-start(f32[24,256]{1,0:T(8,128)S(1)} %shard_map.161.s0), channel_id=1, source_target_pairs={{0,32},{1,33},{32,0},{33,1},{2,34},{3,35},{34,2},{35,3},{4,36},{5,... | collective-permute-start | bytes 73736 | tf_op jit(solution)/shard_map/ppermute | solution.py:51
  102.8 0.0 collective-permute-done.21.s3
  102.9 1.4 %collective-permute-done.20.s2 = f32[24,256]{1,0:T(8,128)S(1)} collective-permute-done((f32[24,256]{1,0:T(8,128)S(1)}, f32[24,256]{1,0:T(8,128)S(1)}, u32[]{:S(2)}, u32[]{:S(2)}) %collective-permute-start.20) | collective-permute-done | bytes 24608 | tf_op jit(solution)/shard_map/ppermute | solution.py:51
  104.3 1.6 %collective-permute-done.19.s1 = f32[24,256]{1,0:T(8,128)S(1)} collective-permute-done((f32[24,256]{1,0:T(8,128)S(1)}, f32[24,256]{1,0:T(8,128)S(1)}, u32[]{:S(2)}, u32[]{:S(2)}) %collective-permute-start.19) | collective-permute-done | bytes 24608 | tf_op jit(solution)/shard_map/ppermute | solution.py:51
  106.0 4.1 %shard_map.162 = (bf16[128,3072]{1,0:T(8,128)(2,1)}, bf16[128,1536]{1,0:T(8,128)(2,1)}, bf16[128,3072]{1,0:T(8,128)(2,1)}, bf16[128,1536]{1,0:T(8,128)(2,1)}) custom-call(s32[12]{0:T(128)S(1)} %copy-done.4, bf16[256,1536]{1,0:T(8,128)(2,1)S(1)} %copy-done, bf16[256,1536]{1,0:T(8,128)(2,1)S(1)} %copy-done.1, f32[24,256]{1,0:T(8,128)S(1)} %shard_map.161.s0, ...), custom_call_target="tpu_custom_call" | custom-call | tf_op jit(solution)/shard_map/pallas_call | solution.py:320
  110.0 2.1 %collective-permute-start.23 = (bf16[128,1536]{1,0:T(8,128)(2,1)}, bf16[128,1536]{1,0:T(8,128)(2,1)S(1)}, u32[]{:S(2)}, u32[]{:S(2)}) collective-permute-start(bf16[128,1536]{1,0:T(8,128)(2,1)} %get-tuple-element.62), channel_id=1, source_target_pairs={{0,2},{2,0},{1,3},{3,1},{4,6},{6,4},{5,7},{7,5},{8,10},{10,8},{9,1... | collective-permute-start | bytes 1179656 | tf_op jit(solution)/shard_map/ppermute | solution.py:51
  112.1 0.1 collective-permute-start.22
  112.2 1.1 convert_reduce_fusion.total
  113.3 1.2 %collective-permute-start.27 = (f32[4,3072]{1,0:T(4,128)S(1)}, f32[4,3072]{1,0:T(4,128)S(1)}, u32[]{:S(2)}, u32[]{:S(2)}) collective-permute-start(f32[4,3072]{1,0:T(4,128)S(1)} %slice.13), channel_id=1, source_target_pairs={{0,2},{2,0},{1,3},{3,1},{4,6},{6,4},{5,7},{7,5},{8,10},{10,8},{9,1... | collective-permute-start | bytes 147464 | tf_op jit(solution)/shard_map/ppermute | solution.py:51
  114.5 0.9 collective-permute-done.27.other
  115.3 0.7 copy-done.8
  116.0 1.7 %shard_map.164 = (bf16[128,3072]{1,0:T(8,128)(2,1)}, bf16[128,3072]{1,0:T(8,128)(2,1)}, bf16[4,3072]{1,0:T(4,128)(2,1)}, bf16[4,3072]{1,0:T(4,128)(2,1)}) custom-call(s32[12]{0:T(128)S(1)} %copy-done.4, bf16[128,1536]{1,0:T(8,128)(2,1)S(1)} %collective-permute-done.22.k1, ...), custom_call_target="tpu_custom_call", output_to_operand_aliasing={{0}: (3, {}), {1}: (4, {})} | custom-call | tf_op jit(solution)/shard_map/pallas_call | solution.py:320
  (51 shorter events, 0.2 us)
Async XLA Ops:
  0.6 18.7 %collective-permute-start.1 = (bf16[128,3072]{1,0:T(8,128)(2,1)}, bf16[128,3072]{1,0:T(8,128)(2,1)S(1)}, u32[]{:S(2)}, u32[]{:S(2)}) collective-permute-start(bf16[128,3072]{1,0:T(8,128)(2,1)} %q0.1), channel_id=1, source_target_pairs={{0,2},{2,0},{1,3},{3,1},{4,6},{6,4},{5,7},{7,5},{8,10},{10,8},{9,1... | collective-permute-start | bytes 2359304 | tf_op jit(solution)/shard_map/ppermute | solution.py:51
  4.0 15.4 %collective-permute-start.2 = (bf16[128,3072]{1,0:T(8,128)(2,1)}, bf16[128,3072]{1,0:T(8,128)(2,1)S(1)}, u32[]{:S(2)}, u32[]{:S(2)}) collective-permute-start(bf16[128,3072]{1,0:T(8,128)(2,1)} %k0.1), channel_id=1, source_target_pairs={{0,2},{2,0},{1,3},{3,1},{4,6},{6,4},{5,7},{7,5},{8,10},{10,8},{9,1... | collective-permute-start | bytes 2359304 | tf_op jit(solution)/shard_map/ppermute | solution.py:51
  4.1 15.3 %collective-permute-start.3 = (bf16[128,3072]{1,0:T(8,128)(2,1)}, bf16[128,3072]{1,0:T(8,128)(2,1)S(1)}, u32[]{:S(2)}, u32[]{:S(2)}) collective-permute-start(bf16[128,3072]{1,0:T(8,128)(2,1)} %v0.1), channel_id=1, source_target_pairs={{0,2},{2,0},{1,3},{3,1},{4,6},{6,4},{5,7},{7,5},{8,10},{10,8},{9,1... | collective-permute-start | bytes 2359304 | tf_op jit(solution)/shard_map/ppermute | solution.py:51
  4.5 14.9 %collective-permute-start.4 = (bf16[128,3072]{1,0:T(8,128)(2,1)}, bf16[128,3072]{1,0:T(8,128)(2,1)}, u32[]{:S(2)}, u32[]{:S(2)}) collective-permute-start(bf16[128,3072]{1,0:T(8,128)(2,1)} %d0.1), channel_id=1, source_target_pairs={{0,2},{2,0},{1,3},{3,1},{4,6},{6,4},{5,7},{7,5},{8,10},{10,8},{9,1... | collective-permute-start | bytes 2359304 | tf_op jit(solution)/shard_map/ppermute | solution.py:51
  5.9 0.7 copy-start.16
  9.3 1.5 %copy-start.5 = (bf16[4,6144]{1,0:T(4,128)(2,1)S(1)}, bf16[4,6144]{1,0:T(4,128)(2,1)}, u32[]{:S(2)}) copy-start(bf16[4,6144]{1,0:T(4,128)(2,1)} %get-tuple-element.35.keep) | copy-start | bytes 147460
  9.3 1.5 %collective-permute-start = (bf16[4,6144]{1,0:T(4,128)(2,1)}, bf16[4,6144]{1,0:T(4,128)(2,1)S(1)}, u32[]{:S(2)}, u32[]{:S(2)}) collective-permute-start(bf16[4,6144]{1,0:T(4,128)(2,1)} %get-tuple-element.36), channel_id=1, source_target_pairs={{0,2},{2,0},{1,3},{3,1},{4,6},{6,4},{5,7},{7,5},{8,10},{10,8},{9,1... | collective-permute-start | bytes 147464 | tf_op jit(solution)/shard_map/ppermute | solution.py:51
  9.8 1.0 copy-start.3
  12.1 21.6 %all-to-all-start = ((bf16[8,8,3072]{2,1,0:T(8,128)(2,1)}), bf16[8,8,3072]{2,1,0:T(8,128)(2,1)S(1)}, u32[]{:S(2)}, u32[]{:S(2)}) async-start(bf16[8,8,3072]{2,1,0:T(8,128)(2,1)} %bitcast.8), calls=%async_computation | async-start | bytes 786432 | tf_op jit(solution)/shard_map/all_to_all | solution.py:366
  19.4 0.9 copy-start.10
  19.4 1.1 copy-start.11
  19.4 1.4 %copy-start.12 = (bf16[128,3072]{1,0:T(8,128)(2,1)}, bf16[128,3072]{1,0:T(8,128)(2,1)S(1)}, u32[]{:S(2)}) copy-start(bf16[128,3072]{1,0:T(8,128)(2,1)S(1)} %collective-permute-done.3.v1) | copy-start | bytes 2359300
  25.1 5.1 %collective-permute-start.7 = (bf16[8,3072]{1,0:T(8,128)(2,1)S(1)}, bf16[8,3072]{1,0:T(8,128)(2,1)S(1)}, u32[]{:S(2)}, u32[]{:S(2)}) collective-permute-start(bf16[8,3072]{1,0:T(8,128)(2,1)S(1)} %get-tuple-element.45), channel_id=1, source_target_pairs={{0,1},{1,32},{32,33},{33,0},{2,3},{3,34},{34,35},{35,2},{4,5},{5,3... | collective-permute-start | bytes 147464 | tf_op jit(solution)/shard_map/ppermute | solution.py:51
  26.5 4.6 %collective-permute-start.6 = (bf16[8,3072]{1,0:T(8,128)(2,1)S(1)}, bf16[8,3072]{1,0:T(8,128)(2,1)S(1)}, u32[]{:S(2)}, u32[]{:S(2)}) collective-permute-start(bf16[8,3072]{1,0:T(8,128)(2,1)S(1)} %get-tuple-element.45), channel_id=1, source_target_pairs={{0,32},{1,33},{32,0},{33,1},{2,34},{3,35},{34,2},{35,3},{4,36},{5,... | collective-permute-start | bytes 147464 | tf_op jit(solution)/shard_map/ppermute | solution.py:51
  29.1 3.2 %collective-permute-start.5 = (bf16[8,3072]{1,0:T(8,128)(2,1)S(1)}, bf16[8,3072]{1,0:T(8,128)(2,1)S(1)}, u32[]{:S(2)}, u32[]{:S(2)}) collective-permute-start(bf16[8,3072]{1,0:T(8,128)(2,1)S(1)} %get-tuple-element.45), channel_id=1, source_target_pairs={{0,33},{1,0},{32,1},{33,32},{2,35},{3,2},{34,3},{35,34},{4,37},{5,... | collective-permute-start | bytes 147464 | tf_op jit(solution)/shard_map/ppermute | solution.py:51
  33.7 23.2 %copy-start.9 = (bf16[8,8,3072]{2,1,0:T(8,128)(2,1)}, bf16[8,8,3072]{2,1,0:T(8,128)(2,1)S(1)}, u32[]{:S(2)}) copy-start(bf16[8,8,3072]{2,1,0:T(8,128)(2,1)S(1)} %all-to-all-done) | copy-start | bytes 1179652
  33.7 7.7 %collective-permute-start.11 = (bf16[32,3072]{1,0:T(8,128)(2,1)S(1)}, bf16[32,3072]{1,0:T(8,128)(2,1)S(1)}, u32[]{:S(2)}, u32[]{:S(2)}) collective-permute-start(bf16[32,3072]{1,0:T(8,128)(2,1)S(1)} %pad_maximum_fusion.refs_0_), channel_id=1, source_target_pairs={{0,4},{4,8},{8,12},{12,16},{16,20},{20,24},{24,28},{28,0},{1,5},{5... | collective-permute-start | bytes 589832 | tf_op jit(solution)/shard_map/ppermute | solution.py:51
  34.0 7.5 %collective-permute-start.8 = (bf16[32,3072]{1,0:T(8,128)(2,1)S(1)}, bf16[32,3072]{1,0:T(8,128)(2,1)S(1)}, u32[]{:S(2)}, u32[]{:S(2)}) collective-permute-start(bf16[32,3072]{1,0:T(8,128)(2,1)S(1)} %pad_maximum_fusion.refs_0_), channel_id=1, source_target_pairs={{0,28},{4,0},{8,4},{12,8},{16,12},{20,16},{24,20},{28,24},{1,29},{... | collective-permute-start | bytes 589832 | tf_op jit(solution)/shard_map/ppermute | solution.py:51
  36.4 13.7 %collective-permute-start.16 = (bf16[64,3072]{1,0:T(8,128)(2,1)S(1)}, bf16[64,3072]{1,0:T(8,128)(2,1)S(1)}, u32[]{:S(2)}, u32[]{:S(2)}) collective-permute-start(bf16[64,3072]{1,0:T(8,128)(2,1)S(1)} %bitcast.15), channel_id=1, source_target_pairs={{0,1},{1,32},{32,33},{33,0},{2,3},{3,34},{34,35},{35,2},{4,5},{5,3... | collective-permute-start | bytes 1179656 | tf_op jit(solution)/shard_map/ppermute | solution.py:51
  37.7 19.1 %collective-permute-start.15 = (bf16[64,3072]{1,0:T(8,128)(2,1)S(1)}, bf16[64,3072]{1,0:T(8,128)(2,1)S(1)}, u32[]{:S(2)}, u32[]{:S(2)}) collective-permute-start(bf16[64,3072]{1,0:T(8,128)(2,1)S(1)} %bitcast.16), channel_id=1, source_target_pairs={{0,32},{1,33},{32,0},{33,1},{2,34},{3,35},{34,2},{35,3},{4,36},{5,... | collective-permute-start | bytes 1179656 | tf_op jit(solution)/shard_map/ppermute | solution.py:51
  40.3 16.5 %collective-permute-start.14 = (bf16[64,3072]{1,0:T(8,128)(2,1)S(1)}, bf16[64,3072]{1,0:T(8,128)(2,1)S(1)}, u32[]{:S(2)}, u32[]{:S(2)}) collective-permute-start(bf16[64,3072]{1,0:T(8,128)(2,1)S(1)} %bitcast.17), channel_id=1, source_target_pairs={{0,33},{1,0},{32,1},{33,32},{2,35},{3,2},{34,3},{35,34},{4,37},{5,... | collective-permute-start | bytes 1179656 | tf_op jit(solution)/shard_map/ppermute | solution.py:51
  41.4 6.0 %collective-permute-start.12 = (bf16[32,3072]{1,0:T(8,128)(2,1)S(1)}, bf16[32,3072]{1,0:T(8,128)(2,1)S(1)}, u32[]{:S(2)}, u32[]{:S(2)}) collective-permute-start(bf16[32,3072]{1,0:T(8,128)(2,1)S(1)} %collective-permute-done.11.refs_8_), channel_id=1, source_target_pairs={{0,4},{4,8},{8,12},{12,16},{16,20},{20,24},{24,28},{28,0},{1,5},{5... | collective-permute-start | bytes 589832 | tf_op jit(solution)/shard_map/ppermute | solution.py:51
  41.4 6.0 %collective-permute-start.9 = (bf16[32,3072]{1,0:T(8,128)(2,1)S(1)}, bf16[32,3072]{1,0:T(8,128)(2,1)S(1)}, u32[]{:S(2)}, u32[]{:S(2)}) collective-permute-start(bf16[32,3072]{1,0:T(8,128)(2,1)S(1)} %collective-permute-done.8.refs_1_), channel_id=1, source_target_pairs={{0,28},{4,0},{8,4},{12,8},{16,12},{20,16},{24,20},{28,24},{1,29},{... | collective-permute-start | bytes 589832 | tf_op jit(solution)/shard_map/ppermute | solution.py:51
  47.4 9.4 %collective-permute-start.13 = (bf16[32,3072]{1,0:T(8,128)(2,1)S(1)}, bf16[32,3072]{1,0:T(8,128)(2,1)S(1)}, u32[]{:S(2)}, u32[]{:S(2)}) collective-permute-start(bf16[32,3072]{1,0:T(8,128)(2,1)S(1)} %collective-permute-done.12.refs_7_), channel_id=1, source_target_pairs={{0,4},{4,8},{8,12},{12,16},{16,20},{20,24},{24,28},{28,0},{1,5},{5... | collective-permute-start | bytes 589832 | tf_op jit(solution)/shard_map/ppermute | solution.py:51
  47.4 9.4 %collective-permute-start.10 = (bf16[32,3072]{1,0:T(8,128)(2,1)S(1)}, bf16[32,3072]{1,0:T(8,128)(2,1)S(1)}, u32[]{:S(2)}, u32[]{:S(2)}) collective-permute-start(bf16[32,3072]{1,0:T(8,128)(2,1)S(1)} %collective-permute-done.9.refs_2_), channel_id=1, source_target_pairs={{0,28},{4,0},{8,4},{12,8},{16,12},{20,16},{24,20},{28,24},{1,29},{... | collective-permute-start | bytes 589832 | tf_op jit(solution)/shard_map/ppermute | solution.py:51
  50.1 9.6 %copy-start.13 = (bf16[64,3072]{1,0:T(8,128)(2,1)}, bf16[64,3072]{1,0:T(8,128)(2,1)S(1)}, u32[]{:S(2)}) copy-start(bf16[64,3072]{1,0:T(8,128)(2,1)S(1)} %collective-permute-done.16.refs_3_) | copy-start | bytes 1179652
  56.9 2.8 %copy-start.14 = (bf16[64,3072]{1,0:T(8,128)(2,1)}, bf16[64,3072]{1,0:T(8,128)(2,1)S(1)}, u32[]{:S(2)}) copy-start(bf16[64,3072]{1,0:T(8,128)(2,1)S(1)} %collective-permute-done.15.refs_2_) | copy-start | bytes 1179652
  56.9 2.8 %copy-start.15 = (bf16[64,3072]{1,0:T(8,128)(2,1)}, bf16[64,3072]{1,0:T(8,128)(2,1)S(1)}, u32[]{:S(2)}) copy-start(bf16[64,3072]{1,0:T(8,128)(2,1)S(1)} %collective-permute-done.14.refs_1_) | copy-start | bytes 1179652
  56.9 14.7 %copy-start = (bf16[256,1536]{1,0:T(8,128)(2,1)S(1)}, bf16[256,1536]{1,0:T(8,128)(2,1)}, u32[]{:S(2)}) copy-start(bf16[256,1536]{1,0:T(8,128)(2,1)} %get-tuple-element.57.k) | copy-start | bytes 2359300
  56.9 14.7 %copy-start.1 = (bf16[256,1536]{1,0:T(8,128)(2,1)S(1)}, bf16[256,1536]{1,0:T(8,128)(2,1)}, u32[]{:S(2)}) copy-start(bf16[256,1536]{1,0:T(8,128)(2,1)} %get-tuple-element.58.v) | copy-start | bytes 2359300
  56.9 14.7 %collective-permute-start.18 = (bf16[16,3072]{1,0:T(8,128)(2,1)S(1)}, bf16[16,3072]{1,0:T(8,128)(2,1)S(1)}, u32[]{:S(2)}, u32[]{:S(2)}) collective-permute-start(bf16[16,3072]{1,0:T(8,128)(2,1)S(1)} %slice.11), channel_id=1, source_target_pairs={{0,4},{4,8},{8,12},{12,16},{16,20},{20,24},{24,28},{28,0},{1,5},{5... | collective-permute-start | bytes 294920 | tf_op jit(solution)/shard_map/ppermute | solution.py:51
  57.0 14.6 %collective-permute-start.17 = (bf16[16,3072]{1,0:T(8,128)(2,1)S(1)}, bf16[16,3072]{1,0:T(8,128)(2,1)S(1)}, u32[]{:S(2)}, u32[]{:S(2)}) collective-permute-start(bf16[16,3072]{1,0:T(8,128)(2,1)S(1)} %slice.10), channel_id=1, source_target_pairs={{0,28},{4,0},{8,4},{12,8},{16,12},{20,16},{24,20},{28,24},{1,29},{... | collective-permute-start | bytes 294920 | tf_op jit(solution)/shard_map/ppermute | solution.py:51
  67.1 13.5 %collective-permute-start.24 = (bf16[64,3072]{1,0:T(8,128)(2,1)}, bf16[64,3072]{1,0:T(8,128)(2,1)}, u32[]{:S(2)}, u32[]{:S(2)}) collective-permute-start(bf16[64,3072]{1,0:T(8,128)(2,1)} %get-tuple-element.54), channel_id=1, source_target_pairs={{0,1},{1,32},{32,33},{33,0},{2,3},{3,34},{34,35},{35,2},{4,5},{5,3... | collective-permute-start | bytes 1179656 | tf_op jit(solution)/shard_map/ppermute | solution.py:51
  68.7 19.8 %collective-permute-start.25 = (bf16[64,3072]{1,0:T(8,128)(2,1)}, bf16[64,3072]{1,0:T(8,128)(2,1)}, u32[]{:S(2)}, u32[]{:S(2)}) collective-permute-start(bf16[64,3072]{1,0:T(8,128)(2,1)} %get-tuple-element.55), channel_id=1, source_target_pairs={{0,32},{1,33},{32,0},{33,1},{2,34},{3,35},{34,2},{35,3},{4,36},{5,... | collective-permute-start | bytes 1179656 | tf_op jit(solution)/shard_map/ppermute | solution.py:51
  71.6 0.6 copy-start.4
  71.6 16.8 %collective-permute-start.26 = (bf16[64,3072]{1,0:T(8,128)(2,1)}, bf16[64,3072]{1,0:T(8,128)(2,1)}, u32[]{:S(2)}, u32[]{:S(2)}) collective-permute-start(bf16[64,3072]{1,0:T(8,128)(2,1)} %get-tuple-element.56), channel_id=1, source_target_pairs={{0,33},{1,0},{32,1},{33,32},{2,35},{3,2},{34,3},{35,34},{4,37},{5,... | collective-permute-start | bytes 1179656 | tf_op jit(solution)/shard_map/ppermute | solution.py:51
  75.3 16.9 %all-to-all-start.1 = ((f32[8,24,256]{2,1,0:T(8,128)}), f32[8,24,256]{2,1,0:T(8,128)S(1)}, u32[]{:S(2)}, u32[]{:S(2)}) async-start(f32[8,24,256]{2,1,0:T(8,128)} %shard_map.160), calls=%async_computation.1 | async-start | bytes 393216 | tf_op jit(solution)/shard_map/all_to_all | solution.py:437
  88.5 1.0 copy-start.2
  92.2 20.0 %all-to-all-start.2 = ((bf16[8,8,3072]{2,1,0:T(8,128)(2,1)}), bf16[8,8,3072]{2,1,0:T(8,128)(2,1)}, u32[]{:S(2)}, u32[]{:S(2)}) async-start(bf16[8,8,3072]{2,1,0:T(8,128)(2,1)} %bitcast.10), calls=%async_computation.2 | async-start | bytes 786432 | tf_op jit(solution)/shard_map/all_to_all | solution.py:468
  97.5 8.4 %copy-start.6 = (f32[2,128]{1,0:T(2,128)S(1)}, f32[2,128]{1,0:T(2,128)}, u32[]{:S(2)}) copy-start(f32[2,128]{1,0:T(2,128)} %get-tuple-element.69.cos) | copy-start | bytes 3076
  97.5 8.4 %copy-start.7 = (f32[2,128]{1,0:T(2,128)S(1)}, f32[2,128]{1,0:T(2,128)}, u32[]{:S(2)}) copy-start(f32[2,128]{1,0:T(2,128)} %get-tuple-element.70.sin) | copy-start | bytes 3076
  98.2 4.7 %collective-permute-start.21 = (f32[24,256]{1,0:T(8,128)S(1)}, f32[24,256]{1,0:T(8,128)S(1)}, u32[]{:S(2)}, u32[]{:S(2)}) collective-permute-start(f32[24,256]{1,0:T(8,128)S(1)} %shard_map.161.s0), channel_id=1, source_target_pairs={{0,1},{1,32},{32,33},{33,0},{2,3},{3,34},{34,35},{35,2},{4,5},{5,3... | collective-permute-start | bytes 73736 | tf_op jit(solution)/shard_map/ppermute | solution.py:51
  99.8 4.5 %collective-permute-start.20 = (f32[24,256]{1,0:T(8,128)S(1)}, f32[24,256]{1,0:T(8,128)S(1)}, u32[]{:S(2)}, u32[]{:S(2)}) collective-permute-start(f32[24,256]{1,0:T(8,128)S(1)} %shard_map.161.s0), channel_id=1, source_target_pairs={{0,32},{1,33},{32,0},{33,1},{2,34},{3,35},{34,2},{35,3},{4,36},{5,... | collective-permute-start | bytes 73736 | tf_op jit(solution)/shard_map/ppermute | solution.py:51
  102.8 3.1 %collective-permute-start.19 = (f32[24,256]{1,0:T(8,128)S(1)}, f32[24,256]{1,0:T(8,128)S(1)}, u32[]{:S(2)}, u32[]{:S(2)}) collective-permute-start(f32[24,256]{1,0:T(8,128)S(1)} %shard_map.161.s0), channel_id=1, source_target_pairs={{0,33},{1,0},{32,1},{33,32},{2,35},{3,2},{34,3},{35,34},{4,37},{5,... | collective-permute-start | bytes 73736 | tf_op jit(solution)/shard_map/ppermute | solution.py:51
  110.0 4.4 %collective-permute-start.23 = (bf16[128,1536]{1,0:T(8,128)(2,1)}, bf16[128,1536]{1,0:T(8,128)(2,1)S(1)}, u32[]{:S(2)}, u32[]{:S(2)}) collective-permute-start(bf16[128,1536]{1,0:T(8,128)(2,1)} %get-tuple-element.62), channel_id=1, source_target_pairs={{0,2},{2,0},{1,3},{3,1},{4,6},{6,4},{5,7},{7,5},{8,10},{10,8},{9,1... | collective-permute-start | bytes 1179656 | tf_op jit(solution)/shard_map/ppermute | solution.py:51
  112.1 2.4 %collective-permute-start.22 = (bf16[128,1536]{1,0:T(8,128)(2,1)}, bf16[128,1536]{1,0:T(8,128)(2,1)S(1)}, u32[]{:S(2)}, u32[]{:S(2)}) collective-permute-start(bf16[128,1536]{1,0:T(8,128)(2,1)} %get-tuple-element.61), channel_id=1, source_target_pairs={{0,2},{2,0},{1,3},{3,1},{4,6},{6,4},{5,7},{7,5},{8,10},{10,8},{9,1... | collective-permute-start | bytes 1179656 | tf_op jit(solution)/shard_map/ppermute | solution.py:51
  113.3 2.1 %collective-permute-start.27 = (f32[4,3072]{1,0:T(4,128)S(1)}, f32[4,3072]{1,0:T(4,128)S(1)}, u32[]{:S(2)}, u32[]{:S(2)}) collective-permute-start(f32[4,3072]{1,0:T(4,128)S(1)} %slice.13), channel_id=1, source_target_pairs={{0,2},{2,0},{1,3},{3,1},{4,6},{6,4},{5,7},{7,5},{8,10},{10,8},{9,1... | collective-permute-start | bytes 147464 | tf_op jit(solution)/shard_map/ppermute | solution.py:51
  115.3 0.7 copy-start.8
